TPU v7x, 32 devices: a whole 2x2x4 slice. The times are simulated.
32 devices in a mesh: section: 2 (over core), dp: 16 (over z, y, x).
Axes of the slice: x: 2, y: 2, z: 4, core: 2. Of those that a mesh axis runs over, the one named last changes fastest.
Arguments:
- tokens: bfloat16 [64, 256, 1024], P('dp'), may hold values from -12 to 12
- clip_frames: int32 [64], P('dp'), may hold values from 4 to 16, as said below
- cotangent: bfloat16 [64, 256, 1024], P('dp'), may hold values from -12 to 12
- embed: bfloat16 [2, 256, 1024], P('section'), may hold values from -6 to 6
- norm_params: float32 [2, 6, 1024], P('section'), may hold values from -1.2 to 1.6
- w_qkv: bfloat16 [2, 1024, 3072], P('section'), may hold values from -0.1875 to 0.1875
- w_out: bfloat16 [2, 1024, 1024], P('section'), may hold values from -0.75 to 0.75
- w_up: bfloat16 [2, 1024, 4096], P('section'), may hold values from -0.1875 to 0.1875
- w_down: bfloat16 [2, 4096, 1024], P('section'), may hold values from -0.09375 to 0.09375
Outputs:
- section_out: float32 [2, 64, 256, 1024], P('section', 'dp')
- section_grad: float32 [2, 64, 256, 1024], P('section', 'dp')
- grad_qkv: float32 [2, 1024, 3072], P('section')
- grad_out: float32 [2, 1024, 1024], P('section')
- grad_up: float32 [2, 1024, 4096], P('section')
- grad_down: float32 [2, 4096, 1024], P('section')
- grad_norm_params: float32 [2, 6, 1024], P('section')
- grad_embed: float32 [2, 256, 1024], P('section')
- norms: float32 [2, 64], P('section', 'dp')
Inputs may be any that keep to these rules, and one draw needn't show every extreme that they name: `clip_frames`: each entry is 4 or 16.
All inputs are finite; a program needn't handle non-finite values.
Results may differ from a plain program's by a relative error of at most 0.015.
Values may be sent and summed in bfloat16 or wider, within the bound.
A program may use at most 320 MiB of HBM per device.

v0:
```python
import jax
import jax.numpy as jnp
from jax import lax
from jax.sharding import PartitionSpec as P

HEADS = 8
MICRO = 4


def from_behind(block, axis, distance):
    devices = range(lax.axis_size(axis))
    route = [(i - distance, i) for i in devices if i - distance in devices]
    return lax.ppermute(block, axis, route)


def layer_norm(values, gain_row, shift_row):
    center = values - jnp.mean(values, -1, keepdims=True)
    spread = jnp.mean(center * center, -1, keepdims=True)
    return center * lax.rsqrt(spread + 1e-05) * gain_row + shift_row


def matmul(left, right, form):
    return jnp.einsum(form, left, right, preferred_element_type=jnp.float32)


def advance(base_in, source, visible, w_qkv, w_out, w_up, w_down, params):
    query_in, query_back = jax.vjp(layer_norm, base_in, params[0], params[1])
    key_in, key_back = jax.vjp(layer_norm, source, params[2], params[3])
    query_low = query_in.astype(jnp.bfloat16)
    key_low = key_in.astype(jnp.bfloat16)
    features = query_low.shape[-1]
    queries = matmul(query_low, w_qkv[:, :features], "gld,de->gle").astype(jnp.bfloat16)
    key_vals = matmul(key_low, w_qkv[:, features:], "gld,de->gle").astype(jnp.bfloat16)
    groups, positions = (queries.shape[0], queries.shape[1])
    head_shape = (groups, positions, HEADS, features // HEADS)
    head_scale = (features // HEADS) ** (-0.5)
    heads_q = queries.reshape(head_shape)
    heads_k = key_vals[..., :features].reshape(head_shape)
    heads_v = key_vals[..., features:].reshape(head_shape)
    scores = matmul(heads_q, heads_k, "gqhd,gkhd->ghqk") * head_scale
    scores = jnp.where(visible[:, None, None, :], scores, -1e30)
    row_max = jnp.max(scores, -1, keepdims=True)
    exponent = jnp.exp(scores - row_max)
    weights_soft = exponent / jnp.sum(exponent, -1, keepdims=True)
    weights_low = weights_soft.astype(jnp.bfloat16)
    mixed_out = (
        matmul(weights_low, heads_v, "ghqk,gkhd->gqhd")
        .reshape(groups, positions, features)
        .astype(jnp.bfloat16)
    )
    hidden = base_in + matmul(mixed_out, w_out, "gld,de->gle")
    normed, normed_back = jax.vjp(layer_norm, hidden, params[4], params[5])
    normed_low = normed.astype(jnp.bfloat16)
    upward = matmul(normed_low, w_up, "gld,df->glf")
    active, active_back = jax.vjp(jax.nn.gelu, upward)
    active_low = active.astype(jnp.bfloat16)
    outcome = hidden + matmul(active_low, w_down, "glf,fd->gld")
    stored_parts = (
        query_back,
        key_back,
        query_low,
        key_low,
        heads_q,
        heads_k,
        heads_v,
        weights_soft,
        weights_low,
        mixed_out,
        normed_back,
        normed_low,
        active_back,
        active_low,
    )
    return (outcome, stored_parts)


def retreat(stored_parts, w_qkv, w_out, w_up, w_down, grad_outcome):
    (
        query_back,
        key_back,
        query_low,
        key_low,
        heads_q,
        heads_k,
        heads_v,
        weights_soft,
        weights_low,
        mixed_out,
        normed_back,
        normed_low,
        active_back,
        active_low,
    ) = stored_parts
    features = query_low.shape[-1]
    groups, positions = (query_low.shape[0], query_low.shape[1])
    head_scale = (features // HEADS) ** (-0.5)
    outcome_low = grad_outcome.astype(jnp.bfloat16)
    grad_down = matmul(active_low, outcome_low, "glf,gld->fd")
    grad_active = matmul(outcome_low, w_down, "gld,fd->glf")
    (grad_upward,) = active_back(grad_active)
    upward_low = grad_upward.astype(jnp.bfloat16)
    grad_up = matmul(normed_low, upward_low, "gld,glf->df")
    grad_normed = matmul(upward_low, w_up, "glf,df->gld")
    grad_from_norm, grad_gain_mlp, grad_shift_mlp = normed_back(grad_normed)
    grad_hidden = grad_outcome + grad_from_norm
    hidden_low = grad_hidden.astype(jnp.bfloat16)
    grad_wout = matmul(mixed_out, hidden_low, "gld,gle->de")
    grad_mixed = (
        matmul(hidden_low, w_out, "gle,de->gld").astype(jnp.bfloat16).reshape(heads_q.shape)
    )
    grad_weights = matmul(grad_mixed, heads_v, "gqhd,gkhd->ghqk")
    grad_values = matmul(weights_low, grad_mixed, "ghqk,gqhd->gkhd").astype(jnp.bfloat16)
    grad_scores = weights_soft * (
        grad_weights - jnp.sum(grad_weights * weights_soft, -1, keepdims=True)
    )
    scores_low = grad_scores.astype(jnp.bfloat16)
    grad_queries = (matmul(scores_low, heads_k, "ghqk,gkhd->gqhd") * head_scale).astype(
        jnp.bfloat16
    )
    grad_keys = (matmul(scores_low, heads_q, "ghqk,gqhd->gkhd") * head_scale).astype(jnp.bfloat16)
    grad_queries = grad_queries.reshape(groups, positions, features)
    grad_pairs = jnp.concatenate(
        [
            grad_keys.reshape(groups, positions, features),
            grad_values.reshape(groups, positions, features),
        ],
        axis=-1,
    )
    grad_qkv = jnp.concatenate(
        [
            matmul(query_low, grad_queries, "gld,gle->de"),
            matmul(key_low, grad_pairs, "gld,gle->de"),
        ],
        axis=1,
    )
    grad_query_in = matmul(grad_queries, w_qkv[:, :features], "gle,de->gld")
    grad_key_in = matmul(grad_pairs, w_qkv[:, features:], "gle,de->gld")
    grad_base_norm, grad_gain_q, grad_shift_q = query_back(grad_query_in)
    grad_source, grad_gain_k, grad_shift_k = key_back(grad_key_in)
    grad_base = grad_hidden + grad_base_norm
    grad_params = jnp.stack(
        [grad_gain_q, grad_shift_q, grad_gain_k, grad_shift_k, grad_gain_mlp, grad_shift_mlp]
    )
    return ((grad_qkv, grad_wout, grad_up, grad_down, grad_params), grad_base, grad_source)


def body(tokens, clip_frames, cotangent, embed, norm_params, w_qkv, w_out, w_up, w_down):
    section_index = lax.axis_index("section")
    is_first = section_index == 0
    matrices = (w_qkv[0], w_out[0], w_up[0], w_down[0])
    params = norm_params[0]
    embed_row = embed[0].astype(jnp.float32)
    total_groups, positions, features = tokens.shape
    per_micro = total_groups // MICRO
    slot_ids = jnp.arange(positions, dtype=jnp.int32)
    visible_all = (slot_ids[None, :] < clip_frames[:, None] * (positions // 16)) | jnp.logical_not(
        is_first
    )
    received = jnp.zeros((per_micro, positions, features), jnp.bfloat16)
    sources = []
    outputs = jnp.zeros((total_groups, positions, features), jnp.float32)
    for time_step in range(MICRO + 1):
        micro_index = time_step - section_index
        is_valid = (micro_index >= 0) & (micro_index < MICRO)
        start_row = jnp.clip(micro_index, 0, MICRO - 1) * per_micro
        own_part = lax.dynamic_slice_in_dim(tokens, start_row, per_micro, 0)
        source = jnp.where(is_first, own_part, received)
        sources.append(source)
        visible = lax.dynamic_slice_in_dim(visible_all, start_row, per_micro, 0)
        source_wide = source.astype(jnp.float32)
        base_in = jnp.where(is_first, 0.0, source_wide) + embed_row
        outcome, unused = advance(base_in, source_wide, visible, *matrices, params)
        updated = lax.dynamic_update_slice_in_dim(outputs, outcome, start_row, 0)
        outputs = jnp.where(is_valid, updated, outputs)
        received = from_behind(outcome.astype(jnp.bfloat16), "section", 1)
    stored = jnp.stack(sources)
    arriving = jnp.zeros((per_micro, positions, features), jnp.bfloat16)
    grad_inputs = jnp.zeros((total_groups, positions, features), jnp.float32)
    totals = None
    for time_step in range(MICRO + 1):
        micro_index = time_step - 1 + section_index
        is_valid = (micro_index >= 0) & (micro_index < MICRO)
        clipped = jnp.clip(micro_index, 0, MICRO - 1)
        start_row = clipped * per_micro
        source = lax.dynamic_index_in_dim(stored, clipped + section_index, 0, keepdims=False)
        visible = lax.dynamic_slice_in_dim(visible_all, start_row, per_micro, 0)
        source_wide = source.astype(jnp.float32)
        base_in = jnp.where(is_first, 0.0, source_wide) + embed_row
        upstream = jnp.where(
            is_first, arriving, lax.dynamic_slice_in_dim(cotangent, start_row, per_micro, 0)
        )
        outcome, stored_parts = advance(base_in, source_wide, visible, *matrices, params)
        weight_grads, grad_base, grad_source = retreat(
            stored_parts, *matrices, upstream.astype(jnp.float32)
        )
        sent_grad = (grad_source + grad_base).astype(jnp.bfloat16)
        grad_here = jnp.where(is_first, grad_source, sent_grad.astype(jnp.float32))
        updated = lax.dynamic_update_slice_in_dim(grad_inputs, grad_here, start_row, 0)
        grad_inputs = jnp.where(is_valid, updated, grad_inputs)
        arriving = from_behind(sent_grad, "section", -1)
        grad_terms = weight_grads + (jnp.sum(grad_base, axis=0),)
        grad_terms = tuple((jnp.where(is_valid, member, 0.0) for member in grad_terms))
        shares = (
            lax.psum_scatter(grad_terms[0], "dp", scatter_dimension=0, tiled=True),
            lax.psum_scatter(grad_terms[1], "dp", scatter_dimension=0, tiled=True),
            lax.psum_scatter(grad_terms[2], "dp", scatter_dimension=0, tiled=True),
            lax.psum_scatter(grad_terms[3], "dp", scatter_dimension=0, tiled=True),
            lax.psum_scatter(grad_terms[4], "dp", scatter_dimension=1, tiled=True),
            lax.psum_scatter(grad_terms[5], "dp", scatter_dimension=0, tiled=True),
        )
        totals = (
            shares
            if totals is None
            else tuple((older + newer for older, newer in zip(totals, shares)))
        )
    magnitude = jnp.sqrt(jnp.mean(grad_inputs * grad_inputs, axis=(1, 2)) + 1e-06)
    overall = lax.psum(jnp.sum(magnitude), "dp")
    norms = magnitude / (overall / (total_groups * lax.axis_size("dp")))
    gathered = (
        lax.all_gather(totals[0].astype(jnp.bfloat16), "dp", axis=0, tiled=True).astype(
            jnp.float32
        ),
        lax.all_gather(totals[1].astype(jnp.bfloat16), "dp", axis=0, tiled=True).astype(
            jnp.float32
        ),
        lax.all_gather(totals[2].astype(jnp.bfloat16), "dp", axis=0, tiled=True).astype(
            jnp.float32
        ),
        lax.all_gather(totals[3].astype(jnp.bfloat16), "dp", axis=0, tiled=True).astype(
            jnp.float32
        ),
        lax.all_gather(totals[4].astype(jnp.bfloat16), "dp", axis=1, tiled=True).astype(
            jnp.float32
        ),
        lax.all_gather(totals[5].astype(jnp.bfloat16), "dp", axis=0, tiled=True).astype(
            jnp.float32
        ),
    )
    return (
        outputs[None],
        grad_inputs[None],
        gathered[0][None],
        gathered[1][None],
        gathered[2][None],
        gathered[3][None],
        gathered[4][None],
        gathered[5][None],
        norms[None],
    )


def solution(mesh):
    placed = (
        P("dp", None, None),
        P("dp"),
        P("dp", None, None),
        P("section", None, None),
        P("section", None, None),
        P("section", None, None),
        P("section", None, None),
        P("section", None, None),
        P("section", None, None),
    )
    return jax.shard_map(
        body,
        mesh=mesh,
        in_specs=placed,
        out_specs=(
            P("section", "dp", None, None),
            P("section", "dp", None, None),
            P("section", None, None),
            P("section", None, None),
            P("section", None, None),
            P("section", None, None),
            P("section", None, None),
            P("section", None, None),
            P("section", "dp"),
        ),
        check_vma=False,
    )
```

profile of v0, /device:TPU:0, one launch (start us, length us, event | category | flops | bytes accessed | tf_op | source)
XLA Modules:
  0.0 2082.3 jit_solution(2583167557467999440)
XLA Ops:
  32.2 12.4 fusion.1075
  71.1 12.7 fusion.1074
  108.8 12.7 fusion.1073
  147.7 12.7 fusion.1072
  171.6 5.2 multiply_reduce_fusion.19
  181.5 3.9 fusion.174
  198.2 6.0 fusion.52
  204.1 9.5 fusion.70
  213.6 7.6 multiply_reduce_fusion.14
  256.4 7.8 fusion.36
  269.7 4.0 fusion.177
  287.3 7.9 fusion.40
  332.6 3.8 fusion.1125
  344.1 5.1 fusion.429
  359.7 5.1 fusion.77
  364.9 7.4 multiply_reduce_fusion.12
  385.4 3.8 fusion.432
  400.3 5.2 fusion.84
  405.6 7.4 multiply_reduce_fusion.10
  443.3 5.0 fusion.91
  448.4 7.4 multiply_reduce_fusion.8
  483.1 8.0 fusion.98
  491.2 7.4 multiply_reduce_fusion.6
  505.9 4.2 fusion.1010
  510.1 6.0 fusion.560
  516.2 4.0 fusion.1007
  520.1 6.0 fusion.558
  526.2 3.9 fusion.1004
  530.1 5.9 fusion.556
  536.0 4.0 fusion.1001
  540.0 5.9 fusion.554
  553.9 4.0 fusion.998
  559.3 6.0 fusion.552
  565.3 25.2 %fusion.13 = f32[1024,3072]{1,0:T(8,128)} fusion(f32[1024,2048]{1,0:T(8,128)} %fusion.560, f32[1024,1024]{1,0:T(8,128)S(1)} %copy-done.13, f32[1024,2048]{1,0:T(8,128)} %fusion.558, f32[1024,1024]{1,0:T(8,128)} %fusion.1007, f32[1024,2048]{1,0:T(8,128)} %fusion.556, f32[1024,1024]{1,0:T(8,128)} %fusion.1004, f32[1024,2048]{1,0:T(8,128)} %fusion.554, ...), kind=kLoop, calls=%fused_computation.16 | loop fusion | flops 44040192 | bytes 75497480 | tf_op jit(solution)/shard_map/add | solution.py:214
  591.0 11.0 fusion.184
  602.0 8.5 fusion.185
  610.5 9.0 fusion.186
  619.5 9.0 fusion.187
  628.5 25.9 %add_add_fusion = f32[4096,1024]{1,0:T(8,128)} fusion(f32[4096,1024]{1,0:T(8,128)} %fusion.187, f32[4096,1024]{1,0:T(8,128)} %fusion.186, f32[4096,1024]{1,0:T(8,128)} %fusion.185, f32[4096,1024]{1,0:T(8,128)} %fusion.184, pred[]{:T(512)S(6)} %and.40, pred[]{:T(512)S(6)} %and.39, pred[]{:T(512)S(6)} %and.38, pred[]{:T(512)S(6)} %and.37, pred[]{:T(512)S(6)} %and.36, ...), kind=kOutput, calls=%fused_computation.10 | convolution fusion | flops 2194669568 | bytes 88604680 | tf_op jit(solution)/shard_map/glf,gld->fd/dot_general | solution.py:23
  655.0 10.4 fusion.994
  665.5 8.6 fusion.995
  674.2 8.7 fusion.996
  683.0 8.7 fusion.997
  691.7 26.0 %add_add_fusion.1 = f32[1024,4096]{1,0:T(8,128)} fusion(f32[1024,4096]{1,0:T(8,128)} %fusion.997, f32[1024,4096]{1,0:T(8,128)} %fusion.996, f32[1024,4096]{1,0:T(8,128)} %fusion.995, f32[1024,4096]{1,0:T(8,128)} %fusion.994, bf16[256,4096]{1,0:T(8,128)(2,1)} %copy-done.118, pred[]{:T(512)S(6)} %and.40, pred[]{:T(512)S(6)} %and.39, pred[]{:T(512)S(6)} %and.38, ...), kind=kOutput, calls=%fused_computation.11 | convolution fusion | flops 2186543104 | bytes 87042056 | tf_op jit(solution)/shard_map/gld,glf->df/dot_general | solution.py:23
  718.8 4.3 fusion.1048
  723.1 4.2 fusion.441
  731.6 6.4 add_bitcast_fusion
  739.9 73.4 %reduce-scatter.9.cloned.1.call-done = f32[64,3072]{1,0:T(8,128)} async-done(((f32[1024,3072]{1,0:T(8,128)}), f32[64,3072]{1,0:T(8,128)}) %reduce-scatter.9.cloned.1.call-update) | async-done | bytes 786448 | tf_op jit(solution)/shard_map/reduce_scatter | solution.py:204
  815.3 346.4 %reduce-scatter.15.cloned.1.call-done = f32[256,1024]{1,0:T(8,128)} async-done(((f32[4096,1024]{1,0:T(8,128)}), f32[256,1024]{1,0:T(8,128)}) %reduce-scatter.15.cloned.1.call-update) | async-done | bytes 1048592 | tf_op jit(solution)/shard_map/reduce_scatter | solution.py:207
  1164.1 352.4 %reduce-scatter.13.cloned.1.call-done = f32[64,4096]{1,0:T(8,128)} async-done(((f32[1024,4096]{1,0:T(8,128)}), f32[64,4096]{1,0:T(8,128)}) %reduce-scatter.13.cloned.1.call-update) | async-done | bytes 1048592 | tf_op jit(solution)/shard_map/reduce_scatter | solution.py:206
  1518.7 4.8 copy.665
  1549.0 12.5 fusion.352
  1561.6 44.8 %psum.7 = f32[]{:T(128)} all-reduce(f32[]{:T(128)} %fusion.992), channel_id=1, replica_groups=mesh['section'=2,'dp'=16] {'dp'}, use_global_device_ids=true, to_apply=%region_177.178 | all-reduce | flops 1 | bytes 8 | tf_op jit(solution)/shard_map/psum | solution.py:217
  1608.4 35.7 %all-gather = bf16[16,64,6]{1,2,0:T(8,128)(2,1)S(1)} all-gather(bf16[1,64,6]{1,2,0:T(8,128)(2,1)S(1)} %bitcast.1637), channel_id=1, replica_groups=mesh['section'=2,'dp'=16] {'dp'}, dimensions={0}, use_global_device_ids=true | all-gather | bytes 13056 | tf_op jit(solution)/shard_map/all_gather | solution.py:232
  1644.8 32.5 %reduce-scatter.17.cloned.1.call-done = f32[16,1024]{1,0:T(8,128)} async-done(((f32[256,1024]{1,0:T(8,128)}), f32[16,1024]{1,0:T(8,128)}) %reduce-scatter.17.cloned.1.call-update) | async-done | bytes 65552 | tf_op jit(solution)/shard_map/reduce_scatter | solution.py:209
  1678.1 40.5 %all_gather.23 = bf16[256,1024]{1,0:T(8,128)(2,1)S(1)} all-gather(bf16[16,1024]{1,0:T(8,128)(2,1)S(1)} %convert_element_type.1247), channel_id=1, replica_groups=mesh['section'=2,'dp'=16] {'dp'}, dimensions={0}, use_global_device_ids=true | all-gather | bytes 557056 | tf_op jit(solution)/shard_map/all_gather | solution.py:235
  1719.7 19.1 all-gather.8.cloned.1.call-done
  1738.8 4.1 bitcast_convert_fusion.3
  1742.9 91.9 %all-gather.6.cloned.1.call-done = bf16[1024,3072]{1,0:T(8,128)(2,1)} async-done(((bf16[64,3072]{1,0:T(8,128)(2,1)}), bf16[1024,3072]{1,0:T(8,128)(2,1)}) %all-gather.6.cloned.1.call-update) | async-done | bytes 6291472 | tf_op jit(solution)/shard_map/all_gather | solution.py:220
  1834.8 9.2 bitcast_convert_fusion.2
  1844.0 105.1 %all-gather.12.cloned.1.call-done = bf16[4096,1024]{1,0:T(8,128)(2,1)} async-done(((bf16[256,1024]{1,0:T(8,128)(2,1)}), bf16[4096,1024]{1,0:T(8,128)(2,1)}) %all-gather.12.cloned.1.call-update) | async-done | bytes 8388624 | tf_op jit(solution)/shard_map/all_gather | solution.py:229
  1949.1 11.7 bitcast_convert_fusion
  1960.8 102.4 %all-gather.10.cloned.1.call-done = bf16[1024,4096]{1,0:T(8,128)(2,1)} async-done(((bf16[64,4096]{1,0:T(8,128)(2,1)}), bf16[1024,4096]{1,0:T(8,128)(2,1)}) %all-gather.10.cloned.1.call-update) | async-done | bytes 8388624 | tf_op jit(solution)/shard_map/all_gather | solution.py:226
  2063.1 11.8 bitcast_convert_fusion.1
  (844 shorter events, 381.3 us)
Async XLA Ops:
  7.2 19.4 copy-start
  7.2 730.9 %reduce-scatter.11.cloned.1.call-start = ((), (), s32[]{:S(2)}) async-start(), calls=%async_computation.11 | async-start | bytes 4456448 | tf_op jit(solution)/shard_map/reduce_scatter | solution.py:205
  11.4 307.0 %copy-start.141 = (f32[1,1,1024]{2,0,1:T(1,128)}, f32[1,1,1024]{2,0,1:T(1,128)S(1)}, u32[]{:S(2)}) copy-start(f32[1,1,1024]{2,0,1:T(1,128)S(1)} %get-tuple-element.217) | copy-start | bytes 12292
  11.4 312.4 %copy-start.119 = (f32[1,1,1024]{2,0,1:T(1,128)}, f32[1,1,1024]{2,0,1:T(1,128)S(1)}, u32[]{:S(2)}) copy-start(f32[1,1,1024]{2,0,1:T(1,128)S(1)} %get-tuple-element.219) | copy-start | bytes 12292
  11.4 384.8 %copy-start.63 = (f32[1,1,1024]{2,0,1:T(1,128)}, f32[1,1,1024]{2,0,1:T(1,128)S(1)}, u32[]{:S(2)}) copy-start(f32[1,1,1024]{2,0,1:T(1,128)S(1)} %get-tuple-element.221) | copy-start | bytes 12292
  44.6 5.3 collective-permute-start
  83.8 3.1 collective-permute-start.1
  121.6 4.1 collective-permute-start.2
  160.3 4.2 collective-permute-start.3
  166.6 10.2 copy-start.39
  171.4 67.6 %copy-start.152 = (f32[256]{0:T(256)}, f32[256]{0:T(256)S(1)}, u32[]{:S(2)}) copy-start(f32[256]{0:T(256)S(1)} %broadcast_multiply_fusion.1) | copy-start | bytes 3076
  171.5 62.1 %copy-start.166 = (f32[256]{0:T(256)}, f32[256]{0:T(256)S(1)}, u32[]{:S(2)}) copy-start(f32[256]{0:T(256)S(1)} %broadcast_multiply_fusion.2) | copy-start | bytes 3076
  176.8 56.8 %copy-start.190 = (f32[256]{0:T(256)}, f32[256]{0:T(256)S(1)}, u32[]{:S(2)}) copy-start(f32[256]{0:T(256)S(1)} %get-tuple-element.56) | copy-start | bytes 3076
  176.8 62.3 %copy-start.192 = (f32[256]{0:T(256)}, f32[256]{0:T(256)S(1)}, u32[]{:S(2)}) copy-start(f32[256]{0:T(256)S(1)} %get-tuple-element.80) | copy-start | bytes 3076
  176.8 87.5 %copy-start.194 = (f32[256]{0:T(256)}, f32[256]{0:T(256)S(1)}, u32[]{:S(2)}) copy-start(f32[256]{0:T(256)S(1)} %get-tuple-element.57) | copy-start | bytes 3076
  176.8 92.9 %copy-start.196 = (f32[256]{0:T(256)}, f32[256]{0:T(256)S(1)}, u32[]{:S(2)}) copy-start(f32[256]{0:T(256)S(1)} %get-tuple-element.76) | copy-start | bytes 3076
  181.4 9.0 copy-start.108
  197.8 23.4 %copy-start.4 = (f32[256,1024]{1,0:T(8,128)}, f32[256,1024]{1,0:T(8,128)S(1)}, u32[]{:S(2)}) copy-start(f32[256,1024]{1,0:T(8,128)S(1)} %get-tuple-element.245) | copy-start | bytes 3145732
  197.8 23.4 %copy-start.144 = (f32[256]{0:T(256)}, f32[256]{0:T(256)S(1)}, u32[]{:S(2)}) copy-start(f32[256]{0:T(256)S(1)} %broadcast_multiply_fusion.12) | copy-start | bytes 3076
  198.1 23.1 %copy-start.154 = (f32[256]{0:T(256)}, f32[256]{0:T(256)S(1)}, u32[]{:S(2)}) copy-start(f32[256]{0:T(256)S(1)} %fusion.902) | copy-start | bytes 3076
  204.1 9.5 copy-start.42
  221.7 132.3 %copy-start.162 = (f32[256]{0:T(256)}, f32[256]{0:T(256)S(1)}, u32[]{:S(2)}) copy-start(f32[256]{0:T(256)S(1)} %negate_multiply_fusion.14) | copy-start | bytes 3076
  232.5 111.6 %copy-start.74 = (bf16[8,128,256]{2,1,0:T(8,128)(2,1)}, bf16[8,128,256]{2,1,0:T(8,128)(2,1)S(1)}, u32[]{:S(2)}) copy-start(bf16[8,128,256]{2,1,0:T(8,128)(2,1)S(1)} %fusion.367) | copy-start | bytes 1572868
  287.0 168.8 %copy-start.146 = (f32[256]{0:T(256)}, f32[256]{0:T(256)S(1)}, u32[]{:S(2)}) copy-start(f32[256]{0:T(256)S(1)} %broadcast_multiply_fusion.3) | copy-start | bytes 3076
  287.2 168.5 %copy-start.156 = (f32[256]{0:T(256)}, f32[256]{0:T(256)S(1)}, u32[]{:S(2)}) copy-start(f32[256]{0:T(256)S(1)} %fusion.911) | copy-start | bytes 3076
  317.1 95.9 %copy-start.148 = (f32[256]{0:T(256)}, f32[256]{0:T(256)S(1)}, u32[]{:S(2)}) copy-start(f32[256]{0:T(256)S(1)} %broadcast_multiply_fusion.6) | copy-start | bytes 3076
  318.3 94.7 %copy-start.158 = (f32[256]{0:T(256)}, f32[256]{0:T(256)S(1)}, u32[]{:S(2)}) copy-start(f32[256]{0:T(256)S(1)} %fusion.908) | copy-start | bytes 3076
  339.3 17.7 slice-start.6
  341.3 31.0 %copy-start.11 = (f32[256,1024]{1,0:T(8,128)}, f32[256,1024]{1,0:T(8,128)S(1)}, u32[]{:S(2)}) copy-start(f32[256,1024]{1,0:T(8,128)S(1)} %get-tuple-element.253) | copy-start | bytes 3145732
  341.3 30.9 %copy-start.150 = (f32[256]{0:T(256)}, f32[256]{0:T(256)S(1)}, u32[]{:S(2)}) copy-start(f32[256]{0:T(256)S(1)} %broadcast_multiply_fusion.9) | copy-start | bytes 3076
  341.6 30.7 %copy-start.160 = (f32[256]{0:T(256)}, f32[256]{0:T(256)S(1)}, u32[]{:S(2)}) copy-start(f32[256]{0:T(256)S(1)} %fusion.905) | copy-start | bytes 3076
  344.1 12.9 slice-start.7
  355.4 4.2 collective-permute-start.4
  359.7 31.6 %copy-start.26 = (bf16[1,256,1024]{2,1,0:T(8,128)(2,1)}, bf16[1,256,1024]{2,1,0:T(8,128)(2,1)S(1)}, u32[]{:S(2)}) copy-start(bf16[1,256,1024]{2,1,0:T(8,128)(2,1)S(1)} %dynamic-slice_select_fusion.3) | copy-start | bytes 1572868
  372.7 18.6 copy-start.168
  383.5 12.7 slice-start.8
  385.4 10.8 slice-start.9
  394.6 4.2 collective-permute-start.5
  400.3 31.5 %copy-start.28 = (bf16[1,256,1024]{2,1,0:T(8,128)(2,1)}, bf16[1,256,1024]{2,1,0:T(8,128)(2,1)S(1)}, u32[]{:S(2)}) copy-start(bf16[1,256,1024]{2,1,0:T(8,128)(2,1)S(1)} %dynamic-slice_select_fusion.2) | copy-start | bytes 1572868
  413.4 18.4 copy-start.170
  431.8 11.5 slice-start.4
  435.1 7.1 collective-permute-start.6
  443.3 31.3 %copy-start.30 = (bf16[1,256,1024]{2,1,0:T(8,128)(2,1)}, bf16[1,256,1024]{2,1,0:T(8,128)(2,1)S(1)}, u32[]{:S(2)}) copy-start(bf16[1,256,1024]{2,1,0:T(8,128)(2,1)S(1)} %dynamic-slice_select_fusion.1) | copy-start | bytes 1572868
  456.2 18.4 copy-start.174
  477.9 4.1 collective-permute-start.7
  491.2 9.9 copy-start.3
  505.3 308.0 %reduce-scatter.9.cloned.1.call-start = ((), (), s32[]{:S(2)}) async-start(), calls=%async_computation.10 | async-start | bytes 13369344 | tf_op jit(solution)/shard_map/reduce_scatter | solution.py:204
  590.5 571.2 %reduce-scatter.15.cloned.1.call-start = ((), (), s32[]{:S(2)}) async-start(), calls=%async_computation.13 | async-start | bytes 17825792 | tf_op jit(solution)/shard_map/reduce_scatter | solution.py:207
  590.9 11.0 copy-start.27
  590.9 11.0 copy-start.46
  610.5 9.0 copy-start.31
  610.5 9.0 copy-start.44
  654.4 11.1 copy-start.151
  654.4 11.1 copy-start.161
  654.4 862.1 %reduce-scatter.13.cloned.1.call-start = ((), (), s32[]{:S(2)}) async-start(), calls=%async_computation.12 | async-start | bytes 17825792 | tf_op jit(solution)/shard_map/reduce_scatter | solution.py:206
  655.0 10.4 copy-start.12
  655.0 10.4 copy-start.113
  674.2 8.8 copy-start.7
  717.9 889.6 %reduce-scatter.19.cloned.1.call-start = ((), (), s32[]{:S(2)}) async-start(), calls=%async_computation.15 | async-start | bytes 557056
  731.5 945.8 %reduce-scatter.17.cloned.1.call-start = ((), (), s32[]{:S(2)}) async-start(), calls=%async_computation.14 | async-start | bytes 1114112 | tf_op jit(solution)/shard_map/reduce_scatter | solution.py:209
  738.0 1000.8 %all-gather.8.cloned.1.call-start = ((), (), s32[]{:S(2)}) async-start(), calls=%async_computation.7 | async-start | bytes 2228224 | tf_op jit(solution)/shard_map/all_gather | solution.py:223
  739.8 1094.9 %all-gather.6.cloned.1.call-start = ((), (), s32[]{:S(2)}) async-start(), calls=%async_computation.6 | async-start | bytes 6684672 | tf_op jit(solution)/shard_map/all_gather | solution.py:220
  815.2 1133.8 %all-gather.12.cloned.1.call-start = ((), (), s32[]{:S(2)}) async-start(), calls=%async_computation.9 | async-start | bytes 8912896 | tf_op jit(solution)/shard_map/all_gather | solution.py:229
  1163.8 899.3 %all-gather.10.cloned.1.call-start = ((), (), s32[]{:S(2)}) async-start(), calls=%async_computation.8 | async-start | bytes 8912896 | tf_op jit(solution)/shard_map/all_gather | solution.py:226
  (204 other events, 737.3 us)
Sparse Core Ops, SparseCore 0:
  505.4 97.8 reduce-scatter.10
  609.5 203.7 reduce-scatter.8
  815.6 345.9 reduce-scatter.14
  1164.5 352.0 reduce-scatter.12
  1518.7 82.1 reduce-scatter.18
  1603.0 74.1 reduce-scatter.16
  1680.4 58.3 all-gather.7
  1741.9 92.7 all-gather.5
  1837.9 111.0 all-gather.11
  1952.1 111.0 all-gather.9
where the time goes:
time: 2090 us; the launch traced here: 2080 us
  waiting for transfers between devices  1130 us (54%)
  matrix products  543 us (26%)
  other arithmetic  146 us (7%)
  blocking collectives  121 us (6%)
  local copies, waits for them, and re-layouts  106 us (5%)
    dot_general x120, matrix products, matmul(): return jnp.einsum(form, left, right, preferred_element_type=jnp.float32)  510 us
    reduce_scatter x1, waiting for transfers between devices, body(): lax.psum_scatter(grad_terms[2], 'dp', scatter_dimension=0, tiled=True)  352 us
    reduce_scatter x1, waiting for transfers between devices, body(): lax.psum_scatter(grad_terms[3], 'dp', scatter_dimension=0, tiled=True)  346 us
    all_gather x1, waiting for transfers between devices, body(): lax.all_gather(totals[3].astype(jnp.bfloat16), 'dp', axis=0, tiled=True)  105 us
    all_gather x1, waiting for transfers between devices, body(): lax.all_gather(totals[2].astype(jnp.bfloat16), 'dp', axis=0, tiled=True)  102 us
    all_gather x1, waiting for transfers between devices, body(): lax.all_gather(totals[0].astype(jnp.bfloat16), 'dp', axis=0, tiled=True)  91.9 us
    reduce_scatter x1, waiting for transfers between devices, body(): lax.psum_scatter(grad_terms[0], 'dp', scatter_dimension=0, tiled=True)  73.4 us
    unnamed x519, local copies, waits for them, and re-layouts  54.5 us
  transfers between devices with their start and end apart: 18, of which 14 were waited for; matrix products, arithmetic and copies ran while one was open for 15% of the time, Pallas kernels for 0%

commit v1 on v0

v1 whole, which is shorter than its diff:
```python
import functools
import jax
import jax.numpy as jnp
from jax import lax
from jax.experimental import pallas as pl
from jax.experimental.pallas import tpu as pltpu
from jax.sharding import PartitionSpec as P

HEADS = 8
MESH = pl.DeviceIdType.MESH
TILE = 256
RING = 8
WIDTH = 1024
SPLIT = (80, 64, 48, 64)
ORDERS = ((2, 1, 0), (1, 2, 0), (0, 2, 1), (0, 1, 2))


def lines_of(size):
    short = 1
    while 2 * short**3 < size:
        short += 1
    assert 2 * short**3 == size
    return (2 * short, short, short)


class Plan:
    def __init__(self, dims):
        d = lax.axis_index("dp")
        self.d = d
        self.dims = dims
        self.strides = (dims[1] * dims[2], dims[2], 1)
        self.coords = tuple(lax.rem(lax.div(d, s), n) for s, n in zip(self.strides, dims))
        self.depth = 2 * (sum(dims) - 3)


def stages(plan):
    found = []
    row = 0
    for kind, order in enumerate(ORDERS):
        delay = 0
        left, free = 0, 0
        active = None
        bases = []
        for phase, axis in enumerate(order):
            n, c = plan.dims[axis], plan.coords[axis]
            w = WIDTH >> (phase + 1)
            bases.append((delay, left, free, active, axis, w))
            delay += n - 1
            top = c == n - 1
            left = left + jnp.where(top, w, 0)
            free = free + jnp.where(top, 0, w)
            if n > 2:
                end = (c == 0) | top
                active = end if active is None else active & end
        for phase in range(3):
            found.append(("sum", kind, phase, row) + tuple(bases[phase]))
        for phase in (2, 1, 0):
            _, left, free, active, axis, w = bases[phase]
            found.append(("spread", kind, phase, row, delay, left, free, active, axis, w))
            delay += plan.dims[axis] - 1
        row += SPLIT[kind]
    return found


def both(*terms):
    out = None
    for t in terms:
        if t is None:
            continue
        out = t if out is None else out & t
    return out


def copies(plan, stage, up, tick, total, held, landing, result, send_sem, recv_sem):
    what, kind, phase, row, delay, left, free, active, axis, w = stage
    n, c, stride = plan.dims[axis], plan.coords[axis], plan.strides[axis]
    toward_top = up if what == "sum" else not up
    hops = c if toward_top else n - 1 - c
    job = tick - delay - hops
    ok = both(job >= 0, job < total, active)
    job = jnp.clip(job, 0, total - 1)
    rows = pl.ds(row, SPLIT[kind])
    col = pl.ds(pl.multiple_of(left + (w if up else 0), 128), w)
    stream = (kind * 6 + (phase if what == "sum" else 3 + phase)) * 2 + int(up)
    if what == "sum":
        land = pl.ds(pl.multiple_of(free + (w if up else 0), 128), w)
        src = held.at[job, rows, col]
        dst = landing.at[job, rows, land]
    else:
        src = result.at[job, rows, col]
        dst = result.at[job, rows, col]
    step = stride if toward_top else -stride
    def make(source):
        return pltpu.make_async_remote_copy(
            src_ref=source, dst_ref=dst,
            send_sem=send_sem.at[stream, lax.rem(job, RING)], recv_sem=recv_sem.at[stream, job],
            device_id={"dp": plan.d + step}, device_id_type=MESH)
    def send(source):
        copy = make(source)
        @pl.when(job >= RING)
        def _():
            copy.wait_send()
        copy.start()
    return make, send, src, dst, ok, hops, n, job, rows, col


def comm_tick(plan, table, kinds, tick, total, held, landing, result, send_sem, recv_sem, own_sem):
    for stage in table:
        what, kind, phase = stage[:3]
        if kind not in kinds:
            continue
        for up in (True, False):
            make, send, src, dst, ok, hops, n, job, rows, col = copies(
                plan, stage, up, tick, total, held, landing, result, send_sem, recv_sem)
            if what == "sum":
                @pl.when(ok & (hops > 0))
                def _():
                    make(src).wait_recv()
                    held[job, rows, col] = held[job, rows, col] + dst[...]
                @pl.when(ok & (hops < n - 1))
                def _():
                    send(src)
            else:
                if phase == 2:
                    @pl.when(ok & (hops == 0))
                    def _():
                        mine = held.at[job, rows, col]
                        send(mine)
                        pltpu.make_async_copy(mine, dst, own_sem.at[kind, job]).start()
                    @pl.when(ok & (hops > 0))
                    def _():
                        make(src).wait_recv()
                    if n > 2:
                        @pl.when(ok & (hops > 0) & (hops < n - 1))
                        def _():
                            send(src)
                else:
                    if phase == 1:
                        last = [s for s in table if s[1] == kind and s[0] == "spread" and s[2] == 2][0]
                        _, _, _, _, _, left3, _, active3, axis3, w3 = last
                        c3, n3 = plan.coords[axis3], plan.dims[axis3]
                        top3 = c3 == n3 - 1
                        own = held.at[job, rows, pl.ds(pl.multiple_of(left3 + jnp.where(top3, w3, 0), 128), w3)]
                        own_dst = result.at[job, rows, pl.ds(pl.multiple_of(left3 + jnp.where(top3, w3, 0), 128), w3)]
                        @pl.when(both(ok, hops == 0, (c3 == 0) | top3 if n3 > 2 else None))
                        def _():
                            pltpu.make_async_copy(own, own_dst, own_sem.at[kind, job]).wait()
                    @pl.when(ok & (hops > 0))
                    def _():
                        make(src).wait_recv()
                    @pl.when(ok & (hops < n - 1))
                    def _():
                        send(src)


def drain(plan, table, tick, total, held, landing, result, send_sem, recv_sem):
    for stage in table:
        what, kind, phase = stage[:3]
        for up in (True, False):
            make, send, src, dst, ok, hops, n, job, rows, col = copies(
                plan, stage, up, tick, total, held, landing, result, send_sem, recv_sem)
            @pl.when(ok & (hops < n - 1) & (job >= total - RING))
            def _():
                make(src).wait_send()


def greet(plan):
    barrier = pltpu.get_barrier_semaphore()
    count = 0
    for n, c, s in zip(plan.dims, plan.coords, plan.strides):
        for inside, step in ((c > 0, -s), (c < n - 1, s)):
            @pl.when(inside)
            def _():
                pl.semaphore_signal(barrier, inc=1, device_id={"dp": plan.d + step}, device_id_type=MESH)
            count = count + inside.astype(jnp.int32)
    pl.semaphore_wait(barrier, count)


def weights_kernel(dims, jobs, extra, left_ref, right_ref, extra_ref, result, held, landing,
                   left_buf, right_buf, load_sem, send_sem, recv_sem, own_sem):
    plan = Plan(dims)
    table = stages(plan)
    total = 4 * jobs + extra
    greet(plan)

    def left_copy(s):
        job, part, slot = lax.div(s, 4), lax.rem(s, 4), lax.rem(s, 2)
        slab = jnp.where(job < 4, job, jnp.where(job < 8, 4, jnp.minimum(job - 3, 7)))
        return pltpu.make_async_copy(
            left_ref.at[:, pl.ds(pl.multiple_of(slab * WIDTH + part * TILE, TILE), TILE)],
            left_buf.at[slot], load_sem.at[slot])

    def right_copy(job):
        slot = lax.rem(job, 2)
        slab = jnp.where(job < 4, 0, job - 3)
        return pltpu.make_async_copy(
            right_ref.at[:, pl.ds(pl.multiple_of(slab * WIDTH, WIDTH), WIDTH)],
            right_buf.at[slot], load_sem.at[2 + slot])

    def product(s):
        job = lax.div(s, 4)
        left_copy(s).wait()
        @pl.when(lax.rem(s, 4) == 0)
        def _():
            right_copy(job).wait()
            @pl.when(job + 1 < jobs)
            def _():
                right_copy(job + 1).start()
        @pl.when(s + 1 < 4 * jobs)
        def _():
            left_copy(s + 1).start()
        a = left_buf[lax.rem(s, 2)]
        b = right_buf[lax.rem(job, 2)]
        held[s] = lax.dot_general(a, b, (((0,), (0,)), ((), ())), preferred_element_type=jnp.float32).astype(jnp.bfloat16)

    extras = pltpu.make_async_copy(extra_ref, held.at[pl.ds(4 * jobs, extra)], load_sem.at[4])
    extras.start()
    left_copy(0).start()
    right_copy(0).start()
    product(0)
    extras.wait()

    args = (total, held, landing, result, send_sem, recv_sem)

    def tick(t, _):
        comm_tick(plan, table, (0, 2), t, *args, own_sem)
        @pl.when(t + 1 < 4 * jobs)
        def _():
            product(t + 1)
        comm_tick(plan, table, (1, 3), t, *args, own_sem)
        return 0

    lax.fori_loop(0, total + plan.depth, tick, 0)

    def finish(t, _):
        drain(plan, table, t, *args)
        return 0

    lax.fori_loop(0, total + plan.depth, finish, 0)


def weight_sums(dims, lefts, rights, extras, cid):
    jobs, extra = 12, extras.shape[0]
    total = 4 * jobs + extra
    rows = lefts.shape[0]
    any_space = pl.BlockSpec(memory_space=pl.ANY)
    return pl.pallas_call(
        functools.partial(weights_kernel, dims, jobs, extra),
        out_shape=jax.ShapeDtypeStruct((total, TILE, WIDTH), jnp.bfloat16),
        in_specs=[any_space] * 3,
        out_specs=any_space,
        scratch_shapes=[
            pltpu.VMEM((total, TILE, WIDTH), jnp.bfloat16),
            pltpu.VMEM((total, TILE, WIDTH), jnp.bfloat16),
            pltpu.VMEM((2, rows, TILE), jnp.bfloat16),
            pltpu.VMEM((2, rows, WIDTH), jnp.bfloat16),
            pltpu.SemaphoreType.DMA((5,)),
            pltpu.SemaphoreType.DMA((48, RING)),
            pltpu.SemaphoreType.DMA((48, total)),
            pltpu.SemaphoreType.DMA((4, total)),
        ],
        compiler_params=pltpu.CompilerParams(collective_id=cid, has_side_effects=True, vmem_limit_bytes=62 * 2**20),
        cost_estimate=pl.CostEstimate(flops=2 * 12 * rows * WIDTH * WIDTH, bytes_accessed=100 * 2**20, transcendentals=0),
    )(lefts, rights, extras)


def layer_norm(values, gain_row, shift_row):
    center = values - jnp.mean(values, -1, keepdims=True)
    spread = jnp.mean(center * center, -1, keepdims=True)
    return center * lax.rsqrt(spread + 1e-05) * gain_row + shift_row


def matmul(left, right, form):
    return jnp.einsum(form, left, right, preferred_element_type=jnp.float32)


def advance(base_in, source, visible, w_qkv, w_out, w_up, w_down, params):
    query_in, query_back = jax.vjp(layer_norm, base_in, params[0], params[1])
    key_in, key_back = jax.vjp(layer_norm, source, params[2], params[3])
    query_low = query_in.astype(jnp.bfloat16)
    key_low = key_in.astype(jnp.bfloat16)
    features = query_low.shape[-1]
    queries = matmul(query_low, w_qkv[:, :features], "gld,de->gle").astype(jnp.bfloat16)
    key_vals = matmul(key_low, w_qkv[:, features:], "gld,de->gle").astype(jnp.bfloat16)
    groups, positions = (queries.shape[0], queries.shape[1])
    head_shape = (groups, positions, HEADS, features // HEADS)
    head_scale = (features // HEADS) ** (-0.5)
    heads_q = queries.reshape(head_shape)
    heads_k = key_vals[..., :features].reshape(head_shape)
    heads_v = key_vals[..., features:].reshape(head_shape)
    scores = matmul(heads_q, heads_k, "gqhd,gkhd->ghqk") * head_scale
    scores = jnp.where(visible[:, None, None, :], scores, -1e30)
    row_max = jnp.max(scores, -1, keepdims=True)
    exponent = jnp.exp(scores - row_max)
    weights_soft = exponent / jnp.sum(exponent, -1, keepdims=True)
    weights_low = weights_soft.astype(jnp.bfloat16)
    mixed_out = (
        matmul(weights_low, heads_v, "ghqk,gkhd->gqhd")
        .reshape(groups, positions, features)
        .astype(jnp.bfloat16)
    )
    hidden = base_in + matmul(mixed_out, w_out, "gld,de->gle")
    normed, normed_back = jax.vjp(layer_norm, hidden, params[4], params[5])
    normed_low = normed.astype(jnp.bfloat16)
    upward = matmul(normed_low, w_up, "gld,df->glf")
    active, active_back = jax.vjp(jax.nn.gelu, upward)
    active_low = active.astype(jnp.bfloat16)
    outcome = hidden + matmul(active_low, w_down, "glf,fd->gld")
    stored_parts = (
        query_back,
        key_back,
        query_low,
        key_low,
        heads_q,
        heads_k,
        heads_v,
        weights_soft,
        weights_low,
        mixed_out,
        normed_back,
        normed_low,
        active_back,
        active_low,
    )
    return (outcome, stored_parts)


def retreat(stored_parts, w_qkv, w_out, w_up, w_down, grad_outcome):
    (
        query_back,
        key_back,
        query_low,
        key_low,
        heads_q,
        heads_k,
        heads_v,
        weights_soft,
        weights_low,
        mixed_out,
        normed_back,
        normed_low,
        active_back,
        active_low,
    ) = stored_parts
    features = query_low.shape[-1]
    groups, positions = (query_low.shape[0], query_low.shape[1])
    head_scale = (features // HEADS) ** (-0.5)
    outcome_low = grad_outcome.astype(jnp.bfloat16)
    grad_active = matmul(outcome_low, w_down, "gld,fd->glf")
    (grad_upward,) = active_back(grad_active)
    upward_low = grad_upward.astype(jnp.bfloat16)
    grad_normed = matmul(upward_low, w_up, "glf,df->gld")
    grad_from_norm, grad_gain_mlp, grad_shift_mlp = normed_back(grad_normed)
    grad_hidden = grad_outcome + grad_from_norm
    hidden_low = grad_hidden.astype(jnp.bfloat16)
    grad_mixed = (
        matmul(hidden_low, w_out, "gle,de->gld").astype(jnp.bfloat16).reshape(heads_q.shape)
    )
    grad_weights = matmul(grad_mixed, heads_v, "gqhd,gkhd->ghqk")
    grad_values = matmul(weights_low, grad_mixed, "ghqk,gqhd->gkhd").astype(jnp.bfloat16)
    grad_scores = weights_soft * (
        grad_weights - jnp.sum(grad_weights * weights_soft, -1, keepdims=True)
    )
    scores_low = grad_scores.astype(jnp.bfloat16)
    grad_queries = (matmul(scores_low, heads_k, "ghqk,gkhd->gqhd") * head_scale).astype(
        jnp.bfloat16
    )
    grad_keys = (matmul(scores_low, heads_q, "ghqk,gqhd->gkhd") * head_scale).astype(jnp.bfloat16)
    grad_queries = grad_queries.reshape(groups, positions, features)
    grad_keys = grad_keys.reshape(groups, positions, features)
    grad_values = grad_values.reshape(groups, positions, features)
    grad_query_in = matmul(grad_queries, w_qkv[:, :features], "gle,de->gld")
    grad_key_in = matmul(grad_keys, w_qkv[:, features : 2 * features], "gle,de->gld") + matmul(
        grad_values, w_qkv[:, 2 * features :], "gle,de->gld"
    )
    grad_base_norm, grad_gain_q, grad_shift_q = query_back(grad_query_in)
    grad_source, grad_gain_k, grad_shift_k = key_back(grad_key_in)
    grad_base = grad_hidden + grad_base_norm
    grad_params = jnp.stack(
        [grad_gain_q, grad_shift_q, grad_gain_k, grad_shift_k, grad_gain_mlp, grad_shift_mlp]
    )
    rights = (outcome_low, upward_low, hidden_low, grad_queries, grad_keys, grad_values)
    return rights, grad_params, grad_base, grad_source


def body(tokens, clip_frames, cotangent, embed, norm_params, w_qkv, w_out, w_up, w_down):
    is_first = lax.axis_index("section") == 0
    matrices = (w_qkv[0], w_out[0], w_up[0], w_down[0])
    params = norm_params[0]
    embed_row = embed[0].astype(jnp.float32)
    groups, positions, features = tokens.shape
    slot_ids = jnp.arange(positions, dtype=jnp.int32)
    visible = (slot_ids[None, :] < clip_frames[:, None] * (positions // 16)) | jnp.logical_not(
        is_first
    )

    def forward(source):
        source_wide = source.astype(jnp.float32)
        base_in = jnp.where(is_first, 0.0, source_wide) + embed_row
        return advance(base_in, source_wide, visible, *matrices, params)

    early, _ = forward(tokens)
    received = lax.ppermute(early.astype(jnp.bfloat16), "section", [(0, 1)])
    outcome, stored = forward(jnp.where(is_first, tokens, received))

    def backward(upstream):
        rights, grad_params, grad_base, grad_source = retreat(
            stored, *matrices, upstream.astype(jnp.float32)
        )
        sent = (grad_source + grad_base).astype(jnp.bfloat16)
        return rights, grad_params, grad_base, grad_source, sent

    sent_early = backward(cotangent)[-1]
    arriving = lax.ppermute(sent_early, "section", [(1, 0)])
    rights, grad_params, grad_base, grad_source, sent = backward(
        jnp.where(is_first, arriving, cotangent)
    )
    grad_inputs = jnp.where(is_first, grad_source, sent.astype(jnp.float32))
    rows = groups * positions
    flat = lambda parts: jnp.concatenate([p.reshape(rows, -1) for p in parts], axis=1)
    (_, _, query_low, key_low, _, _, _, _, _, mixed_low, _, normed_low, _, active_low) = stored
    lefts = flat((active_low, normed_low, mixed_low, query_low, key_low))
    rights = flat(rights)
    magnitude = jnp.sqrt(jnp.mean(grad_inputs * grad_inputs, axis=(1, 2)) + 1e-06)
    overall = lax.psum(jnp.sum(magnitude), "dp")
    norms = magnitude / (overall / (groups * lax.axis_size("dp")))
    extras = jnp.stack(
        [jnp.sum(grad_base, axis=0), jnp.pad(grad_params, ((0, TILE - 6), (0, 0)))]
    ).astype(jnp.bfloat16)
    sums = weight_sums(lines_of(lax.axis_size("dp")), lefts, rights, extras, 1)
    blocks = sums[:48].reshape(12, 1024, 1024)
    beside = lambda first, last: (
        blocks[first:last].transpose(1, 0, 2).reshape(1024, -1).astype(jnp.float32)
    )
    return (
        outcome[None],
        grad_inputs[None],
        beside(9, 12)[None],
        beside(8, 9)[None],
        beside(4, 8)[None],
        blocks[0:4].reshape(4096, 1024).astype(jnp.float32)[None],
        sums[49, :6].astype(jnp.float32)[None],
        sums[48].astype(jnp.float32)[None],
        norms[None],
    )


def solution(mesh):
    placed = (
        P("dp", None, None),
        P("dp"),
        P("dp", None, None),
        P("section", None, None),
        P("section", None, None),
        P("section", None, None),
        P("section", None, None),
        P("section", None, None),
        P("section", None, None),
    )
    return jax.shard_map(
        body,
        mesh=mesh,
        in_specs=placed,
        out_specs=(
            P("section", "dp", None, None),
            P("section", "dp", None, None),
            P("section", None, None),
            P("section", None, None),
            P("section", None, None),
            P("section", None, None),
            P("section", None, None),
            P("section", None, None),
            P("section", "dp"),
        ),
        check_vma=False,
    )
```

time: 2090 us -> 967 us (0.46)
  waiting for transfers between devices: 1130 us -> 3.64 us
  Pallas kernels: 0 us -> 396 us
  matrix products: 543 us -> 254 us
  blocking collectives: 121 us -> 41 us
  local copies, waits for them, and re-layouts: 106 us -> 169 us
  other arithmetic: 146 us -> 91.5 us
    reduce_scatter x5 -> x0, waiting for transfers between devices: 805 us -> none  [the longest x1 352 us: body(): lax.psum_scatter(grad_terms[2], 'dp', scatter_dimension=0, tiled=True)]
    pallas_call x0 -> x1, Pallas kernels: none -> 396 us  [weight_sums(): pl.pallas_call(functools.partial(weights_kernel, dims, jobs, extra), out_...]
    all_gather x4 -> x0, waiting for transfers between devices: 318 us -> none  [the longest x1 105 us: body(): lax.all_gather(totals[3].astype(jnp.bfloat16), 'dp', axis=0, tiled=True)]
    dot_general x120 -> x32, matrix products: 510 us -> 245 us  [matmul(): return jnp.einsum(form, left, right, preferred_element_type=jnp.float32)]
    all_gather x2 -> x0, blocking collectives: 76.2 us -> none  [the longest x1 40.5 us: body(): lax.all_gather(totals[5].astype(jnp.bfloat16), 'dp', axis=0, tiled=True)]
    convert_element_type x0 -> x7, local copies, waits for them, and re-layouts: none -> 71.4 us  [the longest x3 54 us: body(): blocks[first:last].transpose(1, 0, 2).reshape(1024, -1).astype(jnp.float32)]
    another operation x22 -> x1, local copies, waits for them, and re-layouts: 44.2 us -> 0.05 us  [body(): jnp.stack([jnp.sum(grad_base, axis=0), jnp.pad(grad_params, ((0, TILE - 6...]
    convert_element_type x5 -> x10, other arithmetic: 8.67 us -> 43.8 us  [the longest x3 20.6 us: body(): blocks[first:last].transpose(1, 0, 2).reshape(1024, -1).astype(jnp.float32)]
  transfers between devices with their start and end apart: 18 -> 2, of which waited for: 14 -> 1; matrix products, arithmetic and copies ran while one was open for 15% -> 3% of each run, Pallas kernels for 0% -> 0%
where the time goes in v1:
time: 967 us; the launch traced here: 962 us
  Pallas kernels  396 us (41%)
  matrix products  254 us (26%)
  local copies, waits for them, and re-layouts  169 us (17%)
  other arithmetic  91.5 us (9%)
  blocking collectives  41 us (4%)
    pallas_call x1, Pallas kernels, weight_sums(): pl.pallas_call(functools.partial(weights_kernel, dims, jobs, extra), out_...  396 us
    dot_general x32, matrix products, matmul(): return jnp.einsum(form, left, right, preferred_element_type=jnp.float32)  245 us
    unnamed x166, local copies, waits for them, and re-layouts  57.9 us
    convert_element_type x3, local copies, waits for them, and re-layouts, body(): blocks[first:last].transpose(1, 0, 2).reshape(1024, -1).astype(jnp.float32)  54 us
    psum x1, blocking collectives, body(): overall = lax.psum(jnp.sum(magnitude), 'dp')  41 us
    convert_element_type x3, other arithmetic, body(): blocks[first:last].transpose(1, 0, 2).reshape(1024, -1).astype(jnp.float32)  20.6 us
  transfers between devices with their start and end apart: 2, of which 1 were waited for; matrix products, arithmetic and copies ran while one was open for 3% of the time, Pallas kernels for 0%

profile of v1, /device:TPU:0, one launch (start us, length us, event | category | flops | bytes accessed | tf_op | source)
XLA Modules:
  0.0 961.6 jit_solution(10346067352705745697)
XLA Ops:
  3.4 2.4 fusion.58
  8.1 5.1 convolution_convert_fusion.1
  13.2 2.7 slice_bitcast_fusion.6
  15.9 3.9 copy.113
  19.9 4.4 convert_bitcast_fusion.1
  25.7 3.1 fusion.201
  30.3 3.0 fusion.202
  34.0 12.3 %fusion.28 = f32[4,256,4096]{2,1,0:T(8,128)} fusion(bf16[1,1024,4096]{2,1,0:T(8,128)(2,1)S(1)} %bitcast.306, f32[4,256,1024]{2,1,0:T(8,128)S(1)} %get-tuple-element.69, f32[1024]{0:T(1024)S(1)} %bitcast.299, f32[1024]{0:T(1024)S(1)} %bitcast.286, f32[4,256]{1,0:T(4,128)S(1)} %add_rsqrt_fusion, f32[4,256]{1,0:T(4,128)S(1)} %broadcast_multiply_fusion.3), kind=kOutput, calls=%fused_computation.38 | convolution fusion | flops 8595177472 | bytes 29376512 | tf_op jit(solution)/shard_map/gld,df->glf/dot_general | solution.py:274
  46.2 16.8 %add_convert_fusion.6 = bf16[4,256,1024]{2,1,0:T(8,128)(2,1)S(1)} fusion(f32[4,256,1024]{2,1,0:T(8,128)S(1)} %get-tuple-element.69, bf16[1,4096,1024]{2,1,0:T(8,128)(2,1)} %param.17, f32[4,256,4096]{2,1,0:T(8,128)} %fusion.28), kind=kOutput, calls=%fused_computation.135 | convolution fusion | flops 8629780480 | bytes 31457280 | tf_op jit(solution)/shard_map/glf,fd->gld/dot_general | solution.py:274
  63.0 2.5 collective-permute-start
  65.5 3.6 collective-permute-done
  72.6 2.9 fusion.81
  76.8 5.3 convolution_convert_fusion.4
  82.1 3.9 copy.114
  86.0 7.3 convolution_convert_fusion
  93.3 2.7 fusion.199
  96.0 4.1 copy.115
  100.1 8.9 fusion.203
  109.0 5.2 fusion.144
  114.2 2.8 fusion.204
  119.8 19.8 %multiply_convert_fusion = (bf16[4,256,4096]{2,1,0:T(8,128)(2,1)}, f32[4,256,4096]{2,1,0:T(8,128)}) fusion(bf16[4,256,1024]{2,1,0:T(8,128)(2,1)S(1)} %add_convert_fusion.5, bf16[1,1024,4096]{2,1,0:T(8,128)(2,1)} %param.16), kind=kOutput, calls=%fused_computation.21 | convolution fusion | flops 8627683328 | bytes 35651584 | tf_op jit(solution)/shard_map/gld,df->glf/dot_general | solution.py:274
  139.6 31.9 %multiply_reduce_fusion.5 = (f32[4,256]{1,0:T(4,128)S(1)}, f32[4,256,1024]{2,1,0:T(8,128)}) fusion(f32[4,256,1024]{2,1,0:T(8,128)} %copy-done.2, f32[4,256]{1,0:T(4,128)S(1)} %broadcast_multiply_fusion, f32[1024]{0:T(1024)S(1)} %bitcast.288, bf16[1,1024,4096]{2,1,0:T(8,128)(2,1)} %param.16, f32[4,256,4096]{2,1,0:T(8,128)} %get-tuple-element.75, ...), kind=kOutput, calls=%fused_computation.130 | convolution fusion | flops 17267949568 | bytes 44052480 | tf_op jit(solution)/shard_map/glf,df->gld/dot_general | solution.py:274
  171.5 4.3 fusion.197
  177.8 3.7 fusion.149
  181.6 4.0 copy.116
  185.5 7.0 convolution_convert_fusion.3
  192.6 4.4 multiply_reduce_fusion.1
  201.6 2.9 multiply_convert_fusion.6
  204.5 4.3 copy.89
  208.8 4.7 fusion.157
  213.6 4.9 fusion.66
  218.7 6.3 fusion.140
  227.9 4.5 add_convert_fusion.4
  233.7 8.0 constant_dynamic-update-slice_fusion.3
  249.6 15.1 %add_bitcast_fusion = f32[1,4,256,1024]{3,2,1,0:T(8,128)} fusion(f32[4,256,1024]{2,1,0:T(8,128)S(1)} %copy-done.3, bf16[4,256,4096]{2,1,0:T(8,128)(2,1)} %get-tuple-element.74, bf16[1,4096,1024]{2,1,0:T(8,128)(2,1)} %param.17), kind=kOutput, calls=%fused_computation.131 | convolution fusion | flops 8590983168 | bytes 25165824 | tf_op jit(solution)/shard_map/glf,fd->gld/dot_general | solution.py:274
  264.7 3.2 broadcast_select_fusion
  267.9 24.6 %add_convert_fusion = bf16[4,256,4096]{2,1,0:T(8,128)(2,1)} fusion(f32[4,256,4096]{2,1,0:T(8,128)} %get-tuple-element.75, bf16[4,256,1024]{2,1,0:T(8,128)(2,1)} %broadcast_select_fusion, bf16[1,4096,1024]{2,1,0:T(8,128)(2,1)} %param.17), kind=kOutput, calls=%fused_computation.18 | convolution fusion | flops 8673820672 | bytes 35651584 | tf_op jit(solution)/shard_map/gld,fd->glf/dot_general | solution.py:274
  292.5 15.9 %multiply_reduce_fusion.3 = (bf16[1024]{0:T(1024)(128)(2,1)S(1)}, f32[4,256]{1,0:T(4,128)S(1)}, bf16[1024]{0:T(1024)(128)(2,1)S(1)}, f32[4,256,1024]{2,1,0:T(8,128)S(1)}) fusion(f32[4,256,1024]{2,1,0:T(8,128)} %copy-done.2, f32[4,256]{1,0:T(4,128)S(1)} %fusion.174, f32[4,256]{1,0:T(4,128)S(1)} %broadcast_multiply_fusion, f32[1024]{0:T(1024)S(1)} %bitcast.290, ...), kind=kOutput, calls=%fused_computation.117 | convolution fusion | flops 8598320128 | bytes 25186304 | tf_op jit(solution)/shard_map/glf,df->gld/dot_general | solution.py:274
  313.3 3.7 fusion.141
  317.0 3.9 copy.117
  320.9 7.0 convolution_convert_fusion.2
  327.9 4.4 multiply_reduce_fusion
  336.4 2.9 multiply_convert_fusion.4
  339.3 4.3 copy.92
  343.6 4.3 copy.90
  347.9 4.5 copy.91
  352.4 4.7 fusion.156
  357.2 5.0 fusion.67
  362.3 7.7 fusion.195
  372.9 8.1 multiply_reduce_fusion.2
  381.1 3.2 constant_dynamic-update-slice_fusion.6
  385.4 7.9 constant_dynamic-update-slice_fusion.5
  401.4 395.7 %shard_map.160 = bf16[50,256,1024]{2,1,0:T(8,128)(2,1)} custom-call(bf16[1024,8192]{1,0:T(8,128)(2,1)} %constant_dynamic-update-slice_fusion.left_ref, bf16[1024,9216]{1,0:T(8,128)(2,1)} %bitcast_dynamic-update-slice_fusion.right_ref, bf16[2,256,1024]{2,1,0:T(8,128)(2,1)} %pad_maximum_fusion.extra_ref), custom_call_target="tpu_custom_call" | custom-call | flops 25769803776 | bytes 104857600 | tf_op jit(solution)/shard_map/pallas_call | solution.py:247
  800.0 11.7 %fusion.198 = (bf16[16,256,1024]{2,1,0:T(8,128)(2,1)}, bf16[16,256,1024]{2,1,0:T(8,128)(2,1)}) fusion(bf16[50,256,1024]{2,1,0:T(8,128)(2,1)} %shard_map.160), kind=kLoop, calls=%fused_computation.289 | loop fusion | bytes 33554432 | tf_op jit(solution)/shard_map/slice | solution.py:441
  812.3 41.0 %psum.7 = f32[]{:T(128)} all-reduce(f32[]{:T(128)} %fusion.193), channel_id=1, replica_groups=mesh['section'=2,'dp'=16] {'dp'}, use_global_device_ids=true, to_apply=%region_39.40 | all-reduce | flops 1 | bytes 8 | tf_op jit(solution)/shard_map/psum | solution.py:425
  854.5 6.0 fusion.194
  861.1 2.6 bitcast_convert_fusion.2
  864.8 6.3 bitcast_convert_fusion.1
  871.1 12.6 %copy.93 = f32[3,1024,1024]{1,2,0:T(8,128)} copy(f32[3,1024,1024]{2,1,0:T(8,128)} %bitcast_convert_fusion.1) | data formatting | bytes 25165824 | tf_op jit(solution)/shard_map/convert_element_type | solution.py:433
  883.7 12.6 %copy.95 = f32[1,1024,3072]{2,1,0:T(8,128)} copy(f32[1,1024,3072]{1,2,0:T(8,128)} %bitcast.236) | data formatting | bytes 25165824
  896.3 11.7 %convert_bitcast_fusion = f32[1024,4,1024]{2,0,1:T(8,128)} fusion(bf16[4,1024,1024]{2,1,0:T(8,128)(2,1)} %bitcast.243), kind=kLoop, calls=%fused_computation.17 | loop fusion | flops 4194304 | bytes 25165824 | tf_op jit(solution)/shard_map/convert_element_type | solution.py:433
  908.0 20.9 %copy.94 = f32[1024,4,1024]{2,1,0:T(4,128)} copy(f32[1024,4,1024]{2,0,1:T(8,128)} %convert_bitcast_fusion) | data formatting | bytes 33554432 | tf_op jit(solution)/shard_map/convert_element_type | solution.py:433
  928.9 20.5 %reshape.396 = f32[1,1024,4096]{2,1,0:T(8,128)} reshape(f32[1024,4,1024]{2,1,0:T(4,128)} %copy.94) | data formatting | bytes 33554432 | tf_op jit(solution)/shard_map/convert_element_type | solution.py:433
  949.4 11.7 %bitcast_convert_fusion = f32[1,4096,1024]{2,1,0:T(8,128)} fusion(bf16[1,4096,1024]{2,1,0:T(8,128)(2,1)} %bitcast.242), kind=kLoop, calls=%fused_computation.23 | loop fusion | flops 4194304 | bytes 25165824 | tf_op jit(solution)/shard_map/convert_element_type | solution.py:441
  (230 shorter events, 61.2 us)
Async XLA Ops:
  0.6 5.1 copy-start.7
  2.2 70.3 %copy-start.45 = (f32[1,1,1024]{2,0,1:T(1,128)}, f32[1,1,1024]{2,0,1:T(1,128)S(1)}, u32[]{:S(2)}) copy-start(f32[1,1,1024]{2,0,1:T(1,128)S(1)} %get-tuple-element.62) | copy-start | bytes 12292
  2.2 70.3 %copy-start.62 = (f32[1,1,1024]{2,0,1:T(1,128)}, f32[1,1,1024]{2,0,1:T(1,128)S(1)}, u32[]{:S(2)}) copy-start(f32[1,1,1024]{2,0,1:T(1,128)S(1)} %get-tuple-element.64) | copy-start | bytes 12292
  3.4 4.7 copy-start.65
  19.9 4.4 copy-start.33
  25.6 3.1 copy-start.36
  29.6 4.4 slice-start.6
  30.3 3.6 slice-start.7
  46.2 22.9 %copy-start.8 = (bf16[4,256,1024]{2,1,0:T(8,128)(2,1)S(1)}, bf16[4,256,1024]{2,1,0:T(8,128)(2,1)}, u32[]{:S(2)}) copy-start(bf16[4,256,1024]{2,1,0:T(8,128)(2,1)} %param.9) | copy-start | bytes 6291460
  63.0 6.1 collective-permute-start
  70.2 302.2 %copy-start = (bf16[4,256,1024]{2,1,0:T(8,128)(2,1)}, bf16[4,256,1024]{2,1,0:T(8,128)(2,1)S(1)}, u32[]{:S(2)}) copy-start(bf16[4,256,1024]{2,1,0:T(8,128)(2,1)S(1)} %get-tuple-element.51) | copy-start | bytes 6291460
  70.2 5.2 copy-start.43
  71.8 3.7 copy-start.54
  71.8 3.7 copy-start.50
  71.8 3.6 copy-start.47
  72.5 9.5 copy-start.57
  72.6 2.9 copy-start.52
  109.0 5.2 copy-start.67
  117.6 53.9 %copy-start.60 = (f32[4,256]{1,0:T(4,128)}, f32[4,256]{1,0:T(4,128)S(1)}, u32[]{:S(2)}) copy-start(f32[4,256]{1,0:T(4,128)S(1)} %multiply_reduce_fusion.6) | copy-start | bytes 12292
  119.8 19.9 %copy-start.18 = (bf16[4,256,1024]{2,1,0:T(8,128)(2,1)}, bf16[4,256,1024]{2,1,0:T(8,128)(2,1)S(1)}, u32[]{:S(2)}) copy-start(bf16[4,256,1024]{2,1,0:T(8,128)(2,1)S(1)} %add_convert_fusion.5) | copy-start | bytes 6291460
  171.5 6.4 copy-start.30
  171.5 6.3 copy-start.68
  185.5 7.0 copy-start.38
  185.5 7.0 copy-start.40
  185.5 11.5 %slice-start = ((s8[8388608]{0:T(1024)(128)(4,1)}), s8[4194304]{0:T(1024)(128)(4,1)S(1)}, s32[]{:S(2)}) async-start(s8[8388608]{0:T(1024)(128)(4,1)} %bitcast.238), calls=%async_computation | async-start | bytes 8388608
  192.6 4.6 slice-start.1
  208.8 4.8 copy-start.51
  208.8 4.8 copy-start.63
  208.8 4.8 copy-start.70
  213.6 5.0 copy-start.58
  213.6 5.0 copy-start.42
  213.6 5.0 copy-start.44
  213.6 5.0 copy-start.46
  213.6 5.0 copy-start.53
  218.6 6.4 copy-start.55
  218.7 6.4 copy-start.48
  225.0 2.9 copy-start.31
  232.4 32.3 %collective-permute-start.1 = (bf16[4,256,1024]{2,1,0:T(8,128)(2,1)}, bf16[4,256,1024]{2,1,0:T(8,128)(2,1)}, u32[]{:S(2)}, u32[]{:S(2)}) collective-permute-start(bf16[4,256,1024]{2,1,0:T(8,128)(2,1)} %add_convert_fusion.4), channel_id=1, source_target_pairs={{16,0},{17,1},{18,2},{19,3},{20,4},{21,5},{22,6},{23,7},{24,8},{25... | collective-permute-start | bytes 6291464 | tf_op jit(solution)/shard_map/ppermute | solution.py:414
  233.6 8.1 copy-start.19
  241.7 4.2 copy-start.26
  244.0 3.3 copy-start.24
  245.9 3.7 copy-start.3
  249.6 15.1 %copy-start.32 = (bf16[4,256,1024]{2,1,0:T(8,128)(2,1)S(1)}, bf16[4,256,1024]{2,1,0:T(8,128)(2,1)}, u32[]{:S(2)}) copy-start(bf16[4,256,1024]{2,1,0:T(8,128)(2,1)} %param.11) | copy-start | bytes 6291460
  292.5 15.9 %copy-start.61 = (f32[4,256]{1,0:T(4,128)S(1)}, f32[4,256]{1,0:T(4,128)}, u32[]{:S(2)}) copy-start(f32[4,256]{1,0:T(4,128)} %copy-done.60) | copy-start | bytes 12292
  292.5 15.9 %copy-start.4 = (f32[4,256,1024]{2,1,0:T(8,128)S(1)}, f32[4,256,1024]{2,1,0:T(8,128)}, u32[]{:S(2)}) copy-start(f32[4,256,1024]{2,1,0:T(8,128)} %copy-done.2) | copy-start | bytes 12582916
  310.1 3.2 copy-start.69
  320.9 7.0 copy-start.37
  320.9 7.0 copy-start.41
  320.9 11.4 %slice-start.2 = ((s8[8388608]{0:T(1024)(128)(4,1)}), s8[4194304]{0:T(1024)(128)(4,1)S(1)}, s32[]{:S(2)}) async-start(s8[8388608]{0:T(1024)(128)(4,1)} %bitcast.240), calls=%async_computation.2 | async-start | bytes 8388608
  327.9 4.6 slice-start.3
  352.4 4.8 copy-start.35
  352.4 4.8 copy-start.64
  357.2 5.1 copy-start.59
  357.2 5.1 copy-start.29
  362.2 10.1 %copy-start.15 = (f32[4,256,1024]{2,1,0:T(8,128)}, f32[4,256,1024]{2,1,0:T(8,128)S(1)}, u32[]{:S(2)}) copy-start(f32[4,256,1024]{2,1,0:T(8,128)S(1)} %get-tuple-element.87) | copy-start | bytes 12582916
  362.3 7.7 copy-start.56
  362.3 7.8 copy-start.49
  381.0 3.3 copy-start.39
  385.4 7.9 copy-start.28
  393.3 4.3 copy-start.21
  395.6 3.8 copy-start.20
  812.3 42.2 %copy-start.1 = (bf16[4,256,1024]{2,1,0:T(8,128)(2,1)S(1)}, bf16[4,256,1024]{2,1,0:T(8,128)(2,1)}, u32[]{:S(2)}) copy-start(bf16[4,256,1024]{2,1,0:T(8,128)(2,1)} %copy-done) | copy-start | bytes 6291460
  854.5 6.7 slice-start.4
  860.5 4.3 slice-start.5
  (17 other events, 35.2 us)

commit v2 on v1

--- a/solution.py
+++ b/solution.py
@@ -1,4 +1,5 @@
 import functools
+
 import jax
 import jax.numpy as jnp
 from jax import lax
@@ -6,7 +7,6 @@
 from jax.experimental.pallas import tpu as pltpu
 from jax.sharding import PartitionSpec as P
 
-HEADS = 8
 MESH = pl.DeviceIdType.MESH
 TILE = 256
 RING = 8
@@ -264,173 +264,431 @@
     )(lefts, rights, extras)
 
 
-def layer_norm(values, gain_row, shift_row):
+HEADS = 8
+CHUNK = 512
+LOW = jnp.bfloat16
+WIDE = jnp.float32
+NN = (((1,), (0,)), ((), ()))
+NT = (((1,), (1,)), ((), ()))
+TN = (((0,), (0,)), ((), ()))
+
+
+def dot(a, b, form):
+    return lax.dot_general(a, b, form, preferred_element_type=WIDE)
+
+
+def normalize(values):
     center = values - jnp.mean(values, -1, keepdims=True)
-    spread = jnp.mean(center * center, -1, keepdims=True)
-    return center * lax.rsqrt(spread + 1e-05) * gain_row + shift_row
-
-
-def matmul(left, right, form):
-    return jnp.einsum(form, left, right, preferred_element_type=jnp.float32)
-
-
-def advance(base_in, source, visible, w_qkv, w_out, w_up, w_down, params):
-    query_in, query_back = jax.vjp(layer_norm, base_in, params[0], params[1])
-    key_in, key_back = jax.vjp(layer_norm, source, params[2], params[3])
-    query_low = query_in.astype(jnp.bfloat16)
-    key_low = key_in.astype(jnp.bfloat16)
-    features = query_low.shape[-1]
-    queries = matmul(query_low, w_qkv[:, :features], "gld,de->gle").astype(jnp.bfloat16)
-    key_vals = matmul(key_low, w_qkv[:, features:], "gld,de->gle").astype(jnp.bfloat16)
-    groups, positions = (queries.shape[0], queries.shape[1])
-    head_shape = (groups, positions, HEADS, features // HEADS)
-    head_scale = (features // HEADS) ** (-0.5)
-    heads_q = queries.reshape(head_shape)
-    heads_k = key_vals[..., :features].reshape(head_shape)
-    heads_v = key_vals[..., features:].reshape(head_shape)
-    scores = matmul(heads_q, heads_k, "gqhd,gkhd->ghqk") * head_scale
-    scores = jnp.where(visible[:, None, None, :], scores, -1e30)
-    row_max = jnp.max(scores, -1, keepdims=True)
-    exponent = jnp.exp(scores - row_max)
-    weights_soft = exponent / jnp.sum(exponent, -1, keepdims=True)
-    weights_low = weights_soft.astype(jnp.bfloat16)
-    mixed_out = (
-        matmul(weights_low, heads_v, "ghqk,gkhd->gqhd")
-        .reshape(groups, positions, features)
-        .astype(jnp.bfloat16)
-    )
-    hidden = base_in + matmul(mixed_out, w_out, "gld,de->gle")
-    normed, normed_back = jax.vjp(layer_norm, hidden, params[4], params[5])
-    normed_low = normed.astype(jnp.bfloat16)
-    upward = matmul(normed_low, w_up, "gld,df->glf")
-    active, active_back = jax.vjp(jax.nn.gelu, upward)
-    active_low = active.astype(jnp.bfloat16)
-    outcome = hidden + matmul(active_low, w_down, "glf,fd->gld")
-    stored_parts = (
-        query_back,
-        key_back,
-        query_low,
-        key_low,
-        heads_q,
-        heads_k,
-        heads_v,
-        weights_soft,
-        weights_low,
-        mixed_out,
-        normed_back,
-        normed_low,
-        active_back,
-        active_low,
-    )
-    return (outcome, stored_parts)
-
-
-def retreat(stored_parts, w_qkv, w_out, w_up, w_down, grad_outcome):
-    (
-        query_back,
-        key_back,
-        query_low,
-        key_low,
-        heads_q,
-        heads_k,
-        heads_v,
-        weights_soft,
-        weights_low,
-        mixed_out,
-        normed_back,
-        normed_low,
-        active_back,
-        active_low,
-    ) = stored_parts
-    features = query_low.shape[-1]
-    groups, positions = (query_low.shape[0], query_low.shape[1])
-    head_scale = (features // HEADS) ** (-0.5)
-    outcome_low = grad_outcome.astype(jnp.bfloat16)
-    grad_active = matmul(outcome_low, w_down, "gld,fd->glf")
-    (grad_upward,) = active_back(grad_active)
-    upward_low = grad_upward.astype(jnp.bfloat16)
-    grad_normed = matmul(upward_low, w_up, "glf,df->gld")
-    grad_from_norm, grad_gain_mlp, grad_shift_mlp = normed_back(grad_normed)
-    grad_hidden = grad_outcome + grad_from_norm
-    hidden_low = grad_hidden.astype(jnp.bfloat16)
-    grad_mixed = (
-        matmul(hidden_low, w_out, "gle,de->gld").astype(jnp.bfloat16).reshape(heads_q.shape)
-    )
-    grad_weights = matmul(grad_mixed, heads_v, "gqhd,gkhd->ghqk")
-    grad_values = matmul(weights_low, grad_mixed, "ghqk,gqhd->gkhd").astype(jnp.bfloat16)
-    grad_scores = weights_soft * (
-        grad_weights - jnp.sum(grad_weights * weights_soft, -1, keepdims=True)
-    )
-    scores_low = grad_scores.astype(jnp.bfloat16)
-    grad_queries = (matmul(scores_low, heads_k, "ghqk,gkhd->gqhd") * head_scale).astype(
-        jnp.bfloat16
-    )
-    grad_keys = (matmul(scores_low, heads_q, "ghqk,gqhd->gkhd") * head_scale).astype(jnp.bfloat16)
-    grad_queries = grad_queries.reshape(groups, positions, features)
-    grad_keys = grad_keys.reshape(groups, positions, features)
-    grad_values = grad_values.reshape(groups, positions, features)
-    grad_query_in = matmul(grad_queries, w_qkv[:, :features], "gle,de->gld")
-    grad_key_in = matmul(grad_keys, w_qkv[:, features : 2 * features], "gle,de->gld") + matmul(
-        grad_values, w_qkv[:, 2 * features :], "gle,de->gld"
-    )
-    grad_base_norm, grad_gain_q, grad_shift_q = query_back(grad_query_in)
-    grad_source, grad_gain_k, grad_shift_k = key_back(grad_key_in)
-    grad_base = grad_hidden + grad_base_norm
-    grad_params = jnp.stack(
-        [grad_gain_q, grad_shift_q, grad_gain_k, grad_shift_k, grad_gain_mlp, grad_shift_mlp]
-    )
-    rights = (outcome_low, upward_low, hidden_low, grad_queries, grad_keys, grad_values)
-    return rights, grad_params, grad_base, grad_source
+    inverse = lax.rsqrt(jnp.mean(center * center, -1, keepdims=True) + 1e-05)
+    return center * inverse, inverse
+
+
+def norm_back(upstream, gain, xhat, inverse):
+    scaled = upstream * gain
+    return inverse * (scaled - jnp.mean(scaled, -1, keepdims=True)
+                      - xhat * jnp.mean(scaled * xhat, -1, keepdims=True))
+
+
+def gelu_pair(u):
+    c = 0.7978845608028654
+    square = u * u
+    t = jnp.tanh(u * (c + (c * 0.044715) * square))
+    half = 0.5 * (1.0 + t)
+    slope = half + (0.5 * u) * (1.0 - t * t) * (c + (3.0 * c * 0.044715) * square)
+    return u * half, slope
+
+
+def layers_kernel(groups, tokens, cotangent, mask, embed, params, w_qkv, w_out, w_up, w_down,
+                  lefts, rights, sec_out, sec_grad, g_params, g_embed, squares,
+                  qkv_w, out_w, up_w, down_w, emb, src, upstream, qkv, probs, slopes, xhat_f, stats,
+                  active, keep, passed, acc, hid, wide, u_buf,
+                  w_sem, in_sem, left_sem, right_sem, wide_sem, send_sem, recv_sem):
+    section = lax.axis_index("section")
+    first = section == 0
+    other = 1 - section
+    slots, width = emb.shape
+    units = up_w.shape[1]
+    steps = units // CHUNK
+    head = width // HEADS
+    scale = head ** -0.5
+
+    loads = [pltpu.make_async_copy(a, b, w_sem.at[k]) for k, (a, b) in enumerate(
+        ((w_qkv, qkv_w), (w_out, out_w), (w_up, up_w), (w_down, down_w), (embed, emb)))]
+    loads[4].start()
+    loads[0].start()
+
+    def token_load(g):
+        return pltpu.make_async_copy(tokens.at[g], src.at[g], in_sem.at[g])
+
+    def cot_load(g):
+        return pltpu.make_async_copy(cotangent.at[g], upstream.at[g], in_sem.at[groups + g])
+
+    @pl.when(first)
+    def _():
+        for g in range(groups):
+            token_load(g).start()
+    for k in (1, 2, 3):
+        loads[k].start()
+
+    @pl.when(section == 1)
+    def _():
+        for g in range(groups):
+            cot_load(g).start()
+
+    barrier = pltpu.get_barrier_semaphore()
+    pl.semaphore_signal(barrier, inc=1, device_id={"section": other}, device_id_type=MESH)
+    pl.semaphore_wait(barrier, 1)
+
+    def relay(g):
+        return pltpu.make_async_remote_copy(
+            src_ref=passed, dst_ref=src.at[g], send_sem=send_sem.at[g], recv_sem=recv_sem.at[g],
+            device_id={"section": other}, device_id_type=MESH)
+
+    def relay_back(g):
+        return pltpu.make_async_remote_copy(
+            src_ref=passed, dst_ref=upstream.at[g], send_sem=send_sem.at[groups + g],
+            recv_sem=recv_sem.at[groups + g], device_id={"section": other}, device_id_type=MESH)
+
+    def rows_of(g):
+        return pl.ds(pl.multiple_of(g * slots, slots), slots)
+
+    def cols(i, w=CHUNK):
+        return pl.ds(pl.multiple_of(i * w, w), w)
+
+    def left_store(g, k):
+        if k == 0:
+            return pltpu.make_async_copy(active, lefts.at[rows_of(g), pl.ds(0, units)], left_sem.at[0])
+        return pltpu.make_async_copy(
+            keep.at[:, pl.ds((k - 1) * width, width)], lefts.at[rows_of(g), pl.ds(units + (k - 1) * width, width)], left_sem.at[k])
+
+    def right_store(g, k):
+        if k == 0:
+            return pltpu.make_async_copy(upstream.at[g], rights.at[rows_of(g), pl.ds(0, width)], right_sem.at[0])
+        if k == 1:
+            return pltpu.make_async_copy(active, rights.at[rows_of(g), pl.ds(width, units)], right_sem.at[1])
+        return pltpu.make_async_copy(
+            keep.at[:, pl.ds((k - 2) * width, width)],
+            rights.at[rows_of(g), pl.ds(width + units + (k - 2) * width, width)], right_sem.at[k])
+
+    def out_store(g):
+        return pltpu.make_async_copy(wide, sec_out.at[g], wide_sem.at[0])
+
+    def grad_store(g):
+        return pltpu.make_async_copy(wide, sec_grad.at[g], wide_sem.at[1])
+
+    def base_of(g):
+        return jnp.where(first, 0.0, src[g].astype(WIDE)) + emb[...].astype(WIDE)
+
+    def forward(g, _):
+        @pl.when(first)
+        def _():
+            token_load(g).wait()
+        @pl.when(section == 1)
+        def _():
+            relay(g).wait_recv()
+        @pl.when(g == 0)
+        def _():
+            loads[4].wait()
+
+        @pl.when(g > 0)
+        def _():
+            for k in (3, 4):
+                left_store(g - 1, k).wait()
+        source = src[g].astype(WIDE)
+        xhat, inverse = normalize(source)
+        stats[g, :, 0:1] = inverse
+        stats[g, :, 3:4] = jnp.mean(source, -1, keepdims=True)
+        keep[:, 3 * width:4 * width] = (xhat * params[2:3] + params[3:4]).astype(LOW)
+        base = base_of(g)
+        xhat, inverse = normalize(base)
+        stats[g, :, 1:2] = inverse
+        stats[g, :, 4:5] = jnp.mean(base, -1, keepdims=True)
+        keep[:, 2 * width:3 * width] = (xhat * params[0:1] + params[1:2]).astype(LOW)
+        left_store(g, 3).start()
+        left_store(g, 4).start()
+
+        @pl.when(g == 0)
+        def _():
+            loads[0].wait()
+
+        def project(k, a):
+            def step(i, _):
+                qkv[g, :, cols(i)] = dot(a[...], qkv_w[:, cols(i)], NN).astype(LOW)
+                return 0
+            lax.fori_loop(*k, step, 0)
+        per = width // CHUNK
+        project((0, per), keep.at[:, 2 * width:3 * width])
+        project((per, 3 * per), keep.at[:, 3 * width:4 * width])
+
+        @pl.when(g > 0)
+        def _():
+            for k in (0, 1, 2):
+                left_store(g - 1, k).wait()
+        seen = mask[g, 0:1, :] > 0
+        for h in range(HEADS):
+            q = qkv[g, :, h * head:(h + 1) * head]
+            k = qkv[g, :, width + h * head:width + (h + 1) * head]
+            v = qkv[g, :, 2 * width + h * head:2 * width + (h + 1) * head]
+            s = jnp.where(seen, dot(q, k, NT) * scale, -1e30)
+            e = jnp.exp(s - jnp.max(s, -1, keepdims=True))
+            p = (e / jnp.sum(e, -1, keepdims=True)).astype(LOW)
+            probs[g, h] = p
+            keep[:, width + h * head:width + (h + 1) * head] = dot(p, v, NN).astype(LOW)
+        left_store(g, 2).start()
+
+        @pl.when(g == 0)
+        def _():
+            loads[1].wait()
+
+        def mix(i, _):
+            hid[:, cols(i)] = dot(keep[:, width:2 * width], out_w[:, cols(i)], NN)
+            return 0
+        lax.fori_loop(0, width // CHUNK, mix, 0)
+        hidden = base_of(g) + hid[...]
+        hid[...] = hidden
+        xhat, inverse = normalize(hidden)
+        stats[g, :, 2:3] = inverse
+        xhat_f[g] = xhat.astype(LOW)
+        keep[:, 0:width] = (xhat * params[4:5] + params[5:6]).astype(LOW)
+        left_store(g, 1).start()
+
+        @pl.when(g == 0)
+        def _():
+            loads[2].wait()
+            loads[3].wait()
+
+        acc[...] = hid[...]
+        u_buf[0] = dot(keep[:, 0:width], up_w[:, cols(0)], NN)
+
+        def feed(i, _):
+            ahead = jnp.minimum(i + 1, steps - 1)
+            u_buf[lax.rem(i + 1, 2)] = dot(keep[:, 0:width], up_w[:, cols(ahead)], NN)
+            value, slope = gelu_pair(u_buf[lax.rem(i, 2)])
+            slopes[g, :, cols(i)] = slope.astype(LOW)
+            value = value.astype(LOW)
+            active[:, cols(i)] = value
+            acc[...] += dot(value, down_w[cols(i), :], NN)
+            return 0
+        lax.fori_loop(0, steps, feed, 0)
+        left_store(g, 0).start()
+
+        @pl.when(g > 0)
+        def _():
+            out_store(g - 1).wait()
+        wide[...] = acc[...]
+        out_store(g).start()
+
+        @pl.when(first)
+        def _():
+            @pl.when(g > 0)
+            def _():
+                relay(g - 1).wait_send()
+            passed[...] = acc[...].astype(LOW)
+            relay(g).start()
+        return 0
+
+    lax.fori_loop(0, groups, forward, 0)
+    for k in range(5):
+        left_store(groups - 1, k).wait()
+    out_store(groups - 1).wait()
+
+    @pl.when(first)
+    def _():
+        relay(groups - 1).wait_send()
+
+    g_params[...] = jnp.zeros_like(g_params)
+    g_embed[...] = jnp.zeros_like(g_embed)
+    squares[...] = jnp.zeros_like(squares)
+
+    def gains(row, e, xhat):
+        g_params[row:row + 1] += jnp.sum(e * xhat, axis=0, keepdims=True)
+        g_params[row + 1:row + 2] += jnp.sum(e, axis=0, keepdims=True)
+
+    def backward(g, _):
+        @pl.when(first)
+        def _():
+            relay_back(g).wait_recv()
+        @pl.when(section == 1)
+        def _():
+            cot_load(g).wait()
+        @pl.when(g > 0)
+        def _():
+            for k in (0, 1):
+                right_store(g - 1, k).wait()
+        right_store(g, 0).start()
+
+        acc[...] = jnp.zeros_like(acc)
+        u_buf[0] = dot(upstream[g], down_w[cols(0), :], NT)
+
+        def feed(i, _):
+            ahead = jnp.minimum(i + 1, steps - 1)
+            u_buf[lax.rem(i + 1, 2)] = dot(upstream[g], down_w[cols(ahead), :], NT)
+            value = (u_buf[lax.rem(i, 2)] * slopes[g, :, cols(i)].astype(WIDE)).astype(LOW)
+            active[:, cols(i)] = value
+            acc[...] += dot(value, up_w[:, cols(i)], NT)
+            return 0
+        lax.fori_loop(0, steps, feed, 0)
+        right_store(g, 1).start()
+
+        e = acc[...]
+        xhat = xhat_f[g].astype(WIDE)
+        gains(4, e, xhat)
+        grad_hidden = upstream[g].astype(WIDE) + norm_back(e, params[4:5], xhat, stats[g, :, 2:3])
+        hid[...] = grad_hidden
+
+        @pl.when(g > 0)
+        def _():
+            for k in (2, 3, 4, 5):
+                right_store(g - 1, k).wait()
+        keep[:, 0:width] = grad_hidden.astype(LOW)
+        right_store(g, 2).start()
+
+        def mixed_back(i, _):
+            xhat_f[g, :, cols(i)] = dot(keep[:, 0:width], out_w[cols(i), :], NT).astype(LOW)
+            return 0
+        lax.fori_loop(0, width // CHUNK, mixed_back, 0)
+
+        for h in range(HEADS):
+            q = qkv[g, :, h * head:(h + 1) * head]
+            k = qkv[g, :, width + h * head:width + (h + 1) * head]
+            v = qkv[g, :, 2 * width + h * head:2 * width + (h + 1) * head]
+            m = xhat_f[g, :, h * head:(h + 1) * head]
+            low = probs[g, h]
+            p = low.astype(WIDE)
+            gp = dot(m, v, NT)
+            ds = (p * (gp - jnp.sum(gp * p, -1, keepdims=True))).astype(LOW)
+            keep[:, width + h * head:width + (h + 1) * head] = (dot(ds, k, NN) * scale).astype(LOW)
+            keep[:, 2 * width + h * head:2 * width + (h + 1) * head] = (dot(ds, q, TN) * scale).astype(LOW)
+            keep[:, 3 * width + h * head:3 * width + (h + 1) * head] = dot(low, m, TN).astype(LOW)
+        for k in (3, 4, 5):
+            right_store(g, k).start()
+
+        def query_back(i, _):
+            acc[:, cols(i)] = dot(keep[:, width:2 * width], qkv_w[cols(i), 0:width], NT)
+            return 0
+        lax.fori_loop(0, width // CHUNK, query_back, 0)
+        e = acc[...]
+        xhat = (base_of(g) - stats[g, :, 4:5]) * stats[g, :, 1:2]
+        gains(0, e, xhat)
+        grad_base = hid[...] + norm_back(e, params[0:1], xhat, stats[g, :, 1:2])
+        g_embed[...] += grad_base
+        hid[...] = grad_base
+
+        def key_back(i, _):
+            acc[:, cols(i)] = dot(keep[:, 2 * width:4 * width], qkv_w[cols(i), width:3 * width], NT)
+            return 0
+        lax.fori_loop(0, width // CHUNK, key_back, 0)
+        e = acc[...]
+        xhat = (src[g].astype(WIDE) - stats[g, :, 3:4]) * stats[g, :, 0:1]
+        gains(2, e, xhat)
+        grad_source = norm_back(e, params[2:3], xhat, stats[g, :, 0:1])
+
+        @pl.when(g > 0)
+        def _():
+            grad_store(g - 1).wait()
+        wide[...] = grad_source
+
+        @pl.when(section == 1)
+        def _():
+            @pl.when(g > 0)
+            def _():
+                relay_back(g - 1).wait_send()
+            low = (wide[...] + hid[...]).astype(LOW)
+            passed[...] = low
+            relay_back(g).start()
+            wide[...] = low.astype(WIDE)
+        grad_store(g).start()
+        total = wide[...]
+        squares[pl.ds(g, 1), :] = jnp.broadcast_to(
+            jnp.sum(jnp.sum(total * total, axis=0, keepdims=True), axis=1, keepdims=True), (1, squares.shape[1]))
+        return 0
+
+    lax.fori_loop(0, groups, backward, 0)
+    for k in range(6):
+        right_store(groups - 1, k).wait()
+    grad_store(groups - 1).wait()
+
+    @pl.when(section == 1)
+    def _():
+        relay_back(groups - 1).wait_send()
+
+
+def layers(tokens, cotangent, mask, embed, params, w_qkv, w_out, w_up, w_down, cid):
+    groups, slots, width = tokens.shape
+    units = w_up.shape[1]
+    rows = groups * slots
+    hbm = pl.BlockSpec(memory_space=pl.ANY)
+    vmem = pl.BlockSpec(memory_space=pltpu.VMEM)
+    shape = jax.ShapeDtypeStruct
+    return pl.pallas_call(
+        functools.partial(layers_kernel, groups),
+        out_shape=(
+            shape((rows, units + 4 * width), LOW),
+            shape((rows, units + 5 * width), LOW),
+            shape((groups, slots, width), WIDE),
+            shape((groups, slots, width), WIDE),
+            shape((8, width), WIDE),
+            shape((slots, width), WIDE),
+            shape((groups, 128), WIDE),
+        ),
+        in_specs=[hbm, hbm, vmem, hbm, vmem, hbm, hbm, hbm, hbm],
+        out_specs=(hbm, hbm, hbm, hbm, vmem, vmem, vmem),
+        scratch_shapes=[
+            pltpu.VMEM(w_qkv.shape, LOW),
+            pltpu.VMEM(w_out.shape, LOW),
+            pltpu.VMEM(w_up.shape, LOW),
+            pltpu.VMEM(w_down.shape, LOW),
+            pltpu.VMEM((slots, width), LOW),
+            pltpu.VMEM((groups, slots, width), LOW),
+            pltpu.VMEM((groups, slots, width), LOW),
+            pltpu.VMEM((groups, slots, 3 * width), LOW),
+            pltpu.VMEM((groups, HEADS, slots, slots), LOW),
+            pltpu.VMEM((groups, slots, units), LOW),
+            pltpu.VMEM((groups, slots, width), LOW),
+            pltpu.VMEM((groups, slots, 128), WIDE),
+            pltpu.VMEM((slots, units), LOW),
+            pltpu.VMEM((slots, 4 * width), LOW),
+            pltpu.VMEM((slots, width), LOW),
+            pltpu.VMEM((slots, width), WIDE),
+            pltpu.VMEM((slots, width), WIDE),
+            pltpu.VMEM((slots, width), WIDE),
+            pltpu.VMEM((2, slots, CHUNK), WIDE),
+            pltpu.SemaphoreType.DMA((5,)),
+            pltpu.SemaphoreType.DMA((2 * groups,)),
+            pltpu.SemaphoreType.DMA((5,)),
+            pltpu.SemaphoreType.DMA((6,)),
+            pltpu.SemaphoreType.DMA((2,)),
+            pltpu.SemaphoreType.DMA((2 * groups,)),
+            pltpu.SemaphoreType.DMA((2 * groups,)),
+        ],
+        compiler_params=pltpu.CompilerParams(
+            collective_id=cid, has_side_effects=True, vmem_limit_bytes=63 * 2**20),
+        cost_estimate=pl.CostEstimate(flops=54 * 10**9, bytes_accessed=120 * 2**20, transcendentals=10**7),
+    )(tokens, cotangent, mask, embed, params, w_qkv, w_out, w_up, w_down)
 
 
 def body(tokens, clip_frames, cotangent, embed, norm_params, w_qkv, w_out, w_up, w_down):
     is_first = lax.axis_index("section") == 0
-    matrices = (w_qkv[0], w_out[0], w_up[0], w_down[0])
-    params = norm_params[0]
-    embed_row = embed[0].astype(jnp.float32)
-    groups, positions, features = tokens.shape
-    slot_ids = jnp.arange(positions, dtype=jnp.int32)
-    visible = (slot_ids[None, :] < clip_frames[:, None] * (positions // 16)) | jnp.logical_not(
-        is_first
+    groups, slots, width = tokens.shape
+    units = w_up.shape[-1]
+    slot_ids = jnp.arange(slots, dtype=jnp.int32)
+    visible = (slot_ids[None, :] < clip_frames[:, None] * (slots // 16)) | jnp.logical_not(is_first)
+    mask = jnp.broadcast_to(visible[:, None, :].astype(WIDE), (groups, 8, slots))
+    lefts, rights, outcome, grad_inputs, g_params, g_embed, squares = layers(
+        tokens, cotangent, mask, embed[0], norm_params[0], w_qkv[0], w_out[0], w_up[0], w_down[0], 2
     )
-
-    def forward(source):
-        source_wide = source.astype(jnp.float32)
-        base_in = jnp.where(is_first, 0.0, source_wide) + embed_row
-        return advance(base_in, source_wide, visible, *matrices, params)
-
-    early, _ = forward(tokens)
-    received = lax.ppermute(early.astype(jnp.bfloat16), "section", [(0, 1)])
-    outcome, stored = forward(jnp.where(is_first, tokens, received))
-
-    def backward(upstream):
-        rights, grad_params, grad_base, grad_source = retreat(
-            stored, *matrices, upstream.astype(jnp.float32)
-        )
-        sent = (grad_source + grad_base).astype(jnp.bfloat16)
-        return rights, grad_params, grad_base, grad_source, sent
-
-    sent_early = backward(cotangent)[-1]
-    arriving = lax.ppermute(sent_early, "section", [(1, 0)])
-    rights, grad_params, grad_base, grad_source, sent = backward(
-        jnp.where(is_first, arriving, cotangent)
-    )
-    grad_inputs = jnp.where(is_first, grad_source, sent.astype(jnp.float32))
-    rows = groups * positions
-    flat = lambda parts: jnp.concatenate([p.reshape(rows, -1) for p in parts], axis=1)
-    (_, _, query_low, key_low, _, _, _, _, _, mixed_low, _, normed_low, _, active_low) = stored
-    lefts = flat((active_low, normed_low, mixed_low, query_low, key_low))
-    rights = flat(rights)
-    magnitude = jnp.sqrt(jnp.mean(grad_inputs * grad_inputs, axis=(1, 2)) + 1e-06)
-    overall = lax.psum(jnp.sum(magnitude), "dp")
+    magnitude = jnp.sqrt(squares[:, 0] / (slots * width) + 1e-06)
+    factors = 1.0 + jnp.arange(width, dtype=WIDE) / width
+    row = (jnp.sum(magnitude) * factors)[None]
+    extras = jnp.stack(
+        [g_embed, jnp.concatenate([g_params[:6], row, jnp.zeros((TILE - 7, width), WIDE)])]
+    ).astype(LOW)
+    sums = weight_sums(lines_of(lax.axis_size("dp")), lefts, rights, extras, 1)
+    overall = jnp.sum(sums[49, 6].astype(WIDE)) / jnp.sum(factors)
     norms = magnitude / (overall / (groups * lax.axis_size("dp")))
-    extras = jnp.stack(
-        [jnp.sum(grad_base, axis=0), jnp.pad(grad_params, ((0, TILE - 6), (0, 0)))]
-    ).astype(jnp.bfloat16)
-    sums = weight_sums(lines_of(lax.axis_size("dp")), lefts, rights, extras, 1)
-    blocks = sums[:48].reshape(12, 1024, 1024)
+    blocks = sums[:48].reshape(12, width, width)
     beside = lambda first, last: (
-        blocks[first:last].transpose(1, 0, 2).reshape(1024, -1).astype(jnp.float32)
+        blocks[first:last].transpose(1, 0, 2).reshape(width, -1).astype(WIDE)
     )
     return (
         outcome[None],
@@ -438,9 +696,9 @@
         beside(9, 12)[None],
         beside(8, 9)[None],
         beside(4, 8)[None],
-        blocks[0:4].reshape(4096, 1024).astype(jnp.float32)[None],
-        sums[49, :6].astype(jnp.float32)[None],
-        sums[48].astype(jnp.float32)[None],
+        blocks[0:4].reshape(units, width).astype(WIDE)[None],
+        sums[49, :6].astype(WIDE)[None],
+        sums[48].astype(WIDE)[None],
         norms[None],
     )
 

time: 967 us -> 704 us (0.73)
  matrix products: 254 us -> 0 us
  Pallas kernels: 396 us -> 567 us
  local copies, waits for them, and re-layouts: 169 us -> 90.6 us
  other arithmetic: 91.5 us -> 42.9 us
  blocking collectives: 41 us -> 0 us
    dot_general x32 -> x0, matrix products: 245 us -> none  [matmul(): return jnp.einsum(form, left, right, preferred_element_type=jnp.float32)]
    pallas_call x0 -> x1, Pallas kernels: none -> 176 us  [layers(): pl.pallas_call(functools.partial(layers_kernel, groups), out_shape=(shape...]
    psum x1 -> x0, blocking collectives: 41 us -> none  [body(): overall = lax.psum(jnp.sum(magnitude), 'dp')]
    unnamed x166 -> x11, local copies, waits for them, and re-layouts: 57.9 us -> 20.3 us
    reduce_sum x14 -> x3, other arithmetic: 27.7 us -> 3.22 us  [the longest x2 1.94 us: body(): overall = jnp.sum(sums[49, 6].astype(WIDE)) / jnp.sum(factors)]
    reshape x5 -> x0, local copies, waits for them, and re-layouts: 19.9 us -> none  [the longest x2 7.88 us: retreat(): matmul(hidden_low, w_out, 'gle,de->gld').astype(jnp.bfloat16)]
    convert_element_type x7 -> x3, local copies, waits for them, and re-layouts: 71.4 us -> 54 us  [body(): blocks[first:last].transpose(1, 0, 2).reshape(width, -1).astype(WIDE)]
    convert_element_type x12 -> x7, other arithmetic: 47.8 us -> 35.3 us  [the longest x3 20.5 us: body(): blocks[first:last].transpose(1, 0, 2).reshape(width, -1).astype(WIDE)]
  transfers between devices with their start and end apart: 2 -> 0, of which waited for: 1 -> 0; matrix products, arithmetic and copies ran while one was open for 3% -> 0% of each run, Pallas kernels for 0% -> 0%
where the time goes in v2:
time: 704 us; the launch traced here: 702 us
  Pallas kernels  567 us (81%)
  local copies, waits for them, and re-layouts  90.6 us (13%)
  other arithmetic  42.9 us (6%)
    pallas_call x1, Pallas kernels, weight_sums(): pl.pallas_call(functools.partial(weights_kernel, dims, jobs, extra), out_...  390 us
    pallas_call x1, Pallas kernels, layers(): pl.pallas_call(functools.partial(layers_kernel, groups), out_shape=(shape...  176 us
    convert_element_type x3, local copies, waits for them, and re-layouts, body(): blocks[first:last].transpose(1, 0, 2).reshape(width, -1).astype(WIDE)  54 us
    convert_element_type x3, other arithmetic, body(): blocks[first:last].transpose(1, 0, 2).reshape(width, -1).astype(WIDE)  20.5 us
    unnamed x11, local copies, waits for them, and re-layouts  20.3 us

profile of v2, /device:TPU:0, one launch (start us, length us, event | category | flops | bytes accessed | tf_op | source)
XLA Modules:
  0.0 702.1 jit_solution(9121757070558164067)
XLA Ops:
  0.6 0.6 add_reduce_fusion
  1.3 0.7 broadcast_multiply_fusion
  1.9 0.1 pad.4.clone
  2.0 0.1 fusion.1
  2.1 0.6 broadcast_in_dim.8.mask
  2.7 1.4 copy.27
  4.0 176.5 %shard_map.160 = (bf16[1024,8192]{1,0:T(8,128)(2,1)}, bf16[1024,9216]{1,0:T(8,128)(2,1)}, f32[4,256,1024]{2,1,0:T(8,128)}, f32[4,256,1024]{2,1,0:T(8,128)}, f32[...) custom-call(bf16[4,256,1024]{2,1,0:T(8,128)(2,1)} %tokens.1, bf16[4,256,1024]{2,1,0:T(8,128)(2,1)} %cotangent.1, ...), custom_call_target="tpu_custom_call" | custom-call | flops 54000001024 | bytes 125829120 | tf_op jit(solution)/shard_map/pallas_call | solution.py:623
  180.5 1.3 fusion.2
  181.8 0.7 multiply_convert_fusion
  182.5 0.8 slice.56
  183.2 0.1 maximum_bitcast_fusion
  183.3 1.3 convert_bitcast_fusion.1
  184.6 1.1 pad_maximum_fusion.extra_ref
  185.7 0.0 copy-start.2
  185.7 390.1 %shard_map.161 = bf16[50,256,1024]{2,1,0:T(8,128)(2,1)} custom-call(bf16[1024,8192]{1,0:T(8,128)(2,1)} %get-tuple-element.18.left_ref, bf16[1024,9216]{1,0:T(8,128)(2,1)} %get-tuple-element.19.right_ref, bf16[2,256,1024]{2,1,0:T(8,128)(2,1)} %pad_maximum_fusion.extra_ref), custom_call_target="tpu_custom_call" | custom-call | flops 25769803776 | bytes 104857600 | tf_op jit(solution)/shard_map/pallas_call | solution.py:247
  575.8 1.3 convert_reduce_fusion
  578.5 0.0 copy-done.2
  578.5 0.6 divide_reduce_fusion
  579.1 0.7 slice_convert_fusion.2
  579.8 0.6 copy.24
  580.5 2.1 slice_convert_fusion
  582.6 1.8 slice.40
  584.4 2.5 bitcast_convert_fusion.2
  586.8 0.0 slice-start
  586.8 12.5 %fusion.3 = (bf16[16,256,1024]{2,1,0:T(8,128)(2,1)}, bf16[16,256,1024]{2,1,0:T(8,128)(2,1)}) fusion(bf16[50,256,1024]{2,1,0:T(8,128)(2,1)} %shard_map.161), kind=kLoop, calls=%fused_computation.21 | loop fusion | bytes 33554432 | tf_op jit(solution)/shard_map/slice | solution.py:699
  599.3 0.6 slice-done
  599.9 6.3 bitcast_convert_fusion.1
  606.2 12.6 %copy.21 = f32[3,1024,1024]{1,2,0:T(8,128)} copy(f32[3,1024,1024]{2,1,0:T(8,128)} %bitcast_convert_fusion.1) | data formatting | bytes 25165824 | tf_op jit(solution)/shard_map/convert_element_type | solution.py:691
  618.8 12.6 %copy.23 = f32[1,1024,3072]{2,1,0:T(8,128)} copy(f32[1,1024,3072]{1,2,0:T(8,128)} %bitcast.36) | data formatting | bytes 25165824
  631.4 11.7 %convert_bitcast_fusion = f32[1024,4,1024]{2,0,1:T(8,128)} fusion(bf16[4,1024,1024]{2,1,0:T(8,128)(2,1)} %bitcast.38), kind=kLoop, calls=%fused_computation | loop fusion | flops 4194304 | bytes 25165824 | tf_op jit(solution)/shard_map/convert_element_type | solution.py:691
  643.1 20.9 %copy.22 = f32[1024,4,1024]{2,1,0:T(4,128)} copy(f32[1024,4,1024]{2,0,1:T(8,128)} %convert_bitcast_fusion) | data formatting | bytes 33554432 | tf_op jit(solution)/shard_map/convert_element_type | solution.py:691
  664.0 20.5 %reshape.148 = f32[1,1024,4096]{2,1,0:T(8,128)} reshape(f32[1024,4,1024]{2,1,0:T(4,128)} %copy.22) | data formatting | bytes 33554432 | tf_op jit(solution)/shard_map/convert_element_type | solution.py:691
  684.5 0.0 copy-start.1
  684.5 11.8 %bitcast_convert_fusion = f32[1,4096,1024]{2,1,0:T(8,128)} fusion(bf16[1,4096,1024]{2,1,0:T(8,128)(2,1)} %bitcast.37), kind=kLoop, calls=%fused_computation.1 | loop fusion | flops 4194304 | bytes 25165824 | tf_op jit(solution)/shard_map/convert_element_type | solution.py:699
  696.4 0.0 copy-done.1
  696.4 0.0 copy-start
  696.4 2.1 copy.30
  698.5 1.6 copy-done
  700.1 2.0 copy.31
  (1 shorter events, 0.0 us)
Async XLA Ops:
  185.7 392.8 %copy-start.2 = (f32[4,128]{1,0:T(4,128)S(1)}, f32[4,128]{1,0:T(4,128)}, u32[]{:S(2)}) copy-start(f32[4,128]{1,0:T(4,128)} %get-tuple-element.22) | copy-start | bytes 6148
  586.8 13.0 %slice-start = ((bf16[50,256,1024]{2,1,0:T(8,128)(2,1)}), bf16[12,256,1024]{2,1,0:T(8,128)(2,1)S(1)}, s32[]{:S(2)}) async-start(bf16[50,256,1024]{2,1,0:T(8,128)(2,1)} %shard_map.161), calls=%async_computation | async-start | bytes 12582912 | tf_op jit(solution)/shard_map/slice | solution.py:691
  684.5 11.9 %copy-start.1 = (f32[4,256,1024]{2,1,0:T(8,128)S(1)}, f32[4,256,1024]{2,1,0:T(8,128)}, u32[]{:S(2)}) copy-start(f32[4,256,1024]{2,1,0:T(8,128)} %get-tuple-element.16) | copy-start | bytes 12582916
  696.4 3.7 copy-start

commit v3 on v2

--- a/solution.py
+++ b/solution.py
@@ -265,7 +265,7 @@
 
 
 HEADS = 8
-CHUNK = 512
+CHUNK = 1024
 LOW = jnp.bfloat16
 WIDE = jnp.float32
 NN = (((1,), (0,)), ((), ()))
@@ -301,7 +301,7 @@
 def layers_kernel(groups, tokens, cotangent, mask, embed, params, w_qkv, w_out, w_up, w_down,
                   lefts, rights, sec_out, sec_grad, g_params, g_embed, squares,
                   qkv_w, out_w, up_w, down_w, emb, src, upstream, qkv, probs, slopes, xhat_f, stats,
-                  active, keep, passed, acc, hid, wide, u_buf,
+                  keep, passed, acc, hid, u_buf,
                   w_sem, in_sem, left_sem, right_sem, wide_sem, send_sem, recv_sem):
     section = lax.axis_index("section")
     first = section == 0
@@ -330,11 +330,6 @@
     for k in (1, 2, 3):
         loads[k].start()
 
-    @pl.when(section == 1)
-    def _():
-        for g in range(groups):
-            cot_load(g).start()
-
     barrier = pltpu.get_barrier_semaphore()
     pl.semaphore_signal(barrier, inc=1, device_id={"section": other}, device_id_type=MESH)
     pl.semaphore_wait(barrier, 1)
@@ -356,139 +351,152 @@
         return pl.ds(pl.multiple_of(i * w, w), w)
 
     def left_store(g, k):
-        if k == 0:
-            return pltpu.make_async_copy(active, lefts.at[rows_of(g), pl.ds(0, units)], left_sem.at[0])
         return pltpu.make_async_copy(
             keep.at[:, pl.ds((k - 1) * width, width)], lefts.at[rows_of(g), pl.ds(units + (k - 1) * width, width)], left_sem.at[k])
 
     def right_store(g, k):
         if k == 0:
             return pltpu.make_async_copy(upstream.at[g], rights.at[rows_of(g), pl.ds(0, width)], right_sem.at[0])
-        if k == 1:
-            return pltpu.make_async_copy(active, rights.at[rows_of(g), pl.ds(width, units)], right_sem.at[1])
         return pltpu.make_async_copy(
             keep.at[:, pl.ds((k - 2) * width, width)],
             rights.at[rows_of(g), pl.ds(width + units + (k - 2) * width, width)], right_sem.at[k])
 
+    def left_chunk(g, i):
+        return pltpu.make_async_copy(
+            upstream.at[i], lefts.at[rows_of(g), pl.ds(i * CHUNK, CHUNK)], left_sem.at[5 + i])
+
+    def right_chunk(g, i):
+        return pltpu.make_async_copy(
+            slopes.at[g, :, pl.ds(i * CHUNK, CHUNK)],
+            rights.at[rows_of(g), pl.ds(width + i * CHUNK, CHUNK)], right_sem.at[6 + i])
+
     def out_store(g):
-        return pltpu.make_async_copy(wide, sec_out.at[g], wide_sem.at[0])
+        return pltpu.make_async_copy(acc, sec_out.at[g], wide_sem.at[0])
 
     def grad_store(g):
-        return pltpu.make_async_copy(wide, sec_grad.at[g], wide_sem.at[1])
+        return pltpu.make_async_copy(acc, sec_grad.at[g], wide_sem.at[1])
 
     def base_of(g):
         return jnp.where(first, 0.0, src[g].astype(WIDE)) + emb[...].astype(WIDE)
 
-    def forward(g, _):
+    stage = pl.when(section >= 0)
+
+    def heads_of(g, h):
+        return tuple(qkv[g, :, k * width + h * head:k * width + (h + 1) * head] for k in range(3))
+
+    def forward(g):
         @pl.when(first)
         def _():
             token_load(g).wait()
         @pl.when(section == 1)
         def _():
             relay(g).wait_recv()
-        @pl.when(g == 0)
-        def _():
-            loads[4].wait()
-
-        @pl.when(g > 0)
-        def _():
-            for k in (3, 4):
-                left_store(g - 1, k).wait()
-        source = src[g].astype(WIDE)
-        xhat, inverse = normalize(source)
-        stats[g, :, 0:1] = inverse
-        stats[g, :, 3:4] = jnp.mean(source, -1, keepdims=True)
-        keep[:, 3 * width:4 * width] = (xhat * params[2:3] + params[3:4]).astype(LOW)
-        base = base_of(g)
-        xhat, inverse = normalize(base)
-        stats[g, :, 1:2] = inverse
-        stats[g, :, 4:5] = jnp.mean(base, -1, keepdims=True)
-        keep[:, 2 * width:3 * width] = (xhat * params[0:1] + params[1:2]).astype(LOW)
-        left_store(g, 3).start()
-        left_store(g, 4).start()
-
-        @pl.when(g == 0)
-        def _():
-            loads[0].wait()
-
-        def project(k, a):
-            def step(i, _):
-                qkv[g, :, cols(i)] = dot(a[...], qkv_w[:, cols(i)], NN).astype(LOW)
-                return 0
-            lax.fori_loop(*k, step, 0)
-        per = width // CHUNK
-        project((0, per), keep.at[:, 2 * width:3 * width])
-        project((per, 3 * per), keep.at[:, 3 * width:4 * width])
-
-        @pl.when(g > 0)
-        def _():
-            for k in (0, 1, 2):
-                left_store(g - 1, k).wait()
-        seen = mask[g, 0:1, :] > 0
-        for h in range(HEADS):
-            q = qkv[g, :, h * head:(h + 1) * head]
-            k = qkv[g, :, width + h * head:width + (h + 1) * head]
-            v = qkv[g, :, 2 * width + h * head:2 * width + (h + 1) * head]
-            s = jnp.where(seen, dot(q, k, NT) * scale, -1e30)
-            e = jnp.exp(s - jnp.max(s, -1, keepdims=True))
-            p = (e / jnp.sum(e, -1, keepdims=True)).astype(LOW)
-            probs[g, h] = p
-            keep[:, width + h * head:width + (h + 1) * head] = dot(p, v, NN).astype(LOW)
-        left_store(g, 2).start()
-
-        @pl.when(g == 0)
-        def _():
-            loads[1].wait()
-
-        def mix(i, _):
-            hid[:, cols(i)] = dot(keep[:, width:2 * width], out_w[:, cols(i)], NN)
-            return 0
-        lax.fori_loop(0, width // CHUNK, mix, 0)
-        hidden = base_of(g) + hid[...]
-        hid[...] = hidden
-        xhat, inverse = normalize(hidden)
-        stats[g, :, 2:3] = inverse
-        xhat_f[g] = xhat.astype(LOW)
-        keep[:, 0:width] = (xhat * params[4:5] + params[5:6]).astype(LOW)
-        left_store(g, 1).start()
-
-        @pl.when(g == 0)
-        def _():
-            loads[2].wait()
-            loads[3].wait()
-
-        acc[...] = hid[...]
-        u_buf[0] = dot(keep[:, 0:width], up_w[:, cols(0)], NN)
-
-        def feed(i, _):
-            ahead = jnp.minimum(i + 1, steps - 1)
-            u_buf[lax.rem(i + 1, 2)] = dot(keep[:, 0:width], up_w[:, cols(ahead)], NN)
-            value, slope = gelu_pair(u_buf[lax.rem(i, 2)])
-            slopes[g, :, cols(i)] = slope.astype(LOW)
-            value = value.astype(LOW)
-            active[:, cols(i)] = value
-            acc[...] += dot(value, down_w[cols(i), :], NN)
-            return 0
-        lax.fori_loop(0, steps, feed, 0)
-        left_store(g, 0).start()
-
-        @pl.when(g > 0)
-        def _():
-            out_store(g - 1).wait()
-        wide[...] = acc[...]
-        out_store(g).start()
+
+        @stage
+        def _():
+            @pl.when(g == 0)
+            def _():
+                loads[4].wait()
+
+            @pl.when(g > 0)
+            def _():
+                for k in (3, 4):
+                    left_store(g - 1, k).wait()
+            source = src[g].astype(WIDE)
+            xhat, inverse = normalize(source)
+            stats[g, :, 0:1] = inverse
+            stats[g, :, 3:4] = jnp.mean(source, -1, keepdims=True)
+            keep[:, 3 * width:4 * width] = (xhat * params[2:3] + params[3:4]).astype(LOW)
+            @pl.when(g == 0)
+            def _():
+                loads[0].wait()
+            for k, rows in ((1, 3), (2, 3)):
+                part = slice(k * width, (k + 1) * width)
+                qkv[g, :, part] = dot(keep[:, rows * width:(rows + 1) * width], qkv_w[:, part], NN).astype(LOW)
+            base = base_of(g)
+            xhat, inverse = normalize(base)
+            stats[g, :, 1:2] = inverse
+            stats[g, :, 4:5] = jnp.mean(base, -1, keepdims=True)
+            keep[:, 2 * width:3 * width] = (xhat * params[0:1] + params[1:2]).astype(LOW)
+            qkv[g, :, 0:width] = dot(keep[:, 2 * width:3 * width], qkv_w[:, 0:width], NN).astype(LOW)
+            left_store(g, 3).start()
+            left_store(g, 4).start()
+
+        @stage
+        def _():
+            @pl.when(g > 0)
+            def _():
+                for k in (1, 2):
+                    left_store(g - 1, k).wait()
+            seen = mask[g, 0:1, :] > 0
+            for h in range(HEADS):
+                q, k, v = heads_of(g, h)
+                s = jnp.where(seen, dot(q, k, NT) * scale, -1e30)
+                e = jnp.exp(s - jnp.max(s, -1, keepdims=True))
+                p = (e / jnp.sum(e, -1, keepdims=True)).astype(LOW)
+                probs[g, h] = p
+                keep[:, width + h * head:width + (h + 1) * head] = dot(p, v, NN).astype(LOW)
+            left_store(g, 2).start()
+            @pl.when(g == 0)
+            def _():
+                loads[1].wait()
+
+        @stage
+        def _():
+            hid[...] = dot(keep[:, width:2 * width], out_w[...], NN)
+            hidden = base_of(g) + hid[...]
+            hid[...] = hidden
+            xhat, inverse = normalize(hidden)
+            stats[g, :, 2:3] = inverse
+            xhat_f[g] = xhat.astype(LOW)
+            keep[:, 0:width] = (xhat * params[4:5] + params[5:6]).astype(LOW)
+            left_store(g, 1).start()
+            @pl.when(g == 0)
+            def _():
+                loads[2].wait()
+                loads[3].wait()
+
+            @pl.when(g > 0)
+            def _():
+                out_store(g - 1).wait()
+                for i in range(steps):
+                    left_chunk(g - 1, i).wait()
+
+        @stage
+        def _():
+            chunks = [slice(i * CHUNK, (i + 1) * CHUNK) for i in range(steps)]
+            u_buf[0] = dot(keep[:, 0:width], up_w[:, chunks[0]], NN)
+            for i, part in enumerate(chunks):
+                if i + 1 < steps:
+                    u_buf[(i + 1) % 2] = dot(keep[:, 0:width], up_w[:, chunks[i + 1]], NN)
+                value, slope = gelu_pair(u_buf[i % 2])
+                slopes[g, :, part] = slope.astype(LOW)
+                value = value.astype(LOW)
+                upstream[i] = value
+                term = dot(value, down_w[part, :], NN)
+                if i == 0:
+                    acc[...] = hid[...] + term
+                else:
+                    acc[...] += term
+            for i in range(steps):
+                left_chunk(g, i).start()
+            out_store(g).start()
 
         @pl.when(first)
         def _():
             @pl.when(g > 0)
             def _():
                 relay(g - 1).wait_send()
+                @pl.when(g == groups - 1)
+                def _():
+                    for i in range(steps):
+                        left_chunk(g, i).wait()
             passed[...] = acc[...].astype(LOW)
             relay(g).start()
-        return 0
-
-    lax.fori_loop(0, groups, forward, 0)
-    for k in range(5):
+
+    pl.loop(0, groups)(forward)
+
+    for k in range(1, 5):
         left_store(groups - 1, k).wait()
     out_store(groups - 1).wait()
 
@@ -496,6 +504,13 @@
     def _():
         relay(groups - 1).wait_send()
 
+    @pl.when(section == 1)
+    def _():
+        for i in range(steps):
+            left_chunk(groups - 1, i).wait()
+        for g in range(groups):
+            cot_load(g).start()
+
     g_params[...] = jnp.zeros_like(g_params)
     g_embed[...] = jnp.zeros_like(g_embed)
     squares[...] = jnp.zeros_like(squares)
@@ -504,108 +519,103 @@
         g_params[row:row + 1] += jnp.sum(e * xhat, axis=0, keepdims=True)
         g_params[row + 1:row + 2] += jnp.sum(e, axis=0, keepdims=True)
 
-    def backward(g, _):
+    def backward(g):
         @pl.when(first)
         def _():
             relay_back(g).wait_recv()
         @pl.when(section == 1)
         def _():
             cot_load(g).wait()
-        @pl.when(g > 0)
-        def _():
-            for k in (0, 1):
-                right_store(g - 1, k).wait()
-        right_store(g, 0).start()
-
-        acc[...] = jnp.zeros_like(acc)
-        u_buf[0] = dot(upstream[g], down_w[cols(0), :], NT)
-
-        def feed(i, _):
-            ahead = jnp.minimum(i + 1, steps - 1)
-            u_buf[lax.rem(i + 1, 2)] = dot(upstream[g], down_w[cols(ahead), :], NT)
-            value = (u_buf[lax.rem(i, 2)] * slopes[g, :, cols(i)].astype(WIDE)).astype(LOW)
-            active[:, cols(i)] = value
-            acc[...] += dot(value, up_w[:, cols(i)], NT)
-            return 0
-        lax.fori_loop(0, steps, feed, 0)
-        right_store(g, 1).start()
-
-        e = acc[...]
-        xhat = xhat_f[g].astype(WIDE)
-        gains(4, e, xhat)
-        grad_hidden = upstream[g].astype(WIDE) + norm_back(e, params[4:5], xhat, stats[g, :, 2:3])
-        hid[...] = grad_hidden
-
-        @pl.when(g > 0)
-        def _():
+
+        @stage
+        def _():
+            @pl.when(g > 0)
+            def _():
+                for k in (2, 3, 4, 5):
+                    right_store(g - 1, k).wait()
+                right_store(g - 1, 0).wait()
+                for i in range(steps):
+                    right_chunk(g - 1, i).wait()
+                grad_store(g - 1).wait()
+            right_store(g, 0).start()
+            chunks = [slice(i * CHUNK, (i + 1) * CHUNK) for i in range(steps)]
+            u_buf[0] = dot(upstream[g], down_w[chunks[0], :], NT)
+            for i, part in enumerate(chunks):
+                if i + 1 < steps:
+                    u_buf[(i + 1) % 2] = dot(upstream[g], down_w[chunks[i + 1], :], NT)
+                value = (u_buf[i % 2] * slopes[g, :, part].astype(WIDE)).astype(LOW)
+                slopes[g, :, part] = value
+                term = dot(value, up_w[:, part], NT)
+                if i == 0:
+                    acc[...] = term
+                else:
+                    acc[...] += term
+
+        @stage
+        def _():
+            for i in range(steps):
+                right_chunk(g, i).start()
+            e = acc[...]
+            xhat = xhat_f[g].astype(WIDE)
+            gains(4, e, xhat)
+            grad_hidden = upstream[g].astype(WIDE) + norm_back(e, params[4:5], xhat, stats[g, :, 2:3])
+            hid[...] = grad_hidden
+            keep[:, 0:width] = grad_hidden.astype(LOW)
+            xhat_f[g] = dot(keep[:, 0:width], out_w[...], NT).astype(LOW)
+
+        @stage
+        def _():
+            for h in range(HEADS):
+                q, k, v = heads_of(g, h)
+                m = xhat_f[g, :, h * head:(h + 1) * head]
+                low = probs[g, h]
+                p = low.astype(WIDE)
+                gp = dot(m, v, NT)
+                ds = (p * (gp - jnp.sum(gp * p, -1, keepdims=True))).astype(LOW)
+                keep[:, width + h * head:width + (h + 1) * head] = (dot(ds, k, NN) * scale).astype(LOW)
+                keep[:, 2 * width + h * head:2 * width + (h + 1) * head] = (dot(ds, q, TN) * scale).astype(LOW)
+                keep[:, 3 * width + h * head:3 * width + (h + 1) * head] = dot(low, m, TN).astype(LOW)
             for k in (2, 3, 4, 5):
-                right_store(g - 1, k).wait()
-        keep[:, 0:width] = grad_hidden.astype(LOW)
-        right_store(g, 2).start()
-
-        def mixed_back(i, _):
-            xhat_f[g, :, cols(i)] = dot(keep[:, 0:width], out_w[cols(i), :], NT).astype(LOW)
-            return 0
-        lax.fori_loop(0, width // CHUNK, mixed_back, 0)
-
-        for h in range(HEADS):
-            q = qkv[g, :, h * head:(h + 1) * head]
-            k = qkv[g, :, width + h * head:width + (h + 1) * head]
-            v = qkv[g, :, 2 * width + h * head:2 * width + (h + 1) * head]
-            m = xhat_f[g, :, h * head:(h + 1) * head]
-            low = probs[g, h]
-            p = low.astype(WIDE)
-            gp = dot(m, v, NT)
-            ds = (p * (gp - jnp.sum(gp * p, -1, keepdims=True))).astype(LOW)
-            keep[:, width + h * head:width + (h + 1) * head] = (dot(ds, k, NN) * scale).astype(LOW)
-            keep[:, 2 * width + h * head:2 * width + (h + 1) * head] = (dot(ds, q, TN) * scale).astype(LOW)
-            keep[:, 3 * width + h * head:3 * width + (h + 1) * head] = dot(low, m, TN).astype(LOW)
-        for k in (3, 4, 5):
-            right_store(g, k).start()
-
-        def query_back(i, _):
-            acc[:, cols(i)] = dot(keep[:, width:2 * width], qkv_w[cols(i), 0:width], NT)
-            return 0
-        lax.fori_loop(0, width // CHUNK, query_back, 0)
-        e = acc[...]
-        xhat = (base_of(g) - stats[g, :, 4:5]) * stats[g, :, 1:2]
-        gains(0, e, xhat)
-        grad_base = hid[...] + norm_back(e, params[0:1], xhat, stats[g, :, 1:2])
-        g_embed[...] += grad_base
-        hid[...] = grad_base
-
-        def key_back(i, _):
-            acc[:, cols(i)] = dot(keep[:, 2 * width:4 * width], qkv_w[cols(i), width:3 * width], NT)
-            return 0
-        lax.fori_loop(0, width // CHUNK, key_back, 0)
-        e = acc[...]
-        xhat = (src[g].astype(WIDE) - stats[g, :, 3:4]) * stats[g, :, 0:1]
-        gains(2, e, xhat)
-        grad_source = norm_back(e, params[2:3], xhat, stats[g, :, 0:1])
-
-        @pl.when(g > 0)
-        def _():
-            grad_store(g - 1).wait()
-        wide[...] = grad_source
+                right_store(g, k).start()
+
+        @stage
+        def _():
+            acc[...] = dot(keep[:, width:2 * width], qkv_w[:, 0:width], NT)
+            u_buf[0] = dot(keep[:, 2 * width:4 * width], qkv_w[:, width:3 * width], NT)
+            e = acc[...]
+            xhat = (base_of(g) - stats[g, :, 4:5]) * stats[g, :, 1:2]
+            gains(0, e, xhat)
+            grad_base = hid[...] + norm_back(e, params[0:1], xhat, stats[g, :, 1:2])
+            g_embed[...] += grad_base
+            hid[...] = grad_base
+
+        @stage
+        def _():
+            e = u_buf[0]
+            xhat = (src[g].astype(WIDE) - stats[g, :, 3:4]) * stats[g, :, 0:1]
+            gains(2, e, xhat)
+            acc[...] = norm_back(e, params[2:3], xhat, stats[g, :, 0:1])
 
         @pl.when(section == 1)
         def _():
             @pl.when(g > 0)
             def _():
                 relay_back(g - 1).wait_send()
-            low = (wide[...] + hid[...]).astype(LOW)
+            low = (acc[...] + hid[...]).astype(LOW)
             passed[...] = low
             relay_back(g).start()
-            wide[...] = low.astype(WIDE)
+            acc[...] = low.astype(WIDE)
         grad_store(g).start()
-        total = wide[...]
+        total = acc[...]
         squares[pl.ds(g, 1), :] = jnp.broadcast_to(
             jnp.sum(jnp.sum(total * total, axis=0, keepdims=True), axis=1, keepdims=True), (1, squares.shape[1]))
-        return 0
-
-    lax.fori_loop(0, groups, backward, 0)
-    for k in range(6):
+
+    pl.loop(0, groups)(backward)
+
+    for k in (0, 2, 3, 4, 5):
         right_store(groups - 1, k).wait()
+    for i in range(steps):
+        right_chunk(groups - 1, i).wait()
     grad_store(groups - 1).wait()
 
     @pl.when(section == 1)
@@ -640,23 +650,21 @@
             pltpu.VMEM(w_down.shape, LOW),
             pltpu.VMEM((slots, width), LOW),
             pltpu.VMEM((groups, slots, width), LOW),
-            pltpu.VMEM((groups, slots, width), LOW),
+            pltpu.VMEM((max(groups, units // CHUNK), slots, width), LOW),
             pltpu.VMEM((groups, slots, 3 * width), LOW),
             pltpu.VMEM((groups, HEADS, slots, slots), LOW),
             pltpu.VMEM((groups, slots, units), LOW),
             pltpu.VMEM((groups, slots, width), LOW),
             pltpu.VMEM((groups, slots, 128), WIDE),
-            pltpu.VMEM((slots, units), LOW),
             pltpu.VMEM((slots, 4 * width), LOW),
             pltpu.VMEM((slots, width), LOW),
-            pltpu.VMEM((slots, width), WIDE),
             pltpu.VMEM((slots, width), WIDE),
             pltpu.VMEM((slots, width), WIDE),
             pltpu.VMEM((2, slots, CHUNK), WIDE),
             pltpu.SemaphoreType.DMA((5,)),
             pltpu.SemaphoreType.DMA((2 * groups,)),
-            pltpu.SemaphoreType.DMA((5,)),
-            pltpu.SemaphoreType.DMA((6,)),
+            pltpu.SemaphoreType.DMA((5 + units // CHUNK,)),
+            pltpu.SemaphoreType.DMA((6 + units // CHUNK,)),
             pltpu.SemaphoreType.DMA((2,)),
             pltpu.SemaphoreType.DMA((2 * groups,)),
             pltpu.SemaphoreType.DMA((2 * groups,)),
@@ -665,6 +673,37 @@
             collective_id=cid, has_side_effects=True, vmem_limit_bytes=63 * 2**20),
         cost_estimate=pl.CostEstimate(flops=54 * 10**9, bytes_accessed=120 * 2**20, transcendentals=10**7),
     )(tokens, cotangent, mask, embed, params, w_qkv, w_out, w_up, w_down)
+
+
+def widen_kernel(ranges, block, *outs):
+    step = pl.program_id(0)
+    for (first, last), out in zip(ranges, outs):
+        @pl.when((step >= first) & (step < last))
+        def _():
+            out[...] = block[0].astype(out.dtype)
+
+
+def widen(sums, places):
+    tile, width = sums.shape[1:]
+    steps = sum(p[1] for p in places)
+
+    def place(first, count, tall, wide):
+        def index(step):
+            k = jnp.clip(step - first, 0, count - 1)
+            if wide == 1:
+                return k, 0
+            return lax.rem(k, tall), lax.div(k, tall)
+        return pl.BlockSpec((tile, width), index)
+
+    return pl.pallas_call(
+        lambda *refs: widen_kernel(tuple((p[0], p[0] + p[1]) for p in places), *refs),
+        grid=(steps,),
+        out_shape=tuple(jax.ShapeDtypeStruct((p[2] * tile, p[3] * width), jnp.float32) for p in places),
+        in_specs=[pl.BlockSpec((1, tile, width), lambda step: (step, 0, 0))],
+        out_specs=tuple(place(*p) for p in places),
+        compiler_params=pltpu.CompilerParams(vmem_limit_bytes=32 * 2**20),
+        cost_estimate=pl.CostEstimate(flops=0, bytes_accessed=6 * steps * tile * width, transcendentals=0),
+    )(sums)
 
 
 def body(tokens, clip_frames, cotangent, embed, norm_params, w_qkv, w_out, w_up, w_down):
@@ -686,17 +725,14 @@
     sums = weight_sums(lines_of(lax.axis_size("dp")), lefts, rights, extras, 1)
     overall = jnp.sum(sums[49, 6].astype(WIDE)) / jnp.sum(factors)
     norms = magnitude / (overall / (groups * lax.axis_size("dp")))
-    blocks = sums[:48].reshape(12, width, width)
-    beside = lambda first, last: (
-        blocks[first:last].transpose(1, 0, 2).reshape(width, -1).astype(WIDE)
-    )
+    down, up, out, qkv = widen(sums, ((0, 16, 16, 1), (16, 16, 4, 4), (32, 4, 4, 1), (36, 12, 4, 3)))
     return (
         outcome[None],
         grad_inputs[None],
-        beside(9, 12)[None],
-        beside(8, 9)[None],
-        beside(4, 8)[None],
-        blocks[0:4].reshape(units, width).astype(WIDE)[None],
+        qkv[None],
+        out[None],
+        up[None],
+        down[None],
         sums[49, :6].astype(WIDE)[None],
         sums[48].astype(WIDE)[None],
         norms[None],

time: 704 us -> 585 us (0.83)
  local copies, waits for them, and re-layouts: 90.6 us -> 9.17 us
  other arithmetic: 42.9 us -> 10.6 us
    convert_element_type x3 -> x0, local copies, waits for them, and re-layouts: 54 us -> none  [body(): blocks[first:last].transpose(1, 0, 2).reshape(width, -1).astype(WIDE)]
    pallas_call x1, Pallas kernels: 176 us -> 128 us  [layers(): pl.pallas_call(functools.partial(layers_kernel, groups), out_shape=(shape...]
    pallas_call x0 -> x1, Pallas kernels: none -> 40.4 us  [widen(): pl.pallas_call(lambda *refs: widen_kernel(tuple(((p[0], p[0] + p[1]) for...]
    convert_element_type x4 -> x0, other arithmetic: 32.3 us -> none  [the longest x3 20.5 us: body(): blocks[first:last].transpose(1, 0, 2).reshape(width, -1).astype(WIDE)]
    slice x4 -> x0, local copies, waits for them, and re-layouts: 14.8 us -> none  [the longest x1 12.5 us: body(): blocks[0:4].reshape(units, width).astype(WIDE)[None]]
    unnamed x11 -> x10, local copies, waits for them, and re-layouts: 20.3 us -> 7.71 us
where the time goes in v3:
time: 585 us; the launch traced here: 584 us
  Pallas kernels  562 us (96%)
  other arithmetic  10.6 us (2%)
  local copies, waits for them, and re-layouts  9.17 us (2%)
    pallas_call x1, Pallas kernels, weight_sums(): pl.pallas_call(functools.partial(weights_kernel, dims, jobs, extra), out_...  393 us
    pallas_call x1, Pallas kernels, layers(): pl.pallas_call(functools.partial(layers_kernel, groups), out_shape=(shape...  128 us
    pallas_call x1, Pallas kernels, widen(): pl.pallas_call(lambda *refs: widen_kernel(tuple(((p[0], p[0] + p[1]) for...  40.4 us

profile of v3, /device:TPU:0, one launch (start us, length us, event | category | flops | bytes accessed | tf_op | source)
XLA Modules:
  0.0 583.8 jit_solution(5368875701774955244)
XLA Ops:
  0.6 0.6 add_reduce_fusion
  1.3 0.7 broadcast_multiply_fusion
  1.9 0.1 pad.4.clone
  2.0 0.1 fusion.1
  2.1 0.6 broadcast_in_dim.16.mask
  2.7 1.4 copy.22
  4.0 128.3 %shard_map.160 = (bf16[1024,8192]{1,0:T(8,128)(2,1)}, bf16[1024,9216]{1,0:T(8,128)(2,1)}, f32[4,256,1024]{2,1,0:T(8,128)}, f32[4,256,1024]{2,1,0:T(8,128)}, f32[...) custom-call(bf16[4,256,1024]{2,1,0:T(8,128)(2,1)} %tokens.1, bf16[4,256,1024]{2,1,0:T(8,128)(2,1)} %cotangent.1, ...), custom_call_target="tpu_custom_call" | custom-call | flops 54000001024 | bytes 125829120 | tf_op jit(solution)/shard_map/pallas_call | solution.py:633
  132.4 1.3 fusion.2
  133.7 0.7 multiply_convert_fusion
  134.3 0.8 slice.31
  135.1 0.1 maximum_bitcast_fusion
  135.2 1.3 convert_bitcast_fusion
  136.5 1.1 pad_maximum_fusion.extra_ref
  137.6 0.0 copy-start.2
  137.6 393.3 %shard_map.161.refs_0_ = bf16[50,256,1024]{2,1,0:T(8,128)(2,1)} custom-call(bf16[1024,8192]{1,0:T(8,128)(2,1)} %get-tuple-element.22.left_ref, bf16[1024,9216]{1,0:T(8,128)(2,1)} %get-tuple-element.23.right_ref, bf16[2,256,1024]{2,1,0:T(8,128)(2,1)} %pad_maximum_fusion.extra_ref), custom_call_target="tpu_custom_call" | custom-call | flops 25769803776 | bytes 104857600 | tf_op jit(solution)/shard_map/pallas_call | solution.py:247
  530.9 1.3 convert_reduce_fusion
  533.5 0.0 copy-done.2
  533.6 0.6 divide_reduce_fusion
  534.2 0.7 slice_convert_fusion.2
  534.9 0.6 copy.19
  535.5 2.1 slice_convert_fusion
  537.7 0.0 copy-start.1
  537.7 40.4 %shard_map.162 = (f32[4096,1024]{1,0:T(8,128)}, f32[1024,4096]{1,0:T(8,128)}, f32[1024,1024]{1,0:T(8,128)}, f32[1024,3072]{1,0:T(8,128)}) custom-call(bf16[50,256,1024]{2,1,0:T(8,128)(2,1)} %shard_map.161.refs_0_), custom_call_target="tpu_custom_call" | custom-call | bytes 75497472 | tf_op jit(solution)/shard_map/pallas_call | solution.py:698
  578.1 0.0 copy-start
  578.1 0.0 copy-done.1
  578.1 2.1 copy.25
  580.2 1.6 copy-done
  581.8 2.0 copy.26
  (1 shorter events, 0.0 us)
Async XLA Ops:
  137.6 396.0 %copy-start.2 = (f32[4,128]{1,0:T(4,128)S(1)}, f32[4,128]{1,0:T(4,128)}, u32[]{:S(2)}) copy-start(f32[4,128]{1,0:T(4,128)} %get-tuple-element.26) | copy-start | bytes 6148
  537.7 40.4 %copy-start.1 = (f32[4,256,1024]{2,1,0:T(8,128)S(1)}, f32[4,256,1024]{2,1,0:T(8,128)}, u32[]{:S(2)}) copy-start(f32[4,256,1024]{2,1,0:T(8,128)} %get-tuple-element.20) | copy-start | bytes 12582916
  578.1 3.7 copy-start

commit v4 on v3

--- a/solution.py
+++ b/solution.py
@@ -9,10 +9,15 @@
 
 MESH = pl.DeviceIdType.MESH
 TILE = 256
+WIDTH = 1024
 RING = 8
-WIDTH = 1024
-SPLIT = (80, 64, 48, 64)
-ORDERS = ((2, 1, 0), (1, 2, 0), (0, 2, 1), (0, 1, 2))
+SHARES = (
+    (0, 80, 2, ((1, 0),), False),
+    (160, 48, 0, ((2, 1), (1, 2)), False),
+    (208, 48, 0, ((1, 2), (2, 1)), True),
+    (80, 80, 1, ((2, 0),), False),
+)
+MIDDLE_ROWS = 48
 
 
 def lines_of(size):
@@ -23,145 +28,229 @@
     return (2 * short, short, short)
 
 
-class Plan:
-    def __init__(self, dims):
-        d = lax.axis_index("dp")
-        self.d = d
-        self.dims = dims
-        self.strides = (dims[1] * dims[2], dims[2], 1)
-        self.coords = tuple(lax.rem(lax.div(d, s), n) for s, n in zip(self.strides, dims))
-        self.depth = 2 * (sum(dims) - 3)
-
-
-def stages(plan):
-    found = []
-    row = 0
-    for kind, order in enumerate(ORDERS):
-        delay = 0
-        left, free = 0, 0
-        active = None
-        bases = []
-        for phase, axis in enumerate(order):
-            n, c = plan.dims[axis], plan.coords[axis]
-            w = WIDTH >> (phase + 1)
-            bases.append((delay, left, free, active, axis, w))
-            delay += n - 1
-            top = c == n - 1
-            left = left + jnp.where(top, w, 0)
-            free = free + jnp.where(top, 0, w)
-            if n > 2:
-                end = (c == 0) | top
-                active = end if active is None else active & end
-        for phase in range(3):
-            found.append(("sum", kind, phase, row) + tuple(bases[phase]))
-        for phase in (2, 1, 0):
-            _, left, free, active, axis, w = bases[phase]
-            found.append(("spread", kind, phase, row, delay, left, free, active, axis, w))
-            delay += plan.dims[axis] - 1
-        row += SPLIT[kind]
-    return found
-
-
 def both(*terms):
     out = None
     for t in terms:
-        if t is None:
-            continue
-        out = t if out is None else out & t
+        if t is not None:
+            out = t if out is None else out & t
     return out
 
 
-def copies(plan, stage, up, tick, total, held, landing, result, send_sem, recv_sem):
-    what, kind, phase, row, delay, left, free, active, axis, w = stage
-    n, c, stride = plan.dims[axis], plan.coords[axis], plan.strides[axis]
-    toward_top = up if what == "sum" else not up
-    hops = c if toward_top else n - 1 - c
-    job = tick - delay - hops
-    ok = both(job >= 0, job < total, active)
-    job = jnp.clip(job, 0, total - 1)
-    rows = pl.ds(row, SPLIT[kind])
-    col = pl.ds(pl.multiple_of(left + (w if up else 0), 128), w)
-    stream = (kind * 6 + (phase if what == "sum" else 3 + phase)) * 2 + int(up)
-    if what == "sum":
-        land = pl.ds(pl.multiple_of(free + (w if up else 0), 128), w)
-        src = held.at[job, rows, col]
-        dst = landing.at[job, rows, land]
+def lanes_of(n, wide):
+    return 1 if n == 2 else 4 if wide else 2
+
+
+class Flow:
+    def __init__(self, row, count, middle, phase, axis, n, c, w, owners, left, free, active, parity, lag, summing):
+        self.row, self.count, self.middle, self.phase, self.axis = row, count, middle, phase, axis
+        self.n, self.c, self.w, self.owners, self.left, self.free = n, c, w, owners, left, free
+        self.active, self.parity, self.lag, self.summing = active, parity, lag, summing
+
+
+class Own:
+    def __init__(self, row, count, left, active, parity, sem, turns):
+        self.row, self.count, self.left, self.active = row, count, left, active
+        self.parity, self.sem, self.turns = parity, sem, turns
+
+
+class Plan:
+    def __init__(self, dims, total):
+        self.d = lax.axis_index("dp")
+        self.dims = dims
+        self.total = total
+        self.strides = (dims[1] * dims[2], dims[2], 1)
+        self.coords = tuple(lax.rem(lax.div(self.d, s), n) for s, n in zip(self.strides, dims))
+        self.depth = self.streams = self.arrivals = self.owns = 0
+        self.shares = [self.lay_out(*share) for share in SHARES]
+
+    def flow(self, **fields):
+        f = Flow(**fields)
+        f.turns = self.total if f.parity is None else (self.total + 1 - f.parity) // 2
+        f.wide = f.middle and f.phase == 0 and f.n > 2
+        f.lanes = lanes_of(f.n, f.wide)
+        f.stream, f.arrival = self.streams, self.arrivals
+        self.streams += f.lanes
+        self.arrivals += f.lanes * f.turns
+        return f
+
+    def lay_out(self, row, count, axis, orders, middle):
+        share = dict(row=row, count=count, middle=middle)
+
+        def phase(p, axis, lag, left, free, active, parity):
+            n, c = self.dims[axis], self.coords[axis]
+            w = WIDTH >> (p + 1)
+            inner = middle and p == 0 and n > 2
+            owners = (n // 2 - 1, n // 2) if inner else (0, n - 1)
+            top = c == owners[1]
+            half = jnp.where(top, w, 0)
+            used = 0 if middle and p == 0 else w - half
+            now = both(active, (c == owners[0]) | top) if n > 2 else active
+            fields = dict(share, phase=p, axis=axis, n=n, c=c, w=w, owners=owners, left=left, free=free,
+                          active=active, parity=parity)
+            hops = (n // 2 if inner else n - 1, max(owners[1], n - 1 - owners[0]))
+            return fields, hops, left + half, free + used, now
+
+        free = 512 if middle else 0
+        first, hops, left, free, gate = phase(0, axis, 0, 0, free, None, None)
+        start = hops[0]
+        inner = []
+        for parity, order in enumerate(orders):
+            key = None if len(orders) == 1 else parity
+            lag = start
+            second, hops2, left2, free2, gate2 = phase(1, order[0], lag, left, free, gate, key)
+            third, hops3, left3, _, gate3 = phase(2, order[1], lag, left2, free2, gate2, key)
+            own = Own(row=row, count=count, left=left3, active=gate3, parity=key, sem=self.owns,
+                       turns=self.total if key is None else (self.total + 1 - key) // 2)
+            self.owns += own.turns
+            flows = [self.flow(**second, lag=lag, summing=True)]
+            lag += hops2[0]
+            flows.append(self.flow(**third, lag=lag, summing=True))
+            lag += hops3[0]
+            own.start = lag
+            flows.append(self.flow(**third, lag=lag, summing=False))
+            lag += hops3[1]
+            own.end = lag
+            flows.append(self.flow(**second, lag=lag, summing=False))
+            lag += hops2[1]
+            inner.append((key, flows, own))
+        before = self.flow(**first, lag=0, summing=True)
+        after = self.flow(**first, lag=lag, summing=False)
+        self.depth = max(self.depth, lag + hops[1])
+        return before, gate, inner, after
+
+
+def due(plan, job, steady, parity, *terms):
+    return both(None if steady else (job >= 0) & (job < plan.total),
+                None if parity is None else lax.rem(job, 2) == parity, *terms)
+
+
+def when(ok):
+    return (lambda f: f()) if ok is None else pl.when(ok)
+
+
+def move(plan, flow, refs, job, cols, spot, step, lane, short=False):
+    held, landing, side, result, send_sem, recv_sem = refs
+    turn = job if flow.parity is None else lax.div(job, 2)
+    rows = pl.ds(flow.row, flow.count)
+    at = lambda first: pl.ds(first if isinstance(first, int) else pl.multiple_of(first, 128), flow.w)
+    if not flow.summing:
+        src = dst = result.at[job, rows, at(cols)]
     else:
-        src = result.at[job, rows, col]
-        dst = result.at[job, rows, col]
-    step = stride if toward_top else -stride
+        src = held.at[job, rows, at(cols)]
+        if short or (flow.middle and flow.phase > 0):
+            dst = side.at[job, pl.ds(0, flow.count), at(spot)]
+        else:
+            dst = landing.at[job, rows, at(spot)]
+
     def make(source):
         return pltpu.make_async_remote_copy(
-            src_ref=source, dst_ref=dst,
-            send_sem=send_sem.at[stream, lax.rem(job, RING)], recv_sem=recv_sem.at[stream, job],
+            src_ref=source, dst_ref=dst, send_sem=send_sem.at[flow.stream + lane, lax.rem(turn, RING)],
+            recv_sem=recv_sem.at[flow.arrival + lane * flow.turns + turn],
             device_id={"dp": plan.d + step}, device_id_type=MESH)
-    def send(source):
-        copy = make(source)
-        @pl.when(job >= RING)
+
+    def send(first_owner=False):
+        copy = make(held.at[job, rows, at(cols)] if first_owner else src)
+        @pl.when(turn >= RING)
         def _():
             copy.wait_send()
         copy.start()
-    return make, send, src, dst, ok, hops, n, job, rows, col
-
-
-def comm_tick(plan, table, kinds, tick, total, held, landing, result, send_sem, recv_sem, own_sem):
-    for stage in table:
-        what, kind, phase = stage[:3]
-        if kind not in kinds:
-            continue
-        for up in (True, False):
-            make, send, src, dst, ok, hops, n, job, rows, col = copies(
-                plan, stage, up, tick, total, held, landing, result, send_sem, recv_sem)
-            if what == "sum":
-                @pl.when(ok & (hops > 0))
-                def _():
-                    make(src).wait_recv()
-                    held[job, rows, col] = held[job, rows, col] + dst[...]
-                @pl.when(ok & (hops < n - 1))
-                def _():
-                    send(src)
+
+    def receive():
+        make(src).wait_recv()
+        if flow.summing:
+            place = (job, rows, at(cols))
+            held[place] = held[place] + dst[...]
+
+    def finish():
+        @pl.when(turn >= flow.turns - RING)
+        def _():
+            make(src).wait_send()
+
+    return send, receive, finish
+
+
+def run_flow(plan, flow, tick, refs, steady, ending=False):
+    n, c, w, left = flow.n, flow.c, flow.w, flow.left
+    stride = plan.strides[flow.axis]
+    from_held = not flow.summing and flow.phase == 2
+    if n == 2:
+        own, other = jnp.where(c == 1, w, 0), jnp.where(c == 1, 0, w)
+        out, back = (other, own) if flow.summing else (own, other)
+        step = jnp.where(c == 1, -stride, stride)
+        job = tick - flow.lag
+        send, _, finish = move(plan, flow, refs, job, left + out, flow.free + out, step, 0)
+        @when(due(plan, job, steady, flow.parity))
+        def _():
+            finish() if ending else send(from_held)
+        if not ending:
+            job = job - 1
+            _, receive, _ = move(plan, flow, refs, job, left + back, flow.free + back, step, 0)
+            @when(due(plan, job, steady, flow.parity))
+            def _():
+                receive()
+        return
+    for up in (True, False):
+        owner = flow.owners[int(up)]
+        for below in (True, False):
+            if (owner if below else n - 1 - owner) == 0:
+                continue
+            place = c <= owner if below else c >= owner
+            if flow.summing:
+                hops = c if below else n - 1 - c
+                sends = c < owner if below else c > owner
+                step = stride if below else -stride
             else:
-                if phase == 2:
-                    @pl.when(ok & (hops == 0))
-                    def _():
-                        mine = held.at[job, rows, col]
-                        send(mine)
-                        pltpu.make_async_copy(mine, dst, own_sem.at[kind, job]).start()
-                    @pl.when(ok & (hops > 0))
-                    def _():
-                        make(src).wait_recv()
-                    if n > 2:
-                        @pl.when(ok & (hops > 0) & (hops < n - 1))
+                hops = owner - c if below else c - owner
+                sends = c > 0 if below else c < n - 1
+                step = -stride if below else stride
+            job = tick - flow.lag - hops
+            lower = w if up else 0
+            short = flow.summing and flow.middle and flow.phase == 0 and up != below
+            if short:
+                spot = 0
+            elif flow.middle and flow.phase == 0:
+                spot = lower
+            else:
+                spot = flow.free + lower
+            send, receive, finish = move(
+                plan, flow, refs, job, left + lower, spot, step, 2 * int(up) + int(below) if flow.wide else int(up), short)
+            @when(due(plan, job, steady, flow.parity, place, flow.active if flow.phase == 2 else None))
+            def _():
+                if ending:
+                    pl.when(sends)(finish)
+                    return
+                pl.when(hops > 0)(receive)
+                if from_held:
+                    pl.when(sends & (hops == 0))(functools.partial(send, True))
+                    pl.when(sends & (hops > 0))(send)
+                else:
+                    pl.when(sends)(send)
+
+
+def own_copy(plan, own, refs, job, own_sem):
+    turn = job if own.parity is None else lax.div(job, 2)
+    part = (job, pl.ds(own.row, own.count), pl.ds(pl.multiple_of(own.left, 128), WIDTH >> 3))
+    return pltpu.make_async_copy(refs[0].at[part], refs[3].at[part], own_sem.at[own.sem + turn])
+
+
+def serve(plan, shares, tick, refs, own_sem, steady, ending=False):
+    for k in shares:
+        before, gate, inner, after = plan.shares[k]
+        run_flow(plan, before, tick, refs, steady, ending)
+
+        @when(gate)
+        def _():
+            for parity, flows, own in inner:
+                for flow in flows:
+                    if not flow.summing and not ending:
+                        opens = flow.phase == 2
+                        job = tick - (own.start if opens else own.end)
+                        @when(due(plan, job, steady, parity, own.active))
                         def _():
-                            send(src)
-                else:
-                    if phase == 1:
-                        last = [s for s in table if s[1] == kind and s[0] == "spread" and s[2] == 2][0]
-                        _, _, _, _, _, left3, _, active3, axis3, w3 = last
-                        c3, n3 = plan.coords[axis3], plan.dims[axis3]
-                        top3 = c3 == n3 - 1
-                        own = held.at[job, rows, pl.ds(pl.multiple_of(left3 + jnp.where(top3, w3, 0), 128), w3)]
-                        own_dst = result.at[job, rows, pl.ds(pl.multiple_of(left3 + jnp.where(top3, w3, 0), 128), w3)]
-                        @pl.when(both(ok, hops == 0, (c3 == 0) | top3 if n3 > 2 else None))
-                        def _():
-                            pltpu.make_async_copy(own, own_dst, own_sem.at[kind, job]).wait()
-                    @pl.when(ok & (hops > 0))
-                    def _():
-                        make(src).wait_recv()
-                    @pl.when(ok & (hops < n - 1))
-                    def _():
-                        send(src)
-
-
-def drain(plan, table, tick, total, held, landing, result, send_sem, recv_sem):
-    for stage in table:
-        what, kind, phase = stage[:3]
-        for up in (True, False):
-            make, send, src, dst, ok, hops, n, job, rows, col = copies(
-                plan, stage, up, tick, total, held, landing, result, send_sem, recv_sem)
-            @pl.when(ok & (hops < n - 1) & (job >= total - RING))
-            def _():
-                make(src).wait_send()
+                            copy = own_copy(plan, own, refs, job, own_sem)
+                            copy.start() if opens else copy.wait()
+                    run_flow(plan, flow, tick, refs, steady, ending)
+        run_flow(plan, after, tick, refs, steady, ending)
 
 
 def greet(plan):
@@ -176,90 +265,104 @@
     pl.semaphore_wait(barrier, count)
 
 
-def weights_kernel(dims, jobs, extra, left_ref, right_ref, extra_ref, result, held, landing,
+def weights_kernel(dims, tiles, total, left_ref, right_ref, extra_ref, result, held, landing, side,
                    left_buf, right_buf, load_sem, send_sem, recv_sem, own_sem):
-    plan = Plan(dims)
-    table = stages(plan)
-    total = 4 * jobs + extra
+    plan = Plan(dims, total)
+    per = WIDTH // TILE
     greet(plan)
 
     def left_copy(s):
-        job, part, slot = lax.div(s, 4), lax.rem(s, 4), lax.rem(s, 2)
+        job, part = lax.div(s, per), lax.rem(s, per)
         slab = jnp.where(job < 4, job, jnp.where(job < 8, 4, jnp.minimum(job - 3, 7)))
         return pltpu.make_async_copy(
             left_ref.at[:, pl.ds(pl.multiple_of(slab * WIDTH + part * TILE, TILE), TILE)],
-            left_buf.at[slot], load_sem.at[slot])
+            left_buf, load_sem.at[0])
 
     def right_copy(job):
-        slot = lax.rem(job, 2)
         slab = jnp.where(job < 4, 0, job - 3)
         return pltpu.make_async_copy(
             right_ref.at[:, pl.ds(pl.multiple_of(slab * WIDTH, WIDTH), WIDTH)],
-            right_buf.at[slot], load_sem.at[2 + slot])
+            right_buf, load_sem.at[1])
 
     def product(s):
-        job = lax.div(s, 4)
         left_copy(s).wait()
-        @pl.when(lax.rem(s, 4) == 0)
-        def _():
-            right_copy(job).wait()
-            @pl.when(job + 1 < jobs)
-            def _():
-                right_copy(job + 1).start()
-        @pl.when(s + 1 < 4 * jobs)
+        @pl.when(lax.rem(s, per) == 0)
+        def _():
+            right_copy(lax.div(s, per)).wait()
+        held[s] = lax.dot_general(
+            left_buf[...], right_buf[...], (((0,), (0,)), ((), ())),
+            preferred_element_type=jnp.float32).astype(jnp.bfloat16)
+        @pl.when(s + 1 < tiles)
         def _():
             left_copy(s + 1).start()
-        a = left_buf[lax.rem(s, 2)]
-        b = right_buf[lax.rem(job, 2)]
-        held[s] = lax.dot_general(a, b, (((0,), (0,)), ((), ())), preferred_element_type=jnp.float32).astype(jnp.bfloat16)
-
-    extras = pltpu.make_async_copy(extra_ref, held.at[pl.ds(4 * jobs, extra)], load_sem.at[4])
-    extras.start()
+            @pl.when(lax.rem(s + 1, per) == 0)
+            def _():
+                right_copy(lax.div(s + 1, per)).start()
+
+    extras = pltpu.make_async_copy(extra_ref, held.at[pl.ds(tiles, total - tiles)], load_sem.at[2])
     left_copy(0).start()
     right_copy(0).start()
+    extras.start()
     product(0)
     extras.wait()
-
-    args = (total, held, landing, result, send_sem, recv_sem)
-
-    def tick(t, _):
-        comm_tick(plan, table, (0, 2), t, *args, own_sem)
-        @pl.when(t + 1 < 4 * jobs)
+    refs = (held, landing, side, result, send_sem, recv_sem)
+
+    def tick(steady, t, _):
+        serve(plan, (0, 1), t, refs, own_sem, steady)
+        @pl.when(t + 1 < tiles)
         def _():
             product(t + 1)
-        comm_tick(plan, table, (1, 3), t, *args, own_sem)
+        serve(plan, (2, 3), t, refs, own_sem, steady)
         return 0
 
-    lax.fori_loop(0, total + plan.depth, tick, 0)
+    lax.fori_loop(0, plan.depth, functools.partial(tick, False), 0)
+    lax.fori_loop(plan.depth, total, functools.partial(tick, True), 0)
+    lax.fori_loop(total, total + plan.depth, functools.partial(tick, False), 0)
 
     def finish(t, _):
-        drain(plan, table, t, *args)
+        serve(plan, range(len(SHARES)), t, refs, own_sem, False, True)
         return 0
 
     lax.fori_loop(0, total + plan.depth, finish, 0)
 
 
+def semaphores(dims, total):
+    streams = arrivals = owns = 0
+    for _, _, axis, orders, middle in SHARES:
+        for parity, order in enumerate(orders):
+            turns = total if len(orders) == 1 else (total + 1 - parity) // 2
+            owns += turns
+            for line in order:
+                lanes = lanes_of(dims[line], False)
+                streams, arrivals = streams + 2 * lanes, arrivals + 2 * lanes * turns
+        lanes = lanes_of(dims[axis], middle and dims[axis] > 2)
+        streams, arrivals = streams + 2 * lanes, arrivals + 2 * lanes * total
+    return streams, arrivals, owns
+
+
 def weight_sums(dims, lefts, rights, extras, cid):
-    jobs, extra = 12, extras.shape[0]
-    total = 4 * jobs + extra
+    tiles = 12 * (WIDTH // TILE)
+    total = tiles + extras.shape[0]
     rows = lefts.shape[0]
+    streams, arrivals, owns = semaphores(dims, total)
     any_space = pl.BlockSpec(memory_space=pl.ANY)
     return pl.pallas_call(
-        functools.partial(weights_kernel, dims, jobs, extra),
+        functools.partial(weights_kernel, dims, tiles, total),
         out_shape=jax.ShapeDtypeStruct((total, TILE, WIDTH), jnp.bfloat16),
         in_specs=[any_space] * 3,
         out_specs=any_space,
         scratch_shapes=[
             pltpu.VMEM((total, TILE, WIDTH), jnp.bfloat16),
             pltpu.VMEM((total, TILE, WIDTH), jnp.bfloat16),
-            pltpu.VMEM((2, rows, TILE), jnp.bfloat16),
-            pltpu.VMEM((2, rows, WIDTH), jnp.bfloat16),
-            pltpu.SemaphoreType.DMA((5,)),
-            pltpu.SemaphoreType.DMA((48, RING)),
-            pltpu.SemaphoreType.DMA((48, total)),
-            pltpu.SemaphoreType.DMA((4, total)),
+            pltpu.VMEM((total, MIDDLE_ROWS, WIDTH), jnp.bfloat16),
+            pltpu.VMEM((rows, TILE), jnp.bfloat16),
+            pltpu.VMEM((rows, WIDTH), jnp.bfloat16),
+            pltpu.SemaphoreType.DMA((3,)),
+            pltpu.SemaphoreType.DMA((streams, RING)),
+            pltpu.SemaphoreType.DMA((arrivals,)),
+            pltpu.SemaphoreType.DMA((owns,)),
         ],
-        compiler_params=pltpu.CompilerParams(collective_id=cid, has_side_effects=True, vmem_limit_bytes=62 * 2**20),
+        compiler_params=pltpu.CompilerParams(collective_id=cid, has_side_effects=True, vmem_limit_bytes=63 * 2**20),
         cost_estimate=pl.CostEstimate(flops=2 * 12 * rows * WIDTH * WIDTH, bytes_accessed=100 * 2**20, transcendentals=0),
     )(lefts, rights, extras)
 

time: 585 us -> 554 us (0.947)
  Pallas kernels: 562 us -> 531 us
    pallas_call x1, Pallas kernels: 393 us -> 362 us  [weight_sums(): pl.pallas_call(functools.partial(weights_kernel, dims, tiles, total), out...]
where the time goes in v4:
time: 554 us; the launch traced here: 553 us
  Pallas kernels  531 us (96%)
  other arithmetic  10.6 us (2%)
  local copies, waits for them, and re-layouts  9.17 us (2%)
    pallas_call x1, Pallas kernels, weight_sums(): pl.pallas_call(functools.partial(weights_kernel, dims, tiles, total), out...  362 us
    pallas_call x1, Pallas kernels, layers(): pl.pallas_call(functools.partial(layers_kernel, groups), out_shape=(shape...  128 us
    pallas_call x1, Pallas kernels, widen(): pl.pallas_call(lambda *refs: widen_kernel(tuple(((p[0], p[0] + p[1]) for...  40.4 us

profile of v4, /device:TPU:0, one launch (start us, length us, event | category | flops | bytes accessed | tf_op | source)
XLA Modules:
  0.0 552.6 jit_solution(666943471449155746)
XLA Ops:
  0.6 0.6 add_reduce_fusion
  1.3 0.7 broadcast_multiply_fusion
  1.9 0.1 pad.4.clone
  2.0 0.1 fusion.1
  2.1 0.6 broadcast_in_dim.16.mask
  2.7 1.4 copy.22
  4.0 128.3 %shard_map.160 = (bf16[1024,8192]{1,0:T(8,128)(2,1)}, bf16[1024,9216]{1,0:T(8,128)(2,1)}, f32[4,256,1024]{2,1,0:T(8,128)}, f32[4,256,1024]{2,1,0:T(8,128)}, f32[...) custom-call(bf16[4,256,1024]{2,1,0:T(8,128)(2,1)} %tokens.1, bf16[4,256,1024]{2,1,0:T(8,128)(2,1)} %cotangent.1, ...), custom_call_target="tpu_custom_call" | custom-call | flops 54000001024 | bytes 125829120 | tf_op jit(solution)/shard_map/pallas_call | solution.py:736
  132.4 1.3 fusion.2
  133.7 0.7 multiply_convert_fusion
  134.3 0.8 slice.31
  135.1 0.1 maximum_bitcast_fusion
  135.2 1.3 convert_bitcast_fusion
  136.5 1.1 pad_maximum_fusion.extra_ref
  137.6 0.0 copy-start.2
  137.6 362.1 %shard_map.161.refs_0_ = bf16[50,256,1024]{2,1,0:T(8,128)(2,1)} custom-call(bf16[1024,8192]{1,0:T(8,128)(2,1)} %get-tuple-element.22.left_ref, bf16[1024,9216]{1,0:T(8,128)(2,1)} %get-tuple-element.23.right_ref, bf16[2,256,1024]{2,1,0:T(8,128)(2,1)} %pad_maximum_fusion.extra_ref), custom_call_target="tpu_custom_call" | custom-call | flops 25769803776 | bytes 104857600 | tf_op jit(solution)/shard_map/pallas_call | solution.py:349
  499.7 1.3 convert_reduce_fusion
  502.3 0.0 copy-done.2
  502.4 0.6 divide_reduce_fusion
  503.0 0.7 slice_convert_fusion.2
  503.7 0.6 copy.19
  504.3 2.1 slice_convert_fusion
  506.5 0.0 copy-start.1
  506.5 40.4 %shard_map.162 = (f32[4096,1024]{1,0:T(8,128)}, f32[1024,4096]{1,0:T(8,128)}, f32[1024,1024]{1,0:T(8,128)}, f32[1024,3072]{1,0:T(8,128)}) custom-call(bf16[50,256,1024]{2,1,0:T(8,128)(2,1)} %shard_map.161.refs_0_), custom_call_target="tpu_custom_call" | custom-call | bytes 75497472 | tf_op jit(solution)/shard_map/pallas_call | solution.py:801
  546.9 0.0 copy-start
  546.9 0.0 copy-done.1
  546.9 2.1 copy.25
  549.0 1.6 copy-done
  550.6 2.0 copy.26
  (1 shorter events, 0.0 us)
Async XLA Ops:
  137.6 364.8 %copy-start.2 = (f32[4,128]{1,0:T(4,128)S(1)}, f32[4,128]{1,0:T(4,128)}, u32[]{:S(2)}) copy-start(f32[4,128]{1,0:T(4,128)} %get-tuple-element.26) | copy-start | bytes 6148
  506.5 40.4 %copy-start.1 = (f32[4,256,1024]{2,1,0:T(8,128)S(1)}, f32[4,256,1024]{2,1,0:T(8,128)}, u32[]{:S(2)}) copy-start(f32[4,256,1024]{2,1,0:T(8,128)} %get-tuple-element.20) | copy-start | bytes 12582916
  546.9 3.7 copy-start

commit v5 on v4

--- a/solution.py
+++ b/solution.py
@@ -401,8 +401,8 @@
     return u * half, slope
 
 
-def layers_kernel(groups, tokens, cotangent, mask, embed, params, w_qkv, w_out, w_up, w_down,
-                  lefts, rights, sec_out, sec_grad, g_params, g_embed, squares,
+def layers_kernel(groups, tokens, clip_frames, cotangent, embed, norm_params, w_qkv, w_out, w_up, w_down,
+                  lefts, rights, sec_out, sec_grad, extras, sizes, params, g_params, g_embed,
                   qkv_w, out_w, up_w, down_w, emb, src, upstream, qkv, probs, slopes, xhat_f, stats,
                   keep, passed, acc, hid, u_buf,
                   w_sem, in_sem, left_sem, right_sem, wide_sem, send_sem, recv_sem):
@@ -416,8 +416,9 @@
     scale = head ** -0.5
 
     loads = [pltpu.make_async_copy(a, b, w_sem.at[k]) for k, (a, b) in enumerate(
-        ((w_qkv, qkv_w), (w_out, out_w), (w_up, up_w), (w_down, down_w), (embed, emb)))]
+        ((w_qkv, qkv_w), (w_out, out_w), (w_up, up_w), (w_down, down_w), (embed, emb), (norm_params, params)))]
     loads[4].start()
+    loads[5].start()
     loads[0].start()
 
     def token_load(g):
@@ -500,6 +501,7 @@
             @pl.when(g == 0)
             def _():
                 loads[4].wait()
+                loads[5].wait()
 
             @pl.when(g > 0)
             def _():
@@ -531,7 +533,8 @@
             def _():
                 for k in (1, 2):
                     left_store(g - 1, k).wait()
-            seen = mask[g, 0:1, :] > 0
+            limit = jnp.where(first, clip_frames[g] * (slots // 16), slots)
+            seen = lax.broadcasted_iota(jnp.int32, (1, slots), 1) < limit
             for h in range(HEADS):
                 q, k, v = heads_of(g, h)
                 s = jnp.where(seen, dot(q, k, NT) * scale, -1e30)
@@ -616,7 +619,6 @@
 
     g_params[...] = jnp.zeros_like(g_params)
     g_embed[...] = jnp.zeros_like(g_embed)
-    squares[...] = jnp.zeros_like(squares)
 
     def gains(row, e, xhat):
         g_params[row:row + 1] += jnp.sum(e * xhat, axis=0, keepdims=True)
@@ -710,8 +712,9 @@
             acc[...] = low.astype(WIDE)
         grad_store(g).start()
         total = acc[...]
-        squares[pl.ds(g, 1), :] = jnp.broadcast_to(
-            jnp.sum(jnp.sum(total * total, axis=0, keepdims=True), axis=1, keepdims=True), (1, squares.shape[1]))
+        total = jnp.sum(jnp.sum(total * total, axis=0, keepdims=True), axis=1, keepdims=True)
+        sizes[pl.ds(g, 1), :] = jnp.broadcast_to(
+            jnp.sqrt(total / (slots * width) + 1e-06), (1, sizes.shape[1]))
 
     pl.loop(0, groups)(backward)
 
@@ -721,12 +724,25 @@
         right_chunk(groups - 1, i).wait()
     grad_store(groups - 1).wait()
 
+    g_params[6:7] = jnp.sum(sizes[:, 0:1], axis=0, keepdims=True) * spread_of(width)
+    keep[:, 0:width] = g_embed[...].astype(LOW)
+    keep[:, width:2 * width] = jnp.zeros((slots, width), LOW)
+    keep[0:16, width:2 * width] = jnp.concatenate([g_params[...], jnp.zeros_like(g_params)]).astype(LOW)
+    for k in range(2):
+        pltpu.make_async_copy(keep.at[:, pl.ds(k * width, width)], extras.at[k], right_sem.at[k]).start()
+    for k in range(2):
+        pltpu.make_async_copy(keep.at[:, pl.ds(k * width, width)], extras.at[k], right_sem.at[k]).wait()
+
     @pl.when(section == 1)
     def _():
         relay_back(groups - 1).wait_send()
 
 
-def layers(tokens, cotangent, mask, embed, params, w_qkv, w_out, w_up, w_down, cid):
+def spread_of(width):
+    return 1.0 + lax.broadcasted_iota(jnp.int32, (1, width), 1).astype(WIDE) / width
+
+
+def layers(tokens, clip_frames, cotangent, embed, norm_params, w_qkv, w_out, w_up, w_down, cid):
     groups, slots, width = tokens.shape
     units = w_up.shape[1]
     rows = groups * slots
@@ -740,13 +756,15 @@
             shape((rows, units + 5 * width), LOW),
             shape((groups, slots, width), WIDE),
             shape((groups, slots, width), WIDE),
-            shape((8, width), WIDE),
-            shape((slots, width), WIDE),
+            shape((2, slots, width), LOW),
             shape((groups, 128), WIDE),
         ),
-        in_specs=[hbm, hbm, vmem, hbm, vmem, hbm, hbm, hbm, hbm],
-        out_specs=(hbm, hbm, hbm, hbm, vmem, vmem, vmem),
+        in_specs=[hbm, pl.BlockSpec(memory_space=pltpu.SMEM)] + [hbm] * 7,
+        out_specs=(hbm, hbm, hbm, hbm, hbm, vmem),
         scratch_shapes=[
+            pltpu.VMEM(norm_params.shape, WIDE),
+            pltpu.VMEM((8, width), WIDE),
+            pltpu.VMEM((slots, width), WIDE),
             pltpu.VMEM(w_qkv.shape, LOW),
             pltpu.VMEM(w_out.shape, LOW),
             pltpu.VMEM(w_up.shape, LOW),
@@ -764,7 +782,7 @@
             pltpu.VMEM((slots, width), WIDE),
             pltpu.VMEM((slots, width), WIDE),
             pltpu.VMEM((2, slots, CHUNK), WIDE),
-            pltpu.SemaphoreType.DMA((5,)),
+            pltpu.SemaphoreType.DMA((6,)),
             pltpu.SemaphoreType.DMA((2 * groups,)),
             pltpu.SemaphoreType.DMA((5 + units // CHUNK,)),
             pltpu.SemaphoreType.DMA((6 + units // CHUNK,)),
@@ -775,18 +793,32 @@
         compiler_params=pltpu.CompilerParams(
             collective_id=cid, has_side_effects=True, vmem_limit_bytes=63 * 2**20),
         cost_estimate=pl.CostEstimate(flops=54 * 10**9, bytes_accessed=120 * 2**20, transcendentals=10**7),
-    )(tokens, cotangent, mask, embed, params, w_qkv, w_out, w_up, w_down)
-
-
-def widen_kernel(ranges, block, *outs):
+    )(tokens, clip_frames, cotangent, embed, norm_params, w_qkv, w_out, w_up, w_down)
+
+
+def widen_kernel(ranges, count, block, sizes, *outs):
     step = pl.program_id(0)
     for (first, last), out in zip(ranges, outs):
         @pl.when((step >= first) & (step < last))
         def _():
-            out[...] = block[0].astype(out.dtype)
-
-
-def widen(sums, places):
+            out[...] = block[...].reshape(out.shape).astype(out.dtype)
+
+    @pl.when(step == ranges[-1][1])
+    def _():
+        embed, params, norms = outs[len(ranges):]
+        embed[...] = block[0].astype(WIDE)
+        params[...] = block[1, 0:8].astype(WIDE)[0:6]
+        row = block[1, 0:8].astype(WIDE)[6:7]
+        factors = spread_of(row.shape[1])
+        mean = jnp.sum(row, axis=1, keepdims=True) / jnp.sum(factors, axis=1, keepdims=True) / count
+        here = jnp.zeros(norms.shape, WIDE)
+        for g in range(norms.shape[1]):
+            lane = lax.broadcasted_iota(jnp.int32, norms.shape, 1) == g
+            here = jnp.where(lane, sizes[g:g + 1, 0:1] / mean, here)
+        norms[...] = here
+
+
+def widen(sums, sizes, count, places):
     tile, width = sums.shape[1:]
     steps = sum(p[1] for p in places)
 
@@ -796,39 +828,33 @@
             if wide == 1:
                 return k, 0
             return lax.rem(k, tall), lax.div(k, tall)
-        return pl.BlockSpec((tile, width), index)
-
+        return pl.BlockSpec((2 * tile, width), index)
+
+    shape = jax.ShapeDtypeStruct
+    whole = lambda *dims: pl.BlockSpec(dims, lambda step: (0,) * len(dims))
+    groups = sizes.shape[0]
     return pl.pallas_call(
-        lambda *refs: widen_kernel(tuple((p[0], p[0] + p[1]) for p in places), *refs),
-        grid=(steps,),
-        out_shape=tuple(jax.ShapeDtypeStruct((p[2] * tile, p[3] * width), jnp.float32) for p in places),
-        in_specs=[pl.BlockSpec((1, tile, width), lambda step: (step, 0, 0))],
-        out_specs=tuple(place(*p) for p in places),
-        compiler_params=pltpu.CompilerParams(vmem_limit_bytes=32 * 2**20),
-        cost_estimate=pl.CostEstimate(flops=0, bytes_accessed=6 * steps * tile * width, transcendentals=0),
-    )(sums)
+        lambda *refs: widen_kernel(tuple((p[0], p[0] + p[1]) for p in places), count, *refs),
+        grid=(steps + 1,),
+        out_shape=tuple(shape((p[2] * 2 * tile, p[3] * width), WIDE) for p in places)
+        + (shape((tile, width), WIDE), shape((6, width), WIDE), shape((1, groups), WIDE)),
+        in_specs=[pl.BlockSpec((2, tile, width), lambda step: (step, 0, 0)), whole(*sizes.shape)],
+        out_specs=tuple(place(*p) for p in places) + (whole(tile, width), whole(6, width), whole(1, groups)),
+        compiler_params=pltpu.CompilerParams(vmem_limit_bytes=48 * 2**20),
+        cost_estimate=pl.CostEstimate(flops=0, bytes_accessed=12 * steps * tile * width, transcendentals=0),
+    )(sums, sizes)
 
 
 def body(tokens, clip_frames, cotangent, embed, norm_params, w_qkv, w_out, w_up, w_down):
-    is_first = lax.axis_index("section") == 0
-    groups, slots, width = tokens.shape
-    units = w_up.shape[-1]
-    slot_ids = jnp.arange(slots, dtype=jnp.int32)
-    visible = (slot_ids[None, :] < clip_frames[:, None] * (slots // 16)) | jnp.logical_not(is_first)
-    mask = jnp.broadcast_to(visible[:, None, :].astype(WIDE), (groups, 8, slots))
-    lefts, rights, outcome, grad_inputs, g_params, g_embed, squares = layers(
-        tokens, cotangent, mask, embed[0], norm_params[0], w_qkv[0], w_out[0], w_up[0], w_down[0], 2
+    groups = tokens.shape[0]
+    devices = lax.axis_size("dp")
+    lefts, rights, outcome, grad_inputs, extras, sizes = layers(
+        tokens, clip_frames, cotangent, embed[0], norm_params[0], w_qkv[0], w_out[0], w_up[0], w_down[0], 2
     )
-    magnitude = jnp.sqrt(squares[:, 0] / (slots * width) + 1e-06)
-    factors = 1.0 + jnp.arange(width, dtype=WIDE) / width
-    row = (jnp.sum(magnitude) * factors)[None]
-    extras = jnp.stack(
-        [g_embed, jnp.concatenate([g_params[:6], row, jnp.zeros((TILE - 7, width), WIDE)])]
-    ).astype(LOW)
-    sums = weight_sums(lines_of(lax.axis_size("dp")), lefts, rights, extras, 1)
-    overall = jnp.sum(sums[49, 6].astype(WIDE)) / jnp.sum(factors)
-    norms = magnitude / (overall / (groups * lax.axis_size("dp")))
-    down, up, out, qkv = widen(sums, ((0, 16, 16, 1), (16, 16, 4, 4), (32, 4, 4, 1), (36, 12, 4, 3)))
+    sums = weight_sums(lines_of(devices), lefts, rights, extras, 1)
+    down, up, out, qkv, g_embed, g_params, norms = widen(
+        sums, sizes, groups * devices, ((0, 8, 8, 1), (8, 8, 2, 4), (16, 2, 2, 1), (18, 6, 2, 3))
+    )
     return (
         outcome[None],
         grad_inputs[None],
@@ -836,9 +862,9 @@
         out[None],
         up[None],
         down[None],
-        sums[49, :6].astype(WIDE)[None],
-        sums[48].astype(WIDE)[None],
-        norms[None],
+        g_params[None],
+        g_embed[None],
+        norms,
     )
 
 

time: 554 us -> 533 us (0.962)
  other arithmetic: 10.6 us -> 0 us
  Pallas kernels: 531 us -> 525 us
    pallas_call x1, Pallas kernels: 40.4 us -> 33.6 us  [widen(): pl.pallas_call(lambda *refs: widen_kernel(tuple(((p[0], p[0] + p[1]) for...]
where the time goes in v5:
time: 533 us; the launch traced here: 532 us
  Pallas kernels  525 us (98%)
  local copies, waits for them, and re-layouts  7.08 us (1%)
    pallas_call x1, Pallas kernels, weight_sums(): pl.pallas_call(functools.partial(weights_kernel, dims, tiles, total), out...  362 us
    pallas_call x1, Pallas kernels, layers(): pl.pallas_call(functools.partial(layers_kernel, groups), out_shape=(shape...  129 us
    pallas_call x1, Pallas kernels, widen(): pl.pallas_call(lambda *refs: widen_kernel(tuple(((p[0], p[0] + p[1]) for...  33.6 us

profile of v5, /device:TPU:0, one launch (start us, length us, event | category | flops | bytes accessed | tf_op | source)
XLA Modules:
  0.0 532.3 jit_solution(317032019297816855)
XLA Ops:
  0.6 1.4 copy.21
  2.0 128.9 %shard_map.160 = (bf16[1024,8192]{1,0:T(8,128)(2,1)}, bf16[1024,9216]{1,0:T(8,128)(2,1)}, f32[4,256,1024]{2,1,0:T(8,128)}, f32[4,256,1024]{2,1,0:T(8,128)}, bf16...) custom-call(bf16[4,256,1024]{2,1,0:T(8,128)(2,1)} %tokens.1, s32[4]{0:T(128)} %clip_frames.1, ...), custom_call_target="tpu_custom_call" | custom-call | flops 54000001024 | bytes 125829120 | tf_op jit(solution)/shard_map/pallas_call | solution.py:752
  130.9 0.0 copy-start
  130.9 362.0 %shard_map.161.refs_0_ = bf16[50,256,1024]{2,1,0:T(8,128)(2,1)} custom-call(bf16[1024,8192]{1,0:T(8,128)(2,1)} %get-tuple-element.24.left_ref, bf16[1024,9216]{1,0:T(8,128)(2,1)} %get-tuple-element.25.right_ref, bf16[2,256,1024]{2,1,0:T(8,128)(2,1)} %get-tuple-element.26.extra_ref), custom_call_target="tpu_custom_call" | custom-call | flops 25769803776 | bytes 104857600 | tf_op jit(solution)/shard_map/pallas_call | solution.py:349
  492.9 0.0 copy-done
  493.0 0.0 copy-start.2
  493.0 33.6 %shard_map.162 = (f32[4096,1024]{1,0:T(8,128)}, f32[1024,4096]{1,0:T(8,128)}, f32[1024,1024]{1,0:T(8,128)}, f32[1024,3072]{1,0:T(8,128)}, f32[256,1024]{1,0:T(8,...) custom-call(bf16[50,256,1024]{2,1,0:T(8,128)(2,1)} %shard_map.161.refs_0_, f32[4,128]{1,0:T(4,128)S(1)} %copy-done), custom_call_target="tpu_custom_call" | custom-call | bytes 75497472 | tf_op jit(solution)/shard_map/pallas_call | solution.py:836
  526.6 0.0 copy-start.1
  526.6 0.6 copy.18
  527.2 0.0 copy-done.2
  527.2 2.1 copy.24
  529.3 0.9 copy-done.1
  530.3 2.0 copy.25
Async XLA Ops:
  130.9 362.0 %copy-start = (f32[4,128]{1,0:T(4,128)S(1)}, f32[4,128]{1,0:T(4,128)}, u32[]{:S(2)}) copy-start(f32[4,128]{1,0:T(4,128)} %get-tuple-element.27.refs_1_) | copy-start | bytes 6148
  493.0 34.2 %copy-start.2 = (f32[4,256,1024]{2,1,0:T(8,128)S(1)}, f32[4,256,1024]{2,1,0:T(8,128)}, u32[]{:S(2)}) copy-start(f32[4,256,1024]{2,1,0:T(8,128)} %get-tuple-element.22) | copy-start | bytes 12582916
  526.6 3.7 copy-start.1

commit v6 on v5

--- a/solution.py
+++ b/solution.py
@@ -265,8 +265,53 @@
     pl.semaphore_wait(barrier, count)
 
 
-def weights_kernel(dims, tiles, total, left_ref, right_ref, extra_ref, result, held, landing, side,
-                   left_buf, right_buf, load_sem, send_sem, recv_sem, own_sem):
+class Small:
+    def __init__(self, plan, partial, arriving, whole, sems):
+        self.partial, self.whole = partial, whole
+        self.steps, tick, active = [], 0, None
+        for axis in (2, 1, 0):
+            n, c = plan.dims[axis], plan.coords[axis]
+            gather = pltpu.make_async_remote_copy(
+                src_ref=partial, dst_ref=arriving.at[axis], send_sem=sems.at[axis], recv_sem=sems.at[3 + axis],
+                device_id={"dp": plan.d + plan.strides[axis]}, device_id_type=MESH)
+            spread = pltpu.make_async_remote_copy(
+                src_ref=whole, dst_ref=whole, send_sem=sems.at[6 + axis], recv_sem=sems.at[9 + axis],
+                device_id={"dp": plan.d - plan.strides[axis]}, device_id_type=MESH)
+            self.steps.append((n, c, tick, active, gather, spread, arriving.at[axis]))
+            tick += n - 1
+            active = both(active, c == n - 1)
+        self.last = (tick, active)
+
+    def serve(self, t):
+        for n, c, start, active, gather, _, arriving in self.steps:
+            @when(both(t == start + c, active))
+            def _():
+                @pl.when(c > 0)
+                def _():
+                    gather.wait_recv()
+                    self.partial[...] += arriving[...]
+                pl.when(c < n - 1)(gather.start)
+        tick, active = self.last
+
+        @when(both(t == tick, active))
+        def _():
+            self.whole[...] = self.partial[...]
+        for n, c, start, active, _, spread, _ in self.steps[::-1]:
+            @when(both(t == 2 * tick - start - c, active))
+            def _():
+                pl.when(c < n - 1)(spread.wait_recv)
+                pl.when(c > 0)(spread.start)
+
+    def finish(self):
+        for n, c, _, active, gather, spread, _ in self.steps:
+            @when(active)
+            def _():
+                pl.when(c < n - 1)(gather.wait_send)
+                pl.when(c > 0)(spread.wait_send)
+
+
+def weights_kernel(dims, tiles, total, left_ref, right_ref, extra_ref, small_ref, result, small_sum, held, landing, side,
+                   left_buf, right_buf, partial, arriving, whole, load_sem, send_sem, recv_sem, own_sem, small_sem):
     plan = Plan(dims, total)
     per = WIDTH // TILE
     greet(plan)
@@ -308,14 +353,23 @@
     refs = (held, landing, side, result, send_sem, recv_sem)
 
     def tick(steady, t, _):
-        serve(plan, (0, 1), t, refs, own_sem, steady)
+        serve(plan, (1, 0, 2, 3), t, refs, own_sem, steady)
         @pl.when(t + 1 < tiles)
         def _():
             product(t + 1)
-        serve(plan, (2, 3), t, refs, own_sem, steady)
         return 0
 
-    lax.fori_loop(0, plan.depth, functools.partial(tick, False), 0)
+    small = Small(plan, partial, arriving, whole, small_sem)
+    partial[...] = small_ref[...]
+
+    def first_tick(t, _):
+        small.serve(t)
+        return tick(False, t, 0)
+
+    lax.fori_loop(0, plan.depth, first_tick, 0)
+    small.serve(plan.depth)
+    small.finish()
+    small_sum[...] = whole[...]
     lax.fori_loop(plan.depth, total, functools.partial(tick, True), 0)
     lax.fori_loop(total, total + plan.depth, functools.partial(tick, False), 0)
 
@@ -340,31 +394,37 @@
     return streams, arrivals, owns
 
 
-def weight_sums(dims, lefts, rights, extras, cid):
+def weight_sums(dims, lefts, rights, extras, small, cid):
     tiles = 12 * (WIDTH // TILE)
     total = tiles + extras.shape[0]
     rows = lefts.shape[0]
     streams, arrivals, owns = semaphores(dims, total)
     any_space = pl.BlockSpec(memory_space=pl.ANY)
+    vmem = pl.BlockSpec(memory_space=pltpu.VMEM)
     return pl.pallas_call(
         functools.partial(weights_kernel, dims, tiles, total),
-        out_shape=jax.ShapeDtypeStruct((total, TILE, WIDTH), jnp.bfloat16),
-        in_specs=[any_space] * 3,
-        out_specs=any_space,
+        out_shape=(jax.ShapeDtypeStruct((total, TILE, WIDTH), jnp.bfloat16),
+                   jax.ShapeDtypeStruct(small.shape, jnp.float32)),
+        in_specs=[any_space] * 3 + [vmem],
+        out_specs=(any_space, vmem),
         scratch_shapes=[
             pltpu.VMEM((total, TILE, WIDTH), jnp.bfloat16),
             pltpu.VMEM((total, TILE, WIDTH), jnp.bfloat16),
             pltpu.VMEM((total, MIDDLE_ROWS, WIDTH), jnp.bfloat16),
             pltpu.VMEM((rows, TILE), jnp.bfloat16),
             pltpu.VMEM((rows, WIDTH), jnp.bfloat16),
+            pltpu.VMEM(small.shape, jnp.float32),
+            pltpu.VMEM((3,) + small.shape, jnp.float32),
+            pltpu.VMEM(small.shape, jnp.float32),
             pltpu.SemaphoreType.DMA((3,)),
             pltpu.SemaphoreType.DMA((streams, RING)),
             pltpu.SemaphoreType.DMA((arrivals,)),
             pltpu.SemaphoreType.DMA((owns,)),
+            pltpu.SemaphoreType.DMA((12,)),
         ],
         compiler_params=pltpu.CompilerParams(collective_id=cid, has_side_effects=True, vmem_limit_bytes=63 * 2**20),
         cost_estimate=pl.CostEstimate(flops=2 * 12 * rows * WIDTH * WIDTH, bytes_accessed=100 * 2**20, transcendentals=0),
-    )(lefts, rights, extras)
+    )(lefts, rights, extras, small)
 
 
 HEADS = 8
@@ -402,7 +462,7 @@
 
 
 def layers_kernel(groups, tokens, clip_frames, cotangent, embed, norm_params, w_qkv, w_out, w_up, w_down,
-                  lefts, rights, sec_out, sec_grad, extras, sizes, params, g_params, g_embed,
+                  lefts, rights, sec_out, sec_grad, extra, sizes, g_params, params, g_embed,
                   qkv_w, out_w, up_w, down_w, emb, src, upstream, qkv, probs, slopes, xhat_f, stats,
                   keep, passed, acc, hid, u_buf,
                   w_sem, in_sem, left_sem, right_sem, wide_sem, send_sem, recv_sem):
@@ -724,22 +784,14 @@
         right_chunk(groups - 1, i).wait()
     grad_store(groups - 1).wait()
 
-    g_params[6:7] = jnp.sum(sizes[:, 0:1], axis=0, keepdims=True) * spread_of(width)
+    g_params[6:7] = jnp.broadcast_to(jnp.sum(sizes[:, 0:1], axis=0, keepdims=True), (1, width))
     keep[:, 0:width] = g_embed[...].astype(LOW)
-    keep[:, width:2 * width] = jnp.zeros((slots, width), LOW)
-    keep[0:16, width:2 * width] = jnp.concatenate([g_params[...], jnp.zeros_like(g_params)]).astype(LOW)
-    for k in range(2):
-        pltpu.make_async_copy(keep.at[:, pl.ds(k * width, width)], extras.at[k], right_sem.at[k]).start()
-    for k in range(2):
-        pltpu.make_async_copy(keep.at[:, pl.ds(k * width, width)], extras.at[k], right_sem.at[k]).wait()
+    pltpu.make_async_copy(keep.at[:, pl.ds(0, width)], extra.at[0], right_sem.at[0]).start()
+    pltpu.make_async_copy(keep.at[:, pl.ds(0, width)], extra.at[0], right_sem.at[0]).wait()
 
     @pl.when(section == 1)
     def _():
         relay_back(groups - 1).wait_send()
-
-
-def spread_of(width):
-    return 1.0 + lax.broadcasted_iota(jnp.int32, (1, width), 1).astype(WIDE) / width
 
 
 def layers(tokens, clip_frames, cotangent, embed, norm_params, w_qkv, w_out, w_up, w_down, cid):
@@ -756,14 +808,14 @@
             shape((rows, units + 5 * width), LOW),
             shape((groups, slots, width), WIDE),
             shape((groups, slots, width), WIDE),
-            shape((2, slots, width), LOW),
+            shape((1, slots, width), LOW),
             shape((groups, 128), WIDE),
+            shape((8, width), WIDE),
         ),
         in_specs=[hbm, pl.BlockSpec(memory_space=pltpu.SMEM)] + [hbm] * 7,
-        out_specs=(hbm, hbm, hbm, hbm, hbm, vmem),
+        out_specs=(hbm, hbm, hbm, hbm, hbm, vmem, vmem),
         scratch_shapes=[
             pltpu.VMEM(norm_params.shape, WIDE),
-            pltpu.VMEM((8, width), WIDE),
             pltpu.VMEM((slots, width), WIDE),
             pltpu.VMEM(w_qkv.shape, LOW),
             pltpu.VMEM(w_out.shape, LOW),
@@ -796,64 +848,87 @@
     )(tokens, clip_frames, cotangent, embed, norm_params, w_qkv, w_out, w_up, w_down)
 
 
-def widen_kernel(ranges, count, block, sizes, *outs):
-    step = pl.program_id(0)
-    for (first, last), out in zip(ranges, outs):
-        @pl.when((step >= first) & (step < last))
-        def _():
-            out[...] = block[...].reshape(out.shape).astype(out.dtype)
-
-    @pl.when(step == ranges[-1][1])
-    def _():
-        embed, params, norms = outs[len(ranges):]
-        embed[...] = block[0].astype(WIDE)
-        params[...] = block[1, 0:8].astype(WIDE)[0:6]
-        row = block[1, 0:8].astype(WIDE)[6:7]
-        factors = spread_of(row.shape[1])
-        mean = jnp.sum(row, axis=1, keepdims=True) / jnp.sum(factors, axis=1, keepdims=True) / count
-        here = jnp.zeros(norms.shape, WIDE)
-        for g in range(norms.shape[1]):
-            lane = lax.broadcasted_iota(jnp.int32, norms.shape, 1) == g
-            here = jnp.where(lane, sizes[g:g + 1, 0:1] / mean, here)
-        norms[...] = here
-
-
-def widen(sums, sizes, count, places):
+DEEP = 4
+
+
+def widen_kernel(places, count, sums, sizes, shared, *refs):
+    outs, (embed, params, norms, narrow, wide, read_sem, write_sem) = refs[:len(places)], refs[len(places):]
+    steps = places[-1][0] + places[-1][1]
+    tall, width = wide.shape[1:]
+
+    def read(i):
+        slot = lax.rem(i, DEEP)
+        return pltpu.make_async_copy(sums.at[pl.ds(2 * i, 2)], narrow.at[slot], read_sem.at[slot])
+
+    for i in range(DEEP):
+        read(i).start()
+
+    for (first, number, down, across), out in zip(places, outs):
+        def write(i):
+            slot, k = lax.rem(i, DEEP), i - first
+            rows = pl.ds(pl.multiple_of(lax.rem(k, down) * tall, tall), tall)
+            cols = pl.ds(pl.multiple_of(lax.div(k, down) * width, width), width)
+            return pltpu.make_async_copy(wide.at[slot], out.at[rows, cols], write_sem.at[slot])
+
+        @pl.loop(first, first + number)
+        def _(i):
+            slot = lax.rem(i, DEEP)
+            read(i).wait()
+            @pl.when(i >= DEEP)
+            def _():
+                write(i).wait()
+            wide[slot] = narrow[slot].reshape(tall, width).astype(WIDE)
+            write(i).start()
+            @pl.when(i + DEEP < steps)
+            def _():
+                read(i + DEEP).start()
+
+    tail = pltpu.make_async_copy(sums.at[2 * steps], narrow.at[0, 0], read_sem.at[0])
+    tail.start()
+    params[...] = shared[0:6]
+    mean = shared[6:7, 0:1] / count
+    here = jnp.zeros(norms.shape, WIDE)
+    for g in range(norms.shape[1]):
+        lane = lax.broadcasted_iota(jnp.int32, norms.shape, 1) == g
+        here = jnp.where(lane, sizes[g:g + 1, 0:1] / mean, here)
+    norms[...] = here
+    tail.wait()
+    embed[...] = narrow[0, 0].astype(WIDE)
+    for i in range(steps - DEEP, steps):
+        write(i).wait()
+
+
+def widen(sums, sizes, shared, count, places):
     tile, width = sums.shape[1:]
     steps = sum(p[1] for p in places)
-
-    def place(first, count, tall, wide):
-        def index(step):
-            k = jnp.clip(step - first, 0, count - 1)
-            if wide == 1:
-                return k, 0
-            return lax.rem(k, tall), lax.div(k, tall)
-        return pl.BlockSpec((2 * tile, width), index)
-
     shape = jax.ShapeDtypeStruct
-    whole = lambda *dims: pl.BlockSpec(dims, lambda step: (0,) * len(dims))
-    groups = sizes.shape[0]
+    hbm, vmem = pl.BlockSpec(memory_space=pl.ANY), pl.BlockSpec(memory_space=pltpu.VMEM)
     return pl.pallas_call(
-        lambda *refs: widen_kernel(tuple((p[0], p[0] + p[1]) for p in places), count, *refs),
-        grid=(steps + 1,),
+        lambda *refs: widen_kernel(places, count, *refs),
         out_shape=tuple(shape((p[2] * 2 * tile, p[3] * width), WIDE) for p in places)
-        + (shape((tile, width), WIDE), shape((6, width), WIDE), shape((1, groups), WIDE)),
-        in_specs=[pl.BlockSpec((2, tile, width), lambda step: (step, 0, 0)), whole(*sizes.shape)],
-        out_specs=tuple(place(*p) for p in places) + (whole(tile, width), whole(6, width), whole(1, groups)),
+        + (shape((tile, width), WIDE), shape((6, width), WIDE), shape((1, sizes.shape[0]), WIDE)),
+        in_specs=[hbm, vmem, vmem],
+        out_specs=(hbm,) * len(places) + (vmem,) * 3,
+        scratch_shapes=[
+            pltpu.VMEM((DEEP, 2, tile, width), LOW),
+            pltpu.VMEM((DEEP, 2 * tile, width), WIDE),
+            pltpu.SemaphoreType.DMA((DEEP,)),
+            pltpu.SemaphoreType.DMA((DEEP,)),
+        ],
         compiler_params=pltpu.CompilerParams(vmem_limit_bytes=48 * 2**20),
         cost_estimate=pl.CostEstimate(flops=0, bytes_accessed=12 * steps * tile * width, transcendentals=0),
-    )(sums, sizes)
+    )(sums, sizes, shared)
 
 
 def body(tokens, clip_frames, cotangent, embed, norm_params, w_qkv, w_out, w_up, w_down):
     groups = tokens.shape[0]
     devices = lax.axis_size("dp")
-    lefts, rights, outcome, grad_inputs, extras, sizes = layers(
+    lefts, rights, outcome, grad_inputs, extra, sizes, g_params = layers(
         tokens, clip_frames, cotangent, embed[0], norm_params[0], w_qkv[0], w_out[0], w_up[0], w_down[0], 2
     )
-    sums = weight_sums(lines_of(devices), lefts, rights, extras, 1)
+    sums, shared = weight_sums(lines_of(devices), lefts, rights, extra, g_params, 1)
     down, up, out, qkv, g_embed, g_params, norms = widen(
-        sums, sizes, groups * devices, ((0, 8, 8, 1), (8, 8, 2, 4), (16, 2, 2, 1), (18, 6, 2, 3))
+        sums, sizes, shared, groups * devices, ((0, 8, 8, 1), (8, 8, 2, 4), (16, 2, 2, 1), (18, 6, 2, 3))
     )
     return (
         outcome[None],

time: 533 us -> 523 us (0.981)
  Pallas kernels: 525 us -> 514 us
    pallas_call x1, Pallas kernels: 33.6 us -> 27.8 us  [widen(): pl.pallas_call(lambda *refs: widen_kernel(places, count, *refs), out_shap...]
    pallas_call x1, Pallas kernels: 362 us -> 357 us  [weight_sums(): pl.pallas_call(functools.partial(weights_kernel, dims, tiles, total), out...]
where the time goes in v6:
time: 523 us; the launch traced here: 522 us
  Pallas kernels  514 us (98%)
  local copies, waits for them, and re-layouts  7.83 us (1%)
    pallas_call x1, Pallas kernels, weight_sums(): pl.pallas_call(functools.partial(weights_kernel, dims, tiles, total), out...  357 us
    pallas_call x1, Pallas kernels, layers(): pl.pallas_call(functools.partial(layers_kernel, groups), out_shape=(shape...  129 us
    pallas_call x1, Pallas kernels, widen(): pl.pallas_call(lambda *refs: widen_kernel(places, count, *refs), out_shap...  27.8 us

profile of v6, /device:TPU:0, one launch (start us, length us, event | category | flops | bytes accessed | tf_op | source)
XLA Modules:
  0.0 522.3 jit_solution(15846146822332310163)
XLA Ops:
  0.6 1.4 copy.21
  2.0 129.4 %shard_map.160 = (bf16[1024,8192]{1,0:T(8,128)(2,1)}, bf16[1024,9216]{1,0:T(8,128)(2,1)}, f32[4,256,1024]{2,1,0:T(8,128)}, f32[4,256,1024]{2,1,0:T(8,128)}, bf16...) custom-call(bf16[4,256,1024]{2,1,0:T(8,128)(2,1)} %tokens.1, s32[4]{0:T(128)} %clip_frames.1, ...), custom_call_target="tpu_custom_call" | custom-call | flops 54000001024 | bytes 125829120 | tf_op jit(solution)/shard_map/pallas_call | solution.py:804
  131.4 0.0 copy-start.1
  131.4 356.6 %shard_map.161 = (bf16[49,256,1024]{2,1,0:T(8,128)(2,1)}, f32[8,1024]{1,0:T(8,128)}) custom-call(bf16[1024,8192]{1,0:T(8,128)(2,1)} %get-tuple-element.27.left_ref, bf16[1024,9216]{1,0:T(8,128)(2,1)} %get-tuple-element.28.right_ref, bf16[1,256,1024]{2,1,0:T(8,128)(2,1)} %get-tuple-element.29.extra_ref, f32[8,1024]{1,0:T(8,128)} %get-tuple-element.30.small_ref), custom_call_target="tpu_custom_call" | custom-call | flops 25769803776 | bytes 104857600 | tf_op jit(solution)/shard_map/pallas_call | solution.py:404
  488.0 0.0 copy-done.1
  488.0 0.0 copy-start
  488.0 0.7 copy-done
  488.7 0.0 copy-start.3
  488.7 27.8 %shard_map.162 = (f32[4096,1024]{1,0:T(8,128)}, f32[1024,4096]{1,0:T(8,128)}, f32[1024,1024]{1,0:T(8,128)}, f32[1024,3072]{1,0:T(8,128)}, f32[256,1024]{1,0:T(8,...) custom-call(bf16[49,256,1024]{2,1,0:T(8,128)(2,1)} %get-tuple-element.31.refs_0_, f32[4,128]{1,0:T(4,128)S(1)} %copy-done.1, ...), custom_call_target="tpu_custom_call" | custom-call | bytes 75497472 | tf_op jit(solution)/shard_map/pallas_call | solution.py:906
  516.6 0.0 copy-start.2
  516.6 0.6 copy.18
  517.2 0.0 copy-done.3
  517.2 2.1 copy.24
  519.4 0.9 copy-done.2
  520.3 2.0 copy.25
Async XLA Ops:
  131.4 356.6 %copy-start.1 = (f32[4,128]{1,0:T(4,128)S(1)}, f32[4,128]{1,0:T(4,128)}, u32[]{:S(2)}) copy-start(f32[4,128]{1,0:T(4,128)} %get-tuple-element.32.refs_1_) | copy-start | bytes 6148
  488.0 0.8 copy-start
  488.7 28.5 %copy-start.3 = (f32[4,256,1024]{2,1,0:T(8,128)S(1)}, f32[4,256,1024]{2,1,0:T(8,128)}, u32[]{:S(2)}) copy-start(f32[4,256,1024]{2,1,0:T(8,128)} %get-tuple-element.25) | copy-start | bytes 12582916
  516.6 3.7 copy-start.2

commit v7 on v6

--- a/solution.py
+++ b/solution.py
@@ -262,7 +262,7 @@
             def _():
                 pl.semaphore_signal(barrier, inc=1, device_id={"dp": plan.d + step}, device_id_type=MESH)
             count = count + inside.astype(jnp.int32)
-    pl.semaphore_wait(barrier, count)
+    return lambda: pl.semaphore_wait(barrier, count)
 
 
 class Small:
@@ -314,7 +314,7 @@
                    left_buf, right_buf, partial, arriving, whole, load_sem, send_sem, recv_sem, own_sem, small_sem):
     plan = Plan(dims, total)
     per = WIDTH // TILE
-    greet(plan)
+    met = greet(plan)
 
     def left_copy(s):
         job, part = lax.div(s, per), lax.rem(s, per)
@@ -349,6 +349,7 @@
     right_copy(0).start()
     extras.start()
     product(0)
+    met()
     extras.wait()
     refs = (held, landing, side, result, send_sem, recv_sem)
 
@@ -851,8 +852,11 @@
 DEEP = 4
 
 
-def widen_kernel(places, count, sums, sizes, shared, *refs):
-    outs, (embed, params, norms, narrow, wide, read_sem, write_sem) = refs[:len(places)], refs[len(places):]
+def widen_kernel(places, count, sums, sizes, shared, first, second, *refs):
+    outs, (embed, params, norms, first_out, second_out, narrow, wide, held, read_sem, write_sem, pass_sem) = (
+        refs[:len(places)], refs[len(places):])
+    coming = [pltpu.make_async_copy(a, held.at[k], pass_sem.at[k]) for k, a in enumerate((first, second))]
+    going = [pltpu.make_async_copy(held.at[k], a, pass_sem.at[2 + k]) for k, a in enumerate((first_out, second_out))]
     steps = places[-1][0] + places[-1][1]
     tall, width = wide.shape[1:]
 
@@ -862,15 +866,23 @@
 
     for i in range(DEEP):
         read(i).start()
-
-    for (first, number, down, across), out in zip(places, outs):
+    for copy in coming:
+        copy.start()
+
+    for (start, number, down, across), out in zip(places, outs):
         def write(i):
-            slot, k = lax.rem(i, DEEP), i - first
+            slot, k = lax.rem(i, DEEP), i - start
             rows = pl.ds(pl.multiple_of(lax.rem(k, down) * tall, tall), tall)
             cols = pl.ds(pl.multiple_of(lax.div(k, down) * width, width), width)
             return pltpu.make_async_copy(wide.at[slot], out.at[rows, cols], write_sem.at[slot])
 
-        @pl.loop(first, first + number)
+        if start == places[1][0]:
+            for copy in coming:
+                copy.wait()
+            for copy in going:
+                copy.start()
+
+        @pl.loop(start, start + number)
         def _(i):
             slot = lax.rem(i, DEEP)
             read(i).wait()
@@ -896,9 +908,11 @@
     embed[...] = narrow[0, 0].astype(WIDE)
     for i in range(steps - DEEP, steps):
         write(i).wait()
-
-
-def widen(sums, sizes, shared, count, places):
+    for copy in going:
+        copy.wait()
+
+
+def widen(sums, sizes, shared, first, second, count, places):
     tile, width = sums.shape[1:]
     steps = sum(p[1] for p in places)
     shape = jax.ShapeDtypeStruct
@@ -906,18 +920,21 @@
     return pl.pallas_call(
         lambda *refs: widen_kernel(places, count, *refs),
         out_shape=tuple(shape((p[2] * 2 * tile, p[3] * width), WIDE) for p in places)
-        + (shape((tile, width), WIDE), shape((6, width), WIDE), shape((1, sizes.shape[0]), WIDE)),
-        in_specs=[hbm, vmem, vmem],
-        out_specs=(hbm,) * len(places) + (vmem,) * 3,
+        + (shape((tile, width), WIDE), shape((6, width), WIDE), shape((1, sizes.shape[0]), WIDE),
+           shape(first.shape, WIDE), shape(second.shape, WIDE)),
+        in_specs=[hbm, vmem, vmem, hbm, hbm],
+        out_specs=(hbm,) * len(places) + (vmem,) * 3 + (hbm,) * 2,
         scratch_shapes=[
             pltpu.VMEM((DEEP, 2, tile, width), LOW),
             pltpu.VMEM((DEEP, 2 * tile, width), WIDE),
+            pltpu.VMEM((2,) + first.shape, WIDE),
             pltpu.SemaphoreType.DMA((DEEP,)),
             pltpu.SemaphoreType.DMA((DEEP,)),
+            pltpu.SemaphoreType.DMA((4,)),
         ],
-        compiler_params=pltpu.CompilerParams(vmem_limit_bytes=48 * 2**20),
+        compiler_params=pltpu.CompilerParams(vmem_limit_bytes=62 * 2**20),
         cost_estimate=pl.CostEstimate(flops=0, bytes_accessed=12 * steps * tile * width, transcendentals=0),
-    )(sums, sizes, shared)
+    )(sums, sizes, shared, first, second)
 
 
 def body(tokens, clip_frames, cotangent, embed, norm_params, w_qkv, w_out, w_up, w_down):
@@ -927,8 +944,8 @@
         tokens, clip_frames, cotangent, embed[0], norm_params[0], w_qkv[0], w_out[0], w_up[0], w_down[0], 2
     )
     sums, shared = weight_sums(lines_of(devices), lefts, rights, extra, g_params, 1)
-    down, up, out, qkv, g_embed, g_params, norms = widen(
-        sums, sizes, shared, groups * devices, ((0, 8, 8, 1), (8, 8, 2, 4), (16, 2, 2, 1), (18, 6, 2, 3))
+    down, up, out, qkv, g_embed, g_params, norms, outcome, grad_inputs = widen(
+        sums, sizes, shared, outcome, grad_inputs, groups * devices, ((0, 8, 8, 1), (8, 8, 2, 4), (16, 2, 2, 1), (18, 6, 2, 3))
     )
     return (
         outcome[None],

time: 523 us -> 521 us (level)
  no operation moved by 1% of the time
where the time goes in v7:
time: 521 us; the launch traced here: 520 us
  Pallas kernels  517 us (99%)
    pallas_call x1, Pallas kernels, weight_sums(): pl.pallas_call(functools.partial(weights_kernel, dims, tiles, total), out...  356 us
    pallas_call x1, Pallas kernels, layers(): pl.pallas_call(functools.partial(layers_kernel, groups), out_shape=(shape...  129 us
    pallas_call x1, Pallas kernels, widen(): pl.pallas_call(lambda *refs: widen_kernel(places, count, *refs), out_shap...  31.6 us

profile of v7, /device:TPU:0, one launch (start us, length us, event | category | flops | bytes accessed | tf_op | source)
XLA Modules:
  0.0 520.5 jit_solution(1420438769358275409)
XLA Ops:
  0.6 1.4 copy.21
  2.0 129.4 %shard_map.160 = (bf16[1024,8192]{1,0:T(8,128)(2,1)}, bf16[1024,9216]{1,0:T(8,128)(2,1)}, f32[4,256,1024]{2,1,0:T(8,128)}, f32[4,256,1024]{2,1,0:T(8,128)}, bf16...) custom-call(bf16[4,256,1024]{2,1,0:T(8,128)(2,1)} %tokens.1, s32[4]{0:T(128)} %clip_frames.1, ...), custom_call_target="tpu_custom_call" | custom-call | flops 54000001024 | bytes 125829120 | tf_op jit(solution)/shard_map/pallas_call | solution.py:805
  131.4 356.1 %shard_map.161 = (bf16[49,256,1024]{2,1,0:T(8,128)(2,1)}, f32[8,1024]{1,0:T(8,128)}) custom-call(bf16[1024,8192]{1,0:T(8,128)(2,1)} %get-tuple-element.27.left_ref, bf16[1024,9216]{1,0:T(8,128)(2,1)} %get-tuple-element.28.right_ref, bf16[1,256,1024]{2,1,0:T(8,128)(2,1)} %get-tuple-element.29.extra_ref, f32[8,1024]{1,0:T(8,128)} %get-tuple-element.30.small_ref), custom_call_target="tpu_custom_call" | custom-call | flops 25769803776 | bytes 104857600 | tf_op jit(solution)/shard_map/pallas_call | solution.py:405
  487.5 31.6 %shard_map.162 = (f32[4096,1024]{1,0:T(8,128)}, f32[1024,4096]{1,0:T(8,128)}, f32[1024,1024]{1,0:T(8,128)}, f32[1024,3072]{1,0:T(8,128)}, f32[256,1024]{1,0:T(8,...) custom-call(bf16[49,256,1024]{2,1,0:T(8,128)(2,1)} %get-tuple-element.31.refs_0_, ...), custom_call_target="tpu_custom_call" | custom-call | bytes 75497472 | tf_op jit(solution)/shard_map/pallas_call | solution.py:920
  519.1 1.4 copy.18
